TPU v7x, 32 devices: a whole 2x2x4 slice. The times are simulated.
32 devices in a mesh: ctx: 16 (over z, y, core), head: 2 (over x).
Axes of the slice: x: 2, y: 2, z: 4, core: 2. Of those that a mesh axis runs over, the one named last changes fastest.
Arguments:
- queries: bfloat16 [8192, 1024], P(('ctx', 'head')), may hold values from -9 to 9
- keys_in: bfloat16 [8192, 1024], P(('ctx', 'head')), may hold values from -9 to 9
- values: bfloat16 [8192, 1024], P(('ctx', 'head')), may hold values from -6 to 6
- d_out: bfloat16 [8192, 1024], P(('ctx', 'head')), may hold values from -6 to 6
- pair_blocks: int32 [128, 16], replicated, may hold values from 0 to 127, as said below
- pair_count: int32 [128], replicated, may hold values from 1 to 16, as said below
Outputs:
- d_queries: bfloat16 [8192, 1024], P(('ctx', 'head'))
- d_keys: bfloat16 [8192, 1024], P(('ctx', 'head'))
- d_values: bfloat16 [8192, 1024], P(('ctx', 'head'))
Inputs may be any that keep to these rules, and one draw needn't show every extreme that they name: `pair_blocks`: entry 0 of row b is b itself; every entry of row b is a block of a person within 2 persons of the person of block b (a person's tokens are 512 in a row). Entries may repeat. Only the first pair_count[b] entries of row b are listed.
All inputs are finite; a program needn't handle non-finite values.
Results may differ from a plain program's by a relative error of at most 0.012.
The roundings to bfloat16 on the way count: a program that leaves them out, or rounds other values in their place, can miss the bound.
Values may be sent and summed in bfloat16 or wider, within the bound.
No kernel may reach another device: no remote copies, remote signals or barrier semaphores. Data moves between devices by JAX's collectives and lax.ppermute only.
A program may use at most 192 MiB of HBM per device.

v0:
```python
import jax
import jax.numpy as jnp
from jax import lax
from jax.experimental import pallas as pl
from jax.experimental.pallas import tpu as pltpu
from jax.sharding import Mesh
from jax.sharding import PartitionSpec as P

HEAD_DIM = 64
BLOCK = 64
REACH = 2
PERSONS_GROUP = 4
CHUNK = 4
STEP = 4
SENDS = (5, 6, 1, 7, 4, 3, 2)
VMEM_BYTES = 63 * 1024 * 1024
LANES = 2 * HEAD_DIM
masked_value = -1e30


def dot_f32(lhs, rhs, lhs_dim, rhs_dim):
    return lax.dot_general(
        lhs, rhs, (((lhs_dim,), (rhs_dim,)), ((), ())), preferred_element_type=jnp.float32
    )


def mixed_rows(rows, mixer):
    return jnp.concatenate([rows] * 4, axis=0) * mixer[...]


def masked_softmax(both, live, slots, sure):
    biases = [jnp.where(slot < live, 0.0, masked_value) for slot in range(sure, slots)]
    scores = jnp.concatenate(
        [both[: sure * BLOCK, :LANES]]
        + [
            both[(sure + i) * BLOCK : (sure + i + 1) * BLOCK, :LANES] + bias
            for i, bias in enumerate(biases)
        ],
        axis=0,
    )
    d_probs = both[:, LANES:]
    top = jnp.max(scores, axis=0, keepdims=True)
    weights = jnp.exp(scores - top)
    inverse = 1.0 / jnp.sum(weights, axis=0, keepdims=True)
    delta = jnp.sum(weights * d_probs, axis=0, keepdims=True) * inverse
    probs = weights * inverse
    d_scores = probs * (d_probs - delta)
    return d_scores.astype(jnp.bfloat16), probs.astype(jnp.bfloat16)


def attend_step(slots, blocks, lives, lists_ref, qd, kv, acc, mixer, dq):
    rows = [pl.ds(pl.multiple_of(block * BLOCK, BLOCK), BLOCK) for block in blocks]
    places = [
        [
            pl.ds(pl.multiple_of(lists_ref[block, slot] * BLOCK, BLOCK), BLOCK)
            for slot in range(slots)
        ]
        for block in blocks
    ]
    weights = [mixed_rows(qd[row, :], mixer) for row in rows]
    windows = [jnp.concatenate([kv[place, :] for place in spot], axis=0) for spot in places]
    both = [dot_f32(window, weight, 1, 1) for window, weight in zip(windows, weights)]
    sures = [slots - CHUNK + 1] + [1] * (len(blocks) - 1)
    graded = [masked_softmax(b, live, slots, sure) for b, live, sure in zip(both, lives, sures)]
    grads = [
        dot_f32(jnp.concatenate([d_scores, probs], axis=1), weight, 1, 0)
        for (d_scores, probs), weight in zip(graded, weights)
    ]
    turned = [
        dot_f32(d_scores, window[:, :LANES], 0, 0)
        for (d_scores, _), window in zip(graded, windows)
    ]
    lane = lax.broadcasted_iota(jnp.int32, (BLOCK, LANES), 1)
    for row, both_heads in zip(rows, turned):
        picked = jnp.where(lane < HEAD_DIM, both_heads[:BLOCK], both_heads[BLOCK:])
        dq[row, :] = (picked * HEAD_DIM**-0.5).astype(jnp.bfloat16)
    for spot, grad in zip(places, grads):
        for slot, place in enumerate(spot):
            acc[place, :] += grad[slot * BLOCK : (slot + 1) * BLOCK]


def attend_kernel(
    me_ref, lists_ref, counts_ref, order_ref, *refs
):
    peers = len(refs) // 2 - 7
    qd_refs, own_refs = refs[:peers], refs[peers : 2 * peers]
    near_ref, across_ref, dq_ref, grad_left, grad_own, grad_right = refs[2 * peers : 2 * peers + 6]
    qd, kv, acc, mixer, dq, in_sems, sems, dq_sems = refs[2 * peers + 6 :]
    pairs = lists_ref.shape[1]
    halo, own = grad_left.shape[0], grad_own.shape[0]
    spots = [pl.ds(0, halo), pl.ds(halo, own), pl.ds(halo + own, halo)]
    me = me_ref[0]
    piece = own_refs[0].shape[0]
    edge = halo // piece
    lower = me < edge

    def rows_at(base, slab):
        return pl.ds(pl.multiple_of(base + slab * piece, piece), piece)

    copies = []
    for k in range(peers):
        spot = rows_at(0, me ^ k)
        copies.append(pltpu.make_async_copy(qd_refs[k], qd.at[spot, :], in_sems.at[0, k]))
        spot = rows_at(halo, me ^ k)
        copies.append(pltpu.make_async_copy(own_refs[k], kv.at[spot, :], in_sems.at[1, k]))
    for k in range(edge):
        spot = rows_at(jnp.where(lower, halo + own, 0), (me ^ k) % edge)
        copies.append(pltpu.make_async_copy(near_ref.at[k], kv.at[spot, :], in_sems.at[2, k]))
        spot = rows_at(jnp.where(lower, 0, halo + own), (me ^ k) % edge)
        copies.append(
            pltpu.make_async_copy(across_ref.at[k], kv.at[spot, :], in_sems.at[2, edge + k])
        )
    for copy in copies:
        copy.start()
    acc[...] = jnp.zeros_like(acc)
    group_row = lax.broadcasted_iota(jnp.int32, mixer.shape, 0) // HEAD_DIM
    group_lane = lax.broadcasted_iota(jnp.int32, mixer.shape, 1) // HEAD_DIM
    scale = jnp.where(group_row < 2, HEAD_DIM**-0.5, 1.0)
    mixer[...] = jnp.where(group_row == group_lane, scale, 0.0).astype(jnp.bfloat16)
    for copy in copies:
        copy.wait()

    def one_step(step, carry):
        blocks = [order_ref[STEP * step + i] for i in range(STEP)]
        lives = [counts_ref[block] for block in blocks]
        for chunks in range(1, pairs // CHUNK + 1):

            @pl.when((lives[0] + CHUNK - 1) // CHUNK == chunks)
            def _():
                attend_step(chunks * CHUNK, blocks, lives, lists_ref, qd, kv, acc, mixer, dq)

        return carry

    lax.fori_loop(0, counts_ref.shape[0] // STEP, one_step, 0)
    rows = dq_ref.shape[1]
    backs = [
        pltpu.make_async_copy(dq.at[pl.ds(i * rows, rows), :], dq_ref.at[i], dq_sems.at[i])
        for i in range(peers)
    ]
    for back in backs:
        back.start()
    for i, (spot, ref) in enumerate(zip(spots, (grad_left, grad_own, grad_right))):
        kv[spot, :] = acc[spot, :].astype(jnp.bfloat16)
        back = pltpu.make_async_copy(kv.at[spot, :], ref, sems.at[i])
        back.start()
        backs.append(back)
    for back in backs:
        back.wait()


def attend(me, lists, counts, order, qd, own, near, across):
    peers, piece = len(own), own[0].shape[0]
    rows, halo = peers * piece, near.shape[0] * piece
    window = rows + 2 * halo
    scalars = pl.BlockSpec(memory_space=pltpu.SMEM)
    far = pl.BlockSpec(memory_space=pl.ANY)

    def shaped(shape):
        return jax.ShapeDtypeStruct(shape, jnp.bfloat16)

    return pl.pallas_call(
        attend_kernel,
        out_shape=(
            shaped((peers, rows // peers, LANES)),
            shaped((halo, 2 * LANES)),
            shaped((rows, 2 * LANES)),
            shaped((halo, 2 * LANES)),
        ),
        in_specs=[scalars] * 4 + [far] * (2 * peers + 2),
        out_specs=(far, far, far, far),
        scratch_shapes=[
            pltpu.VMEM((rows, 2 * LANES), jnp.bfloat16),
            pltpu.VMEM((window, 2 * LANES), jnp.bfloat16),
            pltpu.VMEM((window, 2 * LANES), jnp.float32),
            pltpu.VMEM((2 * LANES, 2 * LANES), jnp.bfloat16),
            pltpu.VMEM((rows, LANES), jnp.bfloat16),
            pltpu.SemaphoreType.DMA((3, peers)),
            pltpu.SemaphoreType.DMA((3,)),
            pltpu.SemaphoreType.DMA((peers,)),
        ],
        compiler_params=pltpu.CompilerParams(vmem_limit_bytes=VMEM_BYTES),
        cost_estimate=pl.CostEstimate(
            flops=4_000_000_000, bytes_accessed=6_000_000, transcendentals=2_000_000
        ),
        name="attend",
    )(me, lists, counts, order, *qd, *own, near, across)


def pack_kernel(me_ref, first_ref, second_ref, *refs):
    joined_refs, (packed, in_sems, out_sems) = refs[:-3], refs[-3:]
    peers, _, width = packed.shape
    width = width // 2
    me = me_ref[0]
    arriving = [
        [
            pltpu.make_async_copy(
                ref.at[:, pl.ds(pl.multiple_of((me ^ slab) * width, width), width)],
                packed.at[slab, :, pl.ds(half * width, width)],
                in_sems.at[slab, half],
            )
            for half, ref in enumerate((first_ref, second_ref))
        ]
        for slab in range(peers)
    ]
    leaving = [
        pltpu.make_async_copy(packed.at[slab], joined_refs[slab], out_sems.at[slab])
        for slab in range(peers)
    ]
    for halves in arriving:
        for copy in halves:
            copy.start()
    for halves, out in zip(arriving, leaving):
        for copy in halves:
            copy.wait()
        out.start()
    for out in leaving:
        out.wait()


def join_columns(me, first, second, peers):
    rows, features = first.shape
    shape = (peers, rows, 2 * features // peers)
    anywhere = pl.BlockSpec(memory_space=pl.ANY)
    slab = jax.ShapeDtypeStruct(shape[1:], first.dtype)
    return pl.pallas_call(
        pack_kernel,
        out_shape=[slab] * peers,
        in_specs=[pl.BlockSpec(memory_space=pltpu.SMEM), anywhere, anywhere],
        out_specs=[anywhere] * peers,
        scratch_shapes=[
            pltpu.VMEM(shape, first.dtype),
            pltpu.SemaphoreType.DMA((peers, 2)),
            pltpu.SemaphoreType.DMA((peers,)),
        ],
        cost_estimate=pl.CostEstimate(flops=0, bytes_accessed=2_000_000, transcendentals=0),
        name="pack",
    )(me, first, second)


def compact_lists(pair_blocks, pair_count, first, rows, lowest, window_blocks):
    lists = lax.dynamic_slice_in_dim(pair_blocks, first, rows, 0) - lowest
    lists = jnp.clip(lists, 0, window_blocks - 1)
    counts = lax.dynamic_slice_in_dim(pair_count, first, rows, 0)
    slot = jnp.arange(lists.shape[1], dtype=jnp.int32)
    earlier = slot[None, :] < slot[:, None]
    repeat = jnp.any((lists[:, :, None] == lists[:, None, :]) & earlier[None], axis=2)
    keep = (slot[None, :] < counts[:, None]) & ~repeat
    place = jnp.sum(jnp.where(earlier[None], keep[:, None, :].astype(jnp.int32), 0), axis=2)
    chosen = keep[:, :, None] & (place[:, :, None] == slot[None, None, :])
    packed = jnp.sum(jnp.where(chosen, lists[:, :, None], 0), axis=1)
    lives = jnp.sum(keep.astype(jnp.int32), axis=1)
    block = jnp.arange(rows, dtype=jnp.int32)
    ahead = (lives[None, :] > lives[:, None]) | (
        (lives[None, :] == lives[:, None]) & (block[None, :] < block[:, None])
    )
    rank = jnp.sum(ahead.astype(jnp.int32), axis=1)
    order = jnp.sum(jnp.where(rank[:, None] == block[None, :], block[:, None], 0), axis=0)
    return packed, lives, order


def on_device(queries, keys_in, values, d_out, pair_blocks, pair_count):
    group = ("inner", "head")
    peers = lax.axis_size("inner") * lax.axis_size("head")
    outer = lax.axis_size("outer")
    tokens_dev, features = queries.shape
    tokens = tokens_dev * peers
    halo = REACH * (tokens // PERSONS_GROUP)
    blocks, halo_blocks = tokens // BLOCK, halo // BLOCK

    def exchange(parts):
        return lax.all_to_all(parts, group, split_axis=0, concat_axis=0, tiled=True)

    me = lax.axis_index(group)
    my_slab = me.astype(jnp.int32).reshape(1)
    half = peers // 2

    def send(slab, k):
        return lax.ppermute(slab, group, [(i, i ^ k) for i in range(peers)])

    def scatter(slabs):
        moved = {k: send(slabs[k], k) for k in SENDS}
        return [slabs[0]] + [moved[k] for k in range(1, peers)]

    def beside(slabs, lower, upper):
        pairs = [
            (o * peers + i, (o + (lower if i < half else upper)) * peers + i)
            for o in range(outer)
            for i in range(peers)
            if 0 <= o + (lower if i < half else upper) < outer
        ]
        return lax.ppermute(slabs, ("outer",) + group, pairs)

    up = [(i, i + 1) for i in range(outer - 1)]
    down = [(i + 1, i) for i in range(outer - 1)]
    own = scatter(join_columns(my_slab, keys_in, values, peers))
    qd = scatter(join_columns(my_slab, queries, d_out, peers))
    near = beside(jnp.stack(own[:half]), -1, 1)
    across = beside(jnp.stack(own[half:]), 1, -1)
    first = lax.axis_index("outer") * blocks
    lists, counts, order = compact_lists(
        pair_blocks, pair_count, first, blocks, first - halo_blocks, blocks + 2 * halo_blocks
    )
    dq, grad_left, grad_own, grad_right = attend(
        my_slab, lists, counts, order, qd, own, near, across
    )
    from_above = lax.ppermute(grad_left, "outer", down)
    from_below = lax.ppermute(grad_right, "outer", up)
    dq_back = exchange(dq)
    arrived = jnp.concatenate([from_below, from_above], axis=0)
    total = (grad_own.astype(jnp.float32) + arrived.astype(jnp.float32)).astype(jnp.bfloat16)
    grads = exchange(total.reshape(peers, tokens_dev, 2 * LANES))

    def columns(parts):
        return parts.transpose(1, 0, 2).reshape(tokens_dev, features)

    return columns(dq_back), columns(grads[:, :, :LANES]), columns(grads[:, :, LANES:])


def solution(mesh):
    ctx, head = mesh.devices.shape
    grouped = Mesh(
        mesh.devices.reshape(ctx // PERSONS_GROUP, PERSONS_GROUP, head), ("outer", "inner", "head")
    )
    rows = P(("outer", "inner", "head"), None)
    return jax.shard_map(
        on_device,
        mesh=grouped,
        in_specs=(rows, rows, rows, rows, P(), P()),
        out_specs=(rows, rows, rows),
        check_vma=False,
    )
```

profile of v0, /device:TPU:0, one launch (start us, length us, event | category | flops | bytes accessed | tf_op | source)
XLA Modules:
  0.0 98.9 jit_solution(7126969503761772262)
XLA Ops:
  0.7 2.1 %pack.3 = (bf16[256,256]{1,0:T(8,128)(2,1)}, bf16[256,256]{1,0:T(8,128)(2,1)}, bf16[256,256]{1,0:T(8,128)(2,1)}, bf16[256,256]{1,0:T(8,128)(2,1)}, bf16[256,256]...) custom-call(s32[1]{0:T(128)} %bitcast.me_ref, ...), custom_call_target="tpu_custom_call" | custom-call | bytes 2000000 | tf_op jit(solution)/shard_map/pack/pallas_call | solution.py:225
  2.8 3.0 %collective-permute-start.7 = (bf16[256,256]{1,0:T(8,128)(2,1)}, bf16[256,256]{1,0:T(8,128)(2,1)S(1)}, u32[]{:S(2)}, u32[]{:S(2)}) collective-permute-start(bf16[256,256]{1,0:T(8,128)(2,1)} %get-tuple-element.32), channel_id=1, source_target_pairs={{0,1},{1,0},{2,3},{3,2},{4,5},{5,4},{6,7},{7,6},{8,9},{9,8},{10,11... | collective-permute-start | bytes 393224 | tf_op jit(solution)/shard_map/ppermute | solution.py:278
  5.8 0.2 collective-permute-start.9
  6.0 2.0 %collective-permute-start.10 = (bf16[256,256]{1,0:T(8,128)(2,1)}, bf16[256,256]{1,0:T(8,128)(2,1)S(1)}, u32[]{:S(2)}, u32[]{:S(2)}) collective-permute-start(bf16[256,256]{1,0:T(8,128)(2,1)} %get-tuple-element.35), channel_id=1, source_target_pairs={{0,4},{1,5},{2,6},{3,7},{4,0},{5,1},{6,2},{7,3},{8,12},{9,13},{10,... | collective-permute-start | bytes 393224 | tf_op jit(solution)/shard_map/ppermute | solution.py:278
  8.0 1.4 %collective-permute-start.11 = (bf16[256,256]{1,0:T(8,128)(2,1)}, bf16[256,256]{1,0:T(8,128)(2,1)S(1)}, u32[]{:S(2)}, u32[]{:S(2)}) collective-permute-start(bf16[256,256]{1,0:T(8,128)(2,1)} %get-tuple-element.36), channel_id=1, source_target_pairs={{0,5},{1,4},{2,7},{3,6},{4,1},{5,0},{6,3},{7,2},{8,13},{9,12},{10,... | collective-permute-start | bytes 393224 | tf_op jit(solution)/shard_map/ppermute | solution.py:278
  9.4 0.1 subtract_clamp_fusion
  9.5 0.5 collective-permute-done.7.refs_9_
  10.0 0.1 collective-permute-start.12
  10.2 3.4 %collective-permute-start.13 = (bf16[256,256]{1,0:T(8,128)(2,1)}, bf16[256,256]{1,0:T(8,128)(2,1)S(1)}, u32[]{:S(2)}, u32[]{:S(2)}) collective-permute-start(bf16[256,256]{1,0:T(8,128)(2,1)} %get-tuple-element.38), channel_id=1, source_target_pairs={{0,7},{1,6},{2,5},{3,4},{4,3},{5,2},{6,1},{7,0},{8,15},{9,14},{10,... | collective-permute-start | bytes 393224 | tf_op jit(solution)/shard_map/ppermute | solution.py:278
  13.6 0.1 and_reduce_fusion
  13.7 0.1 dynamic_slice.6
  13.8 2.1 %pack.2 = (bf16[256,256]{1,0:T(8,128)(2,1)}, bf16[256,256]{1,0:T(8,128)(2,1)}, bf16[256,256]{1,0:T(8,128)(2,1)}, bf16[256,256]{1,0:T(8,128)(2,1)}, bf16[256,256]...) custom-call(s32[1]{0:T(128)} %bitcast.me_ref, ...), custom_call_target="tpu_custom_call" | custom-call | bytes 2000000 | tf_op jit(solution)/shard_map/pack/pallas_call | solution.py:225
  15.9 0.0 copy-start.21
  15.9 0.0 copy-start.20
  16.0 0.1 collective-permute-start
  16.1 0.1 pad_maximum_fusion
  16.2 0.6 copy-done.21
  16.9 0.3 collective-permute-done.11.refs_13_
  17.2 1.2 %collective-permute-start.2 = (bf16[256,256]{1,0:T(8,128)(2,1)S(1)}, bf16[256,256]{1,0:T(8,128)(2,1)S(1)}, u32[]{:S(2)}, u32[]{:S(2)}) collective-permute-start(bf16[256,256]{1,0:T(8,128)(2,1)S(1)} %copy-done.20), channel_id=1, source_target_pairs={{0,3},{1,2},{2,1},{3,0},{4,7},{5,6},{6,5},{7,4},{8,11},{9,10},{10,... | collective-permute-start | bytes 393224 | tf_op jit(solution)/shard_map/ppermute | solution.py:278
  18.5 2.7 %collective-permute-done.12.refs_14_ = bf16[256,256]{1,0:T(8,128)(2,1)S(1)} collective-permute-done((bf16[256,256]{1,0:T(8,128)(2,1)}, bf16[256,256]{1,0:T(8,128)(2,1)S(1)}, u32[]{:S(2)}, u32[]{:S(2)}) %collective-permute-start.12) | collective-permute-done | bytes 131104 | tf_op jit(solution)/shard_map/ppermute | solution.py:278
  21.1 1.3 %collective-permute-start.14 = (bf16[4,256,256]{2,1,0:T(8,128)(2,1)S(1)}, bf16[4,256,256]{2,1,0:T(8,128)(2,1)S(1)}, u32[]{:S(2)}, u32[]{:S(2)}) collective-permute-start(bf16[4,256,256]{2,1,0:T(8,128)(2,1)S(1)} %pad_maximum_fusion), channel_id=1, source_target_pairs={{4,12},{5,13},{6,14},{7,15},{8,0},{9,1},{10,2},{11,3},{12,20},{13,... | collective-permute-start | bytes 1572872 | tf_op jit(solution)/shard_map/ppermute | solution.py:291
  22.5 0.1 pad_maximum_fusion.1
  22.5 4.6 %collective-permute-start.15 = (bf16[4,256,256]{2,1,0:T(8,128)(2,1)S(1)}, bf16[4,256,256]{2,1,0:T(8,128)(2,1)S(1)}, u32[]{:S(2)}, u32[]{:S(2)}) collective-permute-start(bf16[4,256,256]{2,1,0:T(8,128)(2,1)S(1)} %pad_maximum_fusion.1), channel_id=1, source_target_pairs={{0,8},{1,9},{2,10},{3,11},{8,16},{9,17},{10,18},{11,19},{12,4},{13... | collective-permute-start | bytes 1572872 | tf_op jit(solution)/shard_map/ppermute | solution.py:291
  27.3 0.1 collective-permute-start.3
  27.3 0.1 select_reduce_fusion.1
  27.5 3.4 %collective-permute-start.4 = (bf16[256,256]{1,0:T(8,128)(2,1)}, bf16[256,256]{1,0:T(8,128)(2,1)S(1)}, u32[]{:S(2)}, u32[]{:S(2)}) collective-permute-start(bf16[256,256]{1,0:T(8,128)(2,1)} %get-tuple-element.28), channel_id=1, source_target_pairs={{0,5},{1,4},{2,7},{3,6},{4,1},{5,0},{6,3},{7,2},{8,13},{9,12},{10,... | collective-permute-start | bytes 393224 | tf_op jit(solution)/shard_map/ppermute | solution.py:278
  31.0 0.1 collective-permute-start.5
  31.1 5.5 %collective-permute-done.3.refs_4_ = bf16[256,256]{1,0:T(8,128)(2,1)S(1)} collective-permute-done((bf16[256,256]{1,0:T(8,128)(2,1)S(1)}, bf16[256,256]{1,0:T(8,128)(2,1)S(1)}, u32[]{:S(2)}, u32[]{:S(2)}) %collective-permute-start.3) | collective-permute-done | bytes 131104 | tf_op jit(solution)/shard_map/ppermute | solution.py:278
  36.5 0.6 copy-done.19
  37.2 0.2 convert_reduce_fusion
  37.3 0.7 copy.19.lists_ref
  38.0 0.6 select_reduce_fusion.2.order_ref
  38.6 3.3 %collective-permute-done.6.refs_7_ = bf16[256,256]{1,0:T(8,128)(2,1)} collective-permute-done((bf16[256,256]{1,0:T(8,128)(2,1)S(1)}, bf16[256,256]{1,0:T(8,128)(2,1)}, u32[]{:S(2)}, u32[]{:S(2)}) %collective-permute-start.6) | collective-permute-done | bytes 131104 | tf_op jit(solution)/shard_map/ppermute | solution.py:278
  41.9 0.8 copy-done.11
  42.7 0.8 copy-done.12
  43.6 14.0 %attend.1 = (bf16[8,256,128]{2,1,0:T(8,128)(2,1)}, bf16[1024,256]{1,0:T(8,128)(2,1)}, bf16[2048,256]{1,0:T(8,128)(2,1)}, bf16[1024,256]{1,0:T(8,128)(2,1)}) custom-call(s32[1]{0:T(128)} %bitcast.me_ref, s32[32,16]{1,0:T(8,128)} %copy.19.lists_ref, s32[32]{0:T(128)} %copy-done.10, s32[32]{0:T(128)} %select_reduce_fusion.2.order_ref, ...), custom_call_target="tpu_custom_call" | custom-call | flops 4000000000 | bytes 6000000 | tf_op jit(solution)/shard_map/attend/pallas_call | solution.py:161
  57.6 5.0 %collective-permute-start.16 = (bf16[1024,256]{1,0:T(8,128)(2,1)}, bf16[1024,256]{1,0:T(8,128)(2,1)S(1)}, u32[]{:S(2)}, u32[]{:S(2)}) collective-permute-start(bf16[1024,256]{1,0:T(8,128)(2,1)} %get-tuple-element.41), channel_id=1, source_target_pairs={{0,8},{8,16},{16,24},{1,9},{9,17},{17,25},{2,10},{10,18},{18,26},{... | collective-permute-start | bytes 1572872 | tf_op jit(solution)/shard_map/ppermute | solution.py:307
  62.5 1.3 %collective-permute-start.17 = (bf16[1024,256]{1,0:T(8,128)(2,1)}, bf16[1024,256]{1,0:T(8,128)(2,1)S(1)}, u32[]{:S(2)}, u32[]{:S(2)}) collective-permute-start(bf16[1024,256]{1,0:T(8,128)(2,1)} %get-tuple-element.42), channel_id=1, source_target_pairs={{8,0},{16,8},{24,16},{9,1},{17,9},{25,17},{10,2},{18,10},{26,18},{... | collective-permute-start | bytes 1572872 | tf_op jit(solution)/shard_map/ppermute | solution.py:306
  63.8 3.5 %all-to-all-start = ((bf16[8,256,128]{2,1,0:T(8,128)(2,1)}), bf16[8,256,128]{2,1,0:T(8,128)(2,1)S(1)}, u32[]{:S(2)}, u32[]{:S(2)}) async-start(bf16[8,256,128]{2,1,0:T(8,128)(2,1)} %get-tuple-element.39), calls=%async_computation | async-start | bytes 1048576 | tf_op jit(solution)/shard_map/all_to_all | solution.py:271
  67.3 5.4 %collective-permute-done.16 = bf16[1024,256]{1,0:T(8,128)(2,1)S(1)} collective-permute-done((bf16[1024,256]{1,0:T(8,128)(2,1)}, bf16[1024,256]{1,0:T(8,128)(2,1)S(1)}, u32[]{:S(2)}, u32[]{:S(2)}) %collective-permute-start.16) | collective-permute-done | bytes 524320 | tf_op jit(solution)/shard_map/ppermute | solution.py:307
  72.7 4.0 %collective-permute-done.17 = bf16[1024,256]{1,0:T(8,128)(2,1)S(1)} collective-permute-done((bf16[1024,256]{1,0:T(8,128)(2,1)}, bf16[1024,256]{1,0:T(8,128)(2,1)S(1)}, u32[]{:S(2)}, u32[]{:S(2)}) %collective-permute-start.17) | collective-permute-done | bytes 524320 | tf_op jit(solution)/shard_map/ppermute | solution.py:306
  76.8 1.3 %add_convert_fusion = bf16[2048,256]{1,0:T(8,128)(2,1)} fusion(bf16[2048,256]{1,0:T(8,128)(2,1)S(1)} %copy-done, bf16[1024,256]{1,0:T(8,128)(2,1)S(1)} %collective-permute-done.17, bf16[1024,256]{1,0:T(8,128)(2,1)S(1)} %collective-permute-done.16), kind=kLoop, calls=%fused_computation | loop fusion | flops 3670016 | bytes 3145728 | tf_op jit(solution)/shard_map/convert_element_type | solution.py:310
  78.0 4.5 %all-to-all-start.1 = ((bf16[8,256,256]{2,1,0:T(8,128)(2,1)}), bf16[8,256,256]{2,1,0:T(8,128)(2,1)S(1)}, u32[]{:S(2)}, u32[]{:S(2)}) async-start(bf16[8,256,256]{2,1,0:T(8,128)(2,1)} %bitcast.11), calls=%async_computation.1 | async-start | bytes 2097152 | tf_op jit(solution)/shard_map/all_to_all | solution.py:271
  82.5 0.2 copy.20
  82.8 1.0 %copy.23 = bf16[256,1024]{1,0:T(8,128)(2,1)} copy(bf16[256,1024]{0,1:T(8,128)(2,1)S(1)} %bitcast.23) | data formatting | bytes 1048576
  83.8 13.7 %all-to-all-done.1 = bf16[8,256,256]{2,1,0:T(8,128)(2,1)S(1)} async-done(((bf16[8,256,256]{2,1,0:T(8,128)(2,1)}), bf16[8,256,256]{2,1,0:T(8,128)(2,1)S(1)}, u32[]{:S(2)}, u32[]{:S(2)}) %all-to-all-start.1) | async-done | bytes 1048608 | tf_op jit(solution)/shard_map/all_to_all | solution.py:271
  97.5 0.3 slice_bitcast_fusion
  97.7 1.1 %copy_bitcast_fusion = (bf16[256,1024]{1,0:T(8,128)(2,1)}, bf16[256,1024]{1,0:T(8,128)(2,1)}) fusion(bf16[8,32,8,128]{3,2,1,0:T(8,128)(2,1)S(1)} %get-tuple-element.51, bf16[8,32,8,128]{3,2,1,0:T(8,128)(2,1)S(1)} %get-tuple-element.52), kind=kLoop, calls=%fused_computation.1 | loop fusion | bytes 2097152 | tf_op jit(solution)/shard_map/reshape | solution.py:314
  (61 shorter events, 0.2 us)
Async XLA Ops:
  0.6 8.8 %copy-start.9 = (s32[128,16]{0,1:T(8,128)S(1)}, s32[128,16]{0,1:T(8,128)}, u32[]{:S(2)}) copy-start(s32[128,16]{0,1:T(8,128)} %param.10) | copy-start | bytes 24580
  0.6 13.1 %copy-start.23 = (s32[128]{0:T(128)S(1)}, s32[128]{0:T(128)}, u32[]{:S(2)}) copy-start(s32[128]{0:T(128)} %param.11) | copy-start | bytes 1540
  2.8 13.3 %copy-start.1 = (bf16[256,256]{1,0:T(8,128)(2,1)S(1)}, bf16[256,256]{1,0:T(8,128)(2,1)}, u32[]{:S(2)}) copy-start(bf16[256,256]{1,0:T(8,128)(2,1)} %get-tuple-element.31.refs_8_) | copy-start | bytes 393220
  2.8 7.2 %collective-permute-start.7 = (bf16[256,256]{1,0:T(8,128)(2,1)}, bf16[256,256]{1,0:T(8,128)(2,1)S(1)}, u32[]{:S(2)}, u32[]{:S(2)}) collective-permute-start(bf16[256,256]{1,0:T(8,128)(2,1)} %get-tuple-element.32), channel_id=1, source_target_pairs={{0,1},{1,0},{2,3},{3,2},{4,5},{5,4},{6,7},{7,6},{8,9},{9,8},{10,11... | collective-permute-start | bytes 393224 | tf_op jit(solution)/shard_map/ppermute | solution.py:278
  5.8 4.3 %collective-permute-start.8 = (bf16[256,256]{1,0:T(8,128)(2,1)}, bf16[256,256]{1,0:T(8,128)(2,1)S(1)}, u32[]{:S(2)}, u32[]{:S(2)}) collective-permute-start(bf16[256,256]{1,0:T(8,128)(2,1)} %get-tuple-element.33), channel_id=1, source_target_pairs={{0,2},{1,3},{2,0},{3,1},{4,6},{5,7},{6,4},{7,5},{8,10},{9,11},{10,... | collective-permute-start | bytes 393224 | tf_op jit(solution)/shard_map/ppermute | solution.py:278
  5.8 10.1 %collective-permute-start.9 = (bf16[256,256]{1,0:T(8,128)(2,1)}, bf16[256,256]{1,0:T(8,128)(2,1)S(1)}, u32[]{:S(2)}, u32[]{:S(2)}) collective-permute-start(bf16[256,256]{1,0:T(8,128)(2,1)} %get-tuple-element.34), channel_id=1, source_target_pairs={{0,3},{1,2},{2,1},{3,0},{4,7},{5,6},{6,5},{7,4},{8,11},{9,10},{10,... | collective-permute-start | bytes 393224 | tf_op jit(solution)/shard_map/ppermute | solution.py:278
  6.0 10.2 %collective-permute-start.10 = (bf16[256,256]{1,0:T(8,128)(2,1)}, bf16[256,256]{1,0:T(8,128)(2,1)S(1)}, u32[]{:S(2)}, u32[]{:S(2)}) collective-permute-start(bf16[256,256]{1,0:T(8,128)(2,1)} %get-tuple-element.35), channel_id=1, source_target_pairs={{0,4},{1,5},{2,6},{3,7},{4,0},{5,1},{6,2},{7,3},{8,12},{9,13},{10,... | collective-permute-start | bytes 393224 | tf_op jit(solution)/shard_map/ppermute | solution.py:278
  8.0 9.2 %collective-permute-start.11 = (bf16[256,256]{1,0:T(8,128)(2,1)}, bf16[256,256]{1,0:T(8,128)(2,1)S(1)}, u32[]{:S(2)}, u32[]{:S(2)}) collective-permute-start(bf16[256,256]{1,0:T(8,128)(2,1)} %get-tuple-element.36), channel_id=1, source_target_pairs={{0,5},{1,4},{2,7},{3,6},{4,1},{5,0},{6,3},{7,2},{8,13},{9,12},{10,... | collective-permute-start | bytes 393224 | tf_op jit(solution)/shard_map/ppermute | solution.py:278
  10.0 6.1 %copy-start.2 = (bf16[256,256]{1,0:T(8,128)(2,1)}, bf16[256,256]{1,0:T(8,128)(2,1)S(1)}, u32[]{:S(2)}) copy-start(bf16[256,256]{1,0:T(8,128)(2,1)S(1)} %collective-permute-done.7.refs_9_) | copy-start | bytes 393220
  10.0 11.1 %collective-permute-start.12 = (bf16[256,256]{1,0:T(8,128)(2,1)}, bf16[256,256]{1,0:T(8,128)(2,1)S(1)}, u32[]{:S(2)}, u32[]{:S(2)}) collective-permute-start(bf16[256,256]{1,0:T(8,128)(2,1)} %get-tuple-element.37), channel_id=1, source_target_pairs={{0,6},{1,7},{2,4},{3,5},{4,2},{5,3},{6,0},{7,1},{8,14},{9,15},{10,... | collective-permute-start | bytes 393224 | tf_op jit(solution)/shard_map/ppermute | solution.py:278
  10.2 6.0 %copy-start.3 = (bf16[256,256]{1,0:T(8,128)(2,1)}, bf16[256,256]{1,0:T(8,128)(2,1)S(1)}, u32[]{:S(2)}) copy-start(bf16[256,256]{1,0:T(8,128)(2,1)S(1)} %collective-permute-done.8.refs_10_) | copy-start | bytes 393220
  10.2 12.3 %collective-permute-start.13 = (bf16[256,256]{1,0:T(8,128)(2,1)}, bf16[256,256]{1,0:T(8,128)(2,1)S(1)}, u32[]{:S(2)}, u32[]{:S(2)}) collective-permute-start(bf16[256,256]{1,0:T(8,128)(2,1)} %get-tuple-element.38), channel_id=1, source_target_pairs={{0,7},{1,6},{2,5},{3,4},{4,3},{5,2},{6,1},{7,0},{8,15},{9,14},{10,... | collective-permute-start | bytes 393224 | tf_op jit(solution)/shard_map/ppermute | solution.py:278
  15.9 0.9 copy-start.21
  15.9 1.3 %copy-start.20 = (bf16[256,256]{1,0:T(8,128)(2,1)S(1)}, bf16[256,256]{1,0:T(8,128)(2,1)}, u32[]{:S(2)}) copy-start(bf16[256,256]{1,0:T(8,128)(2,1)} %get-tuple-element.26) | copy-start | bytes 393220
  16.0 6.6 %copy-start.4 = (bf16[256,256]{1,0:T(8,128)(2,1)}, bf16[256,256]{1,0:T(8,128)(2,1)S(1)}, u32[]{:S(2)}) copy-start(bf16[256,256]{1,0:T(8,128)(2,1)S(1)} %collective-permute-done.9.refs_11_) | copy-start | bytes 393220
  16.0 11.3 %collective-permute-start = (bf16[256,256]{1,0:T(8,128)(2,1)}, bf16[256,256]{1,0:T(8,128)(2,1)S(1)}, u32[]{:S(2)}, u32[]{:S(2)}) collective-permute-start(bf16[256,256]{1,0:T(8,128)(2,1)} %get-tuple-element.24), channel_id=1, source_target_pairs={{0,1},{1,0},{2,3},{3,2},{4,5},{5,4},{6,7},{7,6},{8,9},{9,8},{10,11... | collective-permute-start | bytes 393224 | tf_op jit(solution)/shard_map/ppermute | solution.py:278
  16.1 11.2 %copy-start.18 = (bf16[256,256]{1,0:T(8,128)(2,1)S(1)}, bf16[256,256]{1,0:T(8,128)(2,1)}, u32[]{:S(2)}) copy-start(bf16[256,256]{1,0:T(8,128)(2,1)} %get-tuple-element.27) | copy-start | bytes 393220
  16.1 14.9 %copy-start.17 = (bf16[256,256]{1,0:T(8,128)(2,1)S(1)}, bf16[256,256]{1,0:T(8,128)(2,1)}, u32[]{:S(2)}) copy-start(bf16[256,256]{1,0:T(8,128)(2,1)} %get-tuple-element.29) | copy-start | bytes 393220
  16.1 20.4 %copy-start.16 = (bf16[256,256]{1,0:T(8,128)(2,1)S(1)}, bf16[256,256]{1,0:T(8,128)(2,1)}, u32[]{:S(2)}) copy-start(bf16[256,256]{1,0:T(8,128)(2,1)} %get-tuple-element.30) | copy-start | bytes 393220
  16.2 27.3 %copy-start.5 = (bf16[256,256]{1,0:T(8,128)(2,1)}, bf16[256,256]{1,0:T(8,128)(2,1)S(1)}, u32[]{:S(2)}) copy-start(bf16[256,256]{1,0:T(8,128)(2,1)S(1)} %collective-permute-done.10.refs_12_) | copy-start | bytes 393220
  16.9 10.7 %collective-permute-start.1 = (bf16[256,256]{1,0:T(8,128)(2,1)S(1)}, bf16[256,256]{1,0:T(8,128)(2,1)S(1)}, u32[]{:S(2)}, u32[]{:S(2)}) collective-permute-start(bf16[256,256]{1,0:T(8,128)(2,1)S(1)} %copy-done.21), channel_id=1, source_target_pairs={{0,2},{1,3},{2,0},{3,1},{4,6},{5,7},{6,4},{7,5},{8,10},{9,11},{10,... | collective-permute-start | bytes 393224 | tf_op jit(solution)/shard_map/ppermute | solution.py:278
  17.2 26.3 %copy-start.6 = (bf16[256,256]{1,0:T(8,128)(2,1)}, bf16[256,256]{1,0:T(8,128)(2,1)S(1)}, u32[]{:S(2)}) copy-start(bf16[256,256]{1,0:T(8,128)(2,1)S(1)} %collective-permute-done.11.refs_13_) | copy-start | bytes 393220
  17.2 13.8 %collective-permute-start.2 = (bf16[256,256]{1,0:T(8,128)(2,1)S(1)}, bf16[256,256]{1,0:T(8,128)(2,1)S(1)}, u32[]{:S(2)}, u32[]{:S(2)}) collective-permute-start(bf16[256,256]{1,0:T(8,128)(2,1)S(1)} %copy-done.20), channel_id=1, source_target_pairs={{0,3},{1,2},{2,1},{3,0},{4,7},{5,6},{6,5},{7,4},{8,11},{9,10},{10,... | collective-permute-start | bytes 393224 | tf_op jit(solution)/shard_map/ppermute | solution.py:278
  21.1 22.4 %copy-start.7 = (bf16[256,256]{1,0:T(8,128)(2,1)}, bf16[256,256]{1,0:T(8,128)(2,1)S(1)}, u32[]{:S(2)}) copy-start(bf16[256,256]{1,0:T(8,128)(2,1)S(1)} %collective-permute-done.12.refs_14_) | copy-start | bytes 393220
  21.1 20.8 %collective-permute-start.14 = (bf16[4,256,256]{2,1,0:T(8,128)(2,1)S(1)}, bf16[4,256,256]{2,1,0:T(8,128)(2,1)S(1)}, u32[]{:S(2)}, u32[]{:S(2)}) collective-permute-start(bf16[4,256,256]{2,1,0:T(8,128)(2,1)S(1)} %pad_maximum_fusion), channel_id=1, source_target_pairs={{4,12},{5,13},{6,14},{7,15},{8,0},{9,1},{10,2},{11,3},{12,20},{13,... | collective-permute-start | bytes 1572872 | tf_op jit(solution)/shard_map/ppermute | solution.py:291
  22.4 19.5 %copy-start.8 = (bf16[256,256]{1,0:T(8,128)(2,1)}, bf16[256,256]{1,0:T(8,128)(2,1)S(1)}, u32[]{:S(2)}) copy-start(bf16[256,256]{1,0:T(8,128)(2,1)S(1)} %collective-permute-done.13.refs_15_) | copy-start | bytes 393220
  22.5 19.4 %collective-permute-start.15 = (bf16[4,256,256]{2,1,0:T(8,128)(2,1)S(1)}, bf16[4,256,256]{2,1,0:T(8,128)(2,1)S(1)}, u32[]{:S(2)}, u32[]{:S(2)}) collective-permute-start(bf16[4,256,256]{2,1,0:T(8,128)(2,1)S(1)} %pad_maximum_fusion.1), channel_id=1, source_target_pairs={{0,8},{1,9},{2,10},{3,11},{8,16},{9,17},{10,18},{11,19},{12,4},{13... | collective-permute-start | bytes 1572872 | tf_op jit(solution)/shard_map/ppermute | solution.py:291
  27.2 16.3 %copy-start.10 = (s32[32]{0:T(128)}, s32[32]{0:T(128)S(1)}, u32[]{:S(2)}) copy-start(s32[32]{0:T(128)S(1)} %get-tuple-element.49.counts_ref) | copy-start | bytes 388
  27.2 16.3 %copy-start.13 = (bf16[256,256]{1,0:T(8,128)(2,1)}, bf16[256,256]{1,0:T(8,128)(2,1)S(1)}, u32[]{:S(2)}) copy-start(bf16[256,256]{1,0:T(8,128)(2,1)S(1)} %collective-permute-done.refs_1_) | copy-start | bytes 393220
  27.3 9.3 %collective-permute-start.3 = (bf16[256,256]{1,0:T(8,128)(2,1)S(1)}, bf16[256,256]{1,0:T(8,128)(2,1)S(1)}, u32[]{:S(2)}, u32[]{:S(2)}) collective-permute-start(bf16[256,256]{1,0:T(8,128)(2,1)S(1)} %copy-done.18), channel_id=1, source_target_pairs={{0,4},{1,5},{2,6},{3,7},{4,0},{5,1},{6,2},{7,3},{8,12},{9,13},{10,... | collective-permute-start | bytes 393224 | tf_op jit(solution)/shard_map/ppermute | solution.py:278
  27.5 16.0 %copy-start.14 = (bf16[256,256]{1,0:T(8,128)(2,1)}, bf16[256,256]{1,0:T(8,128)(2,1)S(1)}, u32[]{:S(2)}) copy-start(bf16[256,256]{1,0:T(8,128)(2,1)S(1)} %collective-permute-done.1.refs_2_) | copy-start | bytes 393220
  27.5 11.1 %collective-permute-start.4 = (bf16[256,256]{1,0:T(8,128)(2,1)}, bf16[256,256]{1,0:T(8,128)(2,1)S(1)}, u32[]{:S(2)}, u32[]{:S(2)}) collective-permute-start(bf16[256,256]{1,0:T(8,128)(2,1)} %get-tuple-element.28), channel_id=1, source_target_pairs={{0,5},{1,4},{2,7},{3,6},{4,1},{5,0},{6,3},{7,2},{8,13},{9,12},{10,... | collective-permute-start | bytes 393224 | tf_op jit(solution)/shard_map/ppermute | solution.py:278
  31.0 12.6 %copy-start.15 = (bf16[256,256]{1,0:T(8,128)(2,1)}, bf16[256,256]{1,0:T(8,128)(2,1)S(1)}, u32[]{:S(2)}) copy-start(bf16[256,256]{1,0:T(8,128)(2,1)S(1)} %collective-permute-done.2.refs_3_) | copy-start | bytes 393220
  31.0 7.7 %collective-permute-start.5 = (bf16[256,256]{1,0:T(8,128)(2,1)S(1)}, bf16[256,256]{1,0:T(8,128)(2,1)}, u32[]{:S(2)}, u32[]{:S(2)}) collective-permute-start(bf16[256,256]{1,0:T(8,128)(2,1)S(1)} %copy-done.17), channel_id=1, source_target_pairs={{0,6},{1,7},{2,4},{3,5},{4,2},{5,3},{6,0},{7,1},{8,14},{9,15},{10,... | collective-permute-start | bytes 393224 | tf_op jit(solution)/shard_map/ppermute | solution.py:278
  36.5 0.6 copy-start.19
  36.5 5.4 %collective-permute-start.6 = (bf16[256,256]{1,0:T(8,128)(2,1)S(1)}, bf16[256,256]{1,0:T(8,128)(2,1)}, u32[]{:S(2)}, u32[]{:S(2)}) collective-permute-start(bf16[256,256]{1,0:T(8,128)(2,1)S(1)} %copy-done.16), channel_id=1, source_target_pairs={{0,7},{1,6},{2,5},{3,4},{4,3},{5,2},{6,1},{7,0},{8,15},{9,14},{10,... | collective-permute-start | bytes 393224 | tf_op jit(solution)/shard_map/ppermute | solution.py:278
  38.6 3.3 %copy-start.22 = (bf16[256,256]{1,0:T(8,128)(2,1)}, bf16[256,256]{1,0:T(8,128)(2,1)S(1)}, u32[]{:S(2)}) copy-start(bf16[256,256]{1,0:T(8,128)(2,1)S(1)} %collective-permute-done.4.refs_5_) | copy-start | bytes 393220
  41.9 0.8 copy-start.11
  42.7 0.8 copy-start.12
  57.5 19.2 %copy-start = (bf16[2048,256]{1,0:T(8,128)(2,1)S(1)}, bf16[2048,256]{1,0:T(8,128)(2,1)}, u32[]{:S(2)}) copy-start(bf16[2048,256]{1,0:T(8,128)(2,1)} %get-tuple-element.40) | copy-start | bytes 3145732
  57.6 15.2 %collective-permute-start.16 = (bf16[1024,256]{1,0:T(8,128)(2,1)}, bf16[1024,256]{1,0:T(8,128)(2,1)S(1)}, u32[]{:S(2)}, u32[]{:S(2)}) collective-permute-start(bf16[1024,256]{1,0:T(8,128)(2,1)} %get-tuple-element.41), channel_id=1, source_target_pairs={{0,8},{8,16},{16,24},{1,9},{9,17},{17,25},{2,10},{10,18},{18,26},{... | collective-permute-start | bytes 1572872 | tf_op jit(solution)/shard_map/ppermute | solution.py:307
  62.5 14.3 %collective-permute-start.17 = (bf16[1024,256]{1,0:T(8,128)(2,1)}, bf16[1024,256]{1,0:T(8,128)(2,1)S(1)}, u32[]{:S(2)}, u32[]{:S(2)}) collective-permute-start(bf16[1024,256]{1,0:T(8,128)(2,1)} %get-tuple-element.42), channel_id=1, source_target_pairs={{8,0},{16,8},{24,16},{9,1},{17,9},{25,17},{10,2},{18,10},{26,18},{... | collective-permute-start | bytes 1572872 | tf_op jit(solution)/shard_map/ppermute | solution.py:306
  63.8 14.2 %all-to-all-start = ((bf16[8,256,128]{2,1,0:T(8,128)(2,1)}), bf16[8,256,128]{2,1,0:T(8,128)(2,1)S(1)}, u32[]{:S(2)}, u32[]{:S(2)}) async-start(bf16[8,256,128]{2,1,0:T(8,128)(2,1)} %get-tuple-element.39), calls=%async_computation | async-start | bytes 1048576 | tf_op jit(solution)/shard_map/all_to_all | solution.py:271
  78.0 19.4 %all-to-all-start.1 = ((bf16[8,256,256]{2,1,0:T(8,128)(2,1)}), bf16[8,256,256]{2,1,0:T(8,128)(2,1)S(1)}, u32[]{:S(2)}, u32[]{:S(2)}) async-start(bf16[8,256,256]{2,1,0:T(8,128)(2,1)} %bitcast.11), calls=%async_computation.1 | async-start | bytes 2097152 | tf_op jit(solution)/shard_map/all_to_all | solution.py:271
where the time goes:
time: 98.9 us
  waiting for transfers between devices  35.5 us (36%)
  starting transfers between devices  35.2 us (36%)
  Pallas kernels  18.2 us (18%)
  local copies, waits for them, and re-layouts  6.29 us (6%)
  other arithmetic  2.58 us (3%)
  between operations  1.06 us (1%)
    ppermute x14, starting transfers between devices, send(): return lax.ppermute(slab, group, [(i, i ^ k) for i in range(peers)])  15.1 us
    pallas_call x1, Pallas kernels, attend(): pl.pallas_call(attend_kernel, out_shape=(shaped((peers, rows // peers, LA...  14 us
    all_to_all x2, waiting for transfers between devices, exchange(): return lax.all_to_all(parts, group, split_axis=0, concat_axis=0, tiled=True)  13.7 us
    ppermute x14, waiting for transfers between devices, send(): return lax.ppermute(slab, group, [(i, i ^ k) for i in range(peers)])  12.3 us
    all_to_all x2, starting transfers between devices, exchange(): return lax.all_to_all(parts, group, split_axis=0, concat_axis=0, tiled=True)  7.99 us
    ppermute x2, starting transfers between devices, beside(): return lax.ppermute(slabs, ('outer',) + group, pairs)  5.92 us
    ppermute x1, waiting for transfers between devices, on_device(): from_below = lax.ppermute(grad_right, 'outer', up)  5.41 us
    ppermute x1, starting transfers between devices, on_device(): from_below = lax.ppermute(grad_right, 'outer', up)  4.96 us
  transfers between devices with their start and end apart: 20, of which 8 were waited for; matrix products, arithmetic and copies ran while one was open for 5% of the time, Pallas kernels for 2%

commit v1 on v0

--- a/solution.py
+++ b/solution.py
@@ -12,7 +12,7 @@
 PERSONS_GROUP = 4
 CHUNK = 4
 STEP = 4
-SENDS = (5, 6, 1, 7, 4, 3, 2)
+SENDS = (4, 1, 5, 6, 3, 7, 2)
 VMEM_BYTES = 63 * 1024 * 1024
 LANES = 2 * HEAD_DIM
 masked_value = -1e30
@@ -98,11 +98,11 @@
         return pl.ds(pl.multiple_of(base + slab * piece, piece), piece)
 
     copies = []
-    for k in range(peers):
+    for place, k in enumerate((0,) + SENDS):
         spot = rows_at(0, me ^ k)
-        copies.append(pltpu.make_async_copy(qd_refs[k], qd.at[spot, :], in_sems.at[0, k]))
+        copies.append(pltpu.make_async_copy(qd_refs[place], qd.at[spot, :], in_sems.at[0, k]))
         spot = rows_at(halo, me ^ k)
-        copies.append(pltpu.make_async_copy(own_refs[k], kv.at[spot, :], in_sems.at[1, k]))
+        copies.append(pltpu.make_async_copy(own_refs[place], kv.at[spot, :], in_sems.at[1, k]))
     for k in range(edge):
         spot = rows_at(jnp.where(lower, halo + own, 0), (me ^ k) % edge)
         copies.append(pltpu.make_async_copy(near_ref.at[k], kv.at[spot, :], in_sems.at[2, k]))
@@ -300,6 +300,7 @@
     lists, counts, order = compact_lists(
         pair_blocks, pair_count, first, blocks, first - halo_blocks, blocks + 2 * halo_blocks
     )
+    qd, own = ([slabs[k] for k in (0,) + SENDS] for slabs in (qd, own))
     dq, grad_left, grad_own, grad_right = attend(
         my_slab, lists, counts, order, qd, own, near, across
     )

time: 98.9 us -> 96.6 us (0.977)
  starting transfers between devices: 35.2 us -> 32.6 us
  local copies, waits for them, and re-layouts: 6.29 us -> 4.23 us
  Pallas kernels: 18.2 us -> 19.3 us
    ppermute x2, waiting for transfers between devices: 0.01 us -> 3 us  [beside(): return lax.ppermute(slabs, ('outer',) + group, pairs)]
    unnamed x50 -> x46, local copies, waits for them, and re-layouts: 4.19 us -> 2.14 us
    ppermute x14, waiting for transfers between devices: 12.3 us -> 10.6 us  [send(): return lax.ppermute(slab, group, [(i, i ^ k) for i in range(peers)])]
    pallas_call x1, Pallas kernels: 14 us -> 15 us  [attend(): pl.pallas_call(attend_kernel, out_shape=(shaped((peers, rows // peers, LA...]
where the time goes in v1:
time: 96.6 us; the launch traced here: 96 us
  waiting for transfers between devices  36.1 us (37%)
  starting transfers between devices  32.6 us (34%)
  Pallas kernels  19.3 us (20%)
  local copies, waits for them, and re-layouts  4.23 us (4%)
  other arithmetic  2.6 us (3%)
  between operations  1.04 us (1%)
    pallas_call x1, Pallas kernels, attend(): pl.pallas_call(attend_kernel, out_shape=(shaped((peers, rows // peers, LA...  15 us
    ppermute x14, starting transfers between devices, send(): return lax.ppermute(slab, group, [(i, i ^ k) for i in range(peers)])  14.9 us
    all_to_all x2, waiting for transfers between devices, exchange(): return lax.all_to_all(parts, group, split_axis=0, concat_axis=0, tiled=True)  13.6 us
    ppermute x14, waiting for transfers between devices, send(): return lax.ppermute(slab, group, [(i, i ^ k) for i in range(peers)])  10.6 us
    all_to_all x2, starting transfers between devices, exchange(): return lax.all_to_all(parts, group, split_axis=0, concat_axis=0, tiled=True)  7.06 us
    ppermute x2, starting transfers between devices, beside(): return lax.ppermute(slabs, ('outer',) + group, pairs)  5.19 us
    ppermute x1, waiting for transfers between devices, on_device(): from_below = lax.ppermute(grad_right, 'outer', up)  4.87 us
    pallas_call x2, Pallas kernels, join_columns(): pl.pallas_call(pack_kernel, out_shape=[slab] * peers, in_specs=[pl.BlockS...  4.29 us
  transfers between devices with their start and end apart: 20, of which 8 were waited for; matrix products, arithmetic and copies ran while one was open for 5% of the time, Pallas kernels for 2%

profile of v1, /device:TPU:0, one launch (start us, length us, event | category | flops | bytes accessed | tf_op | source)
XLA Modules:
  0.0 96.0 jit_solution(2365257125245169468)
XLA Ops:
  0.7 2.1 %pack.3 = (bf16[256,256]{1,0:T(8,128)(2,1)}, bf16[256,256]{1,0:T(8,128)(2,1)}, bf16[256,256]{1,0:T(8,128)(2,1)}, bf16[256,256]{1,0:T(8,128)(2,1)}, bf16[256,256]...) custom-call(s32[1]{0:T(128)} %bitcast.me_ref, ...), custom_call_target="tpu_custom_call" | custom-call | bytes 2000000 | tf_op jit(solution)/shard_map/pack/pallas_call | solution.py:225
  2.8 3.0 %collective-permute-start.7 = (bf16[256,256]{1,0:T(8,128)(2,1)}, bf16[256,256]{1,0:T(8,128)(2,1)S(1)}, u32[]{:S(2)}, u32[]{:S(2)}) collective-permute-start(bf16[256,256]{1,0:T(8,128)(2,1)} %get-tuple-element.32), channel_id=1, source_target_pairs={{0,4},{1,5},{2,6},{3,7},{4,0},{5,1},{6,2},{7,3},{8,12},{9,13},{10,... | collective-permute-start | bytes 393224 | tf_op jit(solution)/shard_map/ppermute | solution.py:278
  5.8 1.5 %collective-permute-start.8 = (bf16[256,256]{1,0:T(8,128)(2,1)}, bf16[256,256]{1,0:T(8,128)(2,1)S(1)}, u32[]{:S(2)}, u32[]{:S(2)}) collective-permute-start(bf16[256,256]{1,0:T(8,128)(2,1)} %get-tuple-element.33), channel_id=1, source_target_pairs={{0,1},{1,0},{2,3},{3,2},{4,5},{5,4},{6,7},{7,6},{8,9},{9,8},{10,11... | collective-permute-start | bytes 393224 | tf_op jit(solution)/shard_map/ppermute | solution.py:278
  7.3 0.0 collective-permute-start.9
  7.4 0.5 collective-permute-start.10
  7.9 2.6 %collective-permute-start.12 = (bf16[256,256]{1,0:T(8,128)(2,1)}, bf16[256,256]{1,0:T(8,128)(2,1)S(1)}, u32[]{:S(2)}, u32[]{:S(2)}) collective-permute-start(bf16[256,256]{1,0:T(8,128)(2,1)} %get-tuple-element.37), channel_id=1, source_target_pairs={{0,7},{1,6},{2,5},{3,4},{4,3},{5,2},{6,1},{7,0},{8,15},{9,14},{10,... | collective-permute-start | bytes 393224 | tf_op jit(solution)/shard_map/ppermute | solution.py:278
  10.5 0.1 subtract_clamp_fusion
  10.6 0.0 collective-permute-done.7.refs_9_
  10.6 0.1 collective-permute-start.11
  10.7 4.3 %collective-permute-done.9.refs_11_ = bf16[256,256]{1,0:T(8,128)(2,1)S(1)} collective-permute-done((bf16[256,256]{1,0:T(8,128)(2,1)}, bf16[256,256]{1,0:T(8,128)(2,1)S(1)}, u32[]{:S(2)}, u32[]{:S(2)}) %collective-permute-start.9) | collective-permute-done | bytes 131104 | tf_op jit(solution)/shard_map/ppermute | solution.py:278
  15.0 0.0 collective-permute-start.13
  15.0 0.1 and_reduce_fusion
  15.1 0.1 dynamic_slice.6
  15.2 2.2 %pack.2 = (bf16[256,256]{1,0:T(8,128)(2,1)}, bf16[256,256]{1,0:T(8,128)(2,1)}, bf16[256,256]{1,0:T(8,128)(2,1)}, bf16[256,256]{1,0:T(8,128)(2,1)}, bf16[256,256]...) custom-call(s32[1]{0:T(128)} %bitcast.me_ref, ...), custom_call_target="tpu_custom_call" | custom-call | bytes 2000000 | tf_op jit(solution)/shard_map/pack/pallas_call | solution.py:225
  17.4 1.3 %collective-permute-done.10.refs_12_ = bf16[256,256]{1,0:T(8,128)(2,1)S(1)} collective-permute-done((bf16[256,256]{1,0:T(8,128)(2,1)}, bf16[256,256]{1,0:T(8,128)(2,1)S(1)}, u32[]{:S(2)}, u32[]{:S(2)}) %collective-permute-start.10) | collective-permute-done | bytes 131104 | tf_op jit(solution)/shard_map/ppermute | solution.py:278
  18.6 1.1 %collective-permute-start = (bf16[256,256]{1,0:T(8,128)(2,1)}, bf16[256,256]{1,0:T(8,128)(2,1)S(1)}, u32[]{:S(2)}, u32[]{:S(2)}) collective-permute-start(bf16[256,256]{1,0:T(8,128)(2,1)} %get-tuple-element.24), channel_id=1, source_target_pairs={{0,4},{1,5},{2,6},{3,7},{4,0},{5,1},{6,2},{7,3},{8,12},{9,13},{10,... | collective-permute-start | bytes 393224 | tf_op jit(solution)/shard_map/ppermute | solution.py:278
  19.8 1.5 %collective-permute-start.1 = (bf16[256,256]{1,0:T(8,128)(2,1)}, bf16[256,256]{1,0:T(8,128)(2,1)S(1)}, u32[]{:S(2)}, u32[]{:S(2)}) collective-permute-start(bf16[256,256]{1,0:T(8,128)(2,1)} %get-tuple-element.25), channel_id=1, source_target_pairs={{0,1},{1,0},{2,3},{3,2},{4,5},{5,4},{6,7},{7,6},{8,9},{9,8},{10,11... | collective-permute-start | bytes 393224 | tf_op jit(solution)/shard_map/ppermute | solution.py:278
  21.3 0.1 pad_maximum_fusion.1
  21.4 0.9 collective-permute-start.2
  22.3 3.9 %collective-permute-start.15 = (bf16[4,256,256]{2,1,0:T(8,128)(2,1)S(1)}, bf16[4,256,256]{2,1,0:T(8,128)(2,1)S(1)}, u32[]{:S(2)}, u32[]{:S(2)}) collective-permute-start(bf16[4,256,256]{2,1,0:T(8,128)(2,1)S(1)} %pad_maximum_fusion.1), channel_id=1, source_target_pairs={{0,8},{1,9},{2,10},{3,11},{8,16},{9,17},{10,18},{11,19},{12,4},{13... | collective-permute-start | bytes 1572872 | tf_op jit(solution)/shard_map/ppermute | solution.py:291
  26.3 0.1 pad_maximum_fusion
  26.4 1.3 %collective-permute-start.14 = (bf16[4,256,256]{2,1,0:T(8,128)(2,1)S(1)}, bf16[4,256,256]{2,1,0:T(8,128)(2,1)S(1)}, u32[]{:S(2)}, u32[]{:S(2)}) collective-permute-start(bf16[4,256,256]{2,1,0:T(8,128)(2,1)S(1)} %pad_maximum_fusion), channel_id=1, source_target_pairs={{4,12},{5,13},{6,14},{7,15},{8,0},{9,1},{10,2},{11,3},{12,20},{13,... | collective-permute-start | bytes 1572872 | tf_op jit(solution)/shard_map/ppermute | solution.py:291
  27.7 0.1 collective-permute-start.3
  27.8 0.1 select_reduce_fusion.1
  28.0 3.1 %collective-permute-start.4 = (bf16[256,256]{1,0:T(8,128)(2,1)}, bf16[256,256]{1,0:T(8,128)(2,1)S(1)}, u32[]{:S(2)}, u32[]{:S(2)}) collective-permute-start(bf16[256,256]{1,0:T(8,128)(2,1)} %get-tuple-element.28), channel_id=1, source_target_pairs={{0,3},{1,2},{2,1},{3,0},{4,7},{5,6},{6,5},{7,4},{8,11},{9,10},{10,... | collective-permute-start | bytes 393224 | tf_op jit(solution)/shard_map/ppermute | solution.py:278
  31.1 2.2 %collective-permute-done.3.refs_4_ = bf16[256,256]{1,0:T(8,128)(2,1)S(1)} collective-permute-done((bf16[256,256]{1,0:T(8,128)(2,1)S(1)}, bf16[256,256]{1,0:T(8,128)(2,1)S(1)}, u32[]{:S(2)}, u32[]{:S(2)}) %collective-permute-start.3) | collective-permute-done | bytes 131104 | tf_op jit(solution)/shard_map/ppermute | solution.py:278
  33.3 0.4 collective-permute-start.6
  33.7 0.2 convert_reduce_fusion
  33.9 0.7 copy.19.lists_ref
  34.6 0.7 select_reduce_fusion.2.order_ref
  35.2 2.8 %collective-permute-done.5.refs_6_ = bf16[256,256]{1,0:T(8,128)(2,1)S(1)} collective-permute-done((bf16[256,256]{1,0:T(8,128)(2,1)}, bf16[256,256]{1,0:T(8,128)(2,1)S(1)}, u32[]{:S(2)}, u32[]{:S(2)}) %collective-permute-start.5) | collective-permute-done | bytes 131104 | tf_op jit(solution)/shard_map/ppermute | solution.py:278
  38.1 0.0 copy-start.11
  38.1 3.0 %collective-permute-done.14.refs_16_ = bf16[4,256,256]{2,1,0:T(8,128)(2,1)S(1)} collective-permute-done((bf16[4,256,256]{2,1,0:T(8,128)(2,1)S(1)}, bf16[4,256,256]{2,1,0:T(8,128)(2,1)S(1)}, u32[]{:S(2)}, u32[]{:S(2)}) %collective-permute-start.14) | collective-permute-done | bytes 524320 | tf_op jit(solution)/shard_map/ppermute | solution.py:291
  41.1 0.0 copy-start.12
  41.1 0.8 copy-done.12
  41.9 15.0 %attend.1 = (bf16[8,256,128]{2,1,0:T(8,128)(2,1)}, bf16[1024,256]{1,0:T(8,128)(2,1)}, bf16[2048,256]{1,0:T(8,128)(2,1)}, bf16[1024,256]{1,0:T(8,128)(2,1)}) custom-call(s32[1]{0:T(128)} %bitcast.me_ref, s32[32,16]{1,0:T(8,128)} %copy.19.lists_ref, s32[32]{0:T(128)} %copy-done.10, s32[32]{0:T(128)} %select_reduce_fusion.2.order_ref, ...), custom_call_target="tpu_custom_call" | custom-call | flops 4000000000 | bytes 6000000 | tf_op jit(solution)/shard_map/attend/pallas_call | solution.py:161
  57.0 4.2 %collective-permute-start.16 = (bf16[1024,256]{1,0:T(8,128)(2,1)}, bf16[1024,256]{1,0:T(8,128)(2,1)S(1)}, u32[]{:S(2)}, u32[]{:S(2)}) collective-permute-start(bf16[1024,256]{1,0:T(8,128)(2,1)} %get-tuple-element.41), channel_id=1, source_target_pairs={{0,8},{8,16},{16,24},{1,9},{9,17},{17,25},{2,10},{10,18},{18,26},{... | collective-permute-start | bytes 1572872 | tf_op jit(solution)/shard_map/ppermute | solution.py:308
  61.2 1.3 %collective-permute-start.17 = (bf16[1024,256]{1,0:T(8,128)(2,1)}, bf16[1024,256]{1,0:T(8,128)(2,1)S(1)}, u32[]{:S(2)}, u32[]{:S(2)}) collective-permute-start(bf16[1024,256]{1,0:T(8,128)(2,1)} %get-tuple-element.42), channel_id=1, source_target_pairs={{8,0},{16,8},{24,16},{9,1},{17,9},{25,17},{10,2},{18,10},{26,18},{... | collective-permute-start | bytes 1572872 | tf_op jit(solution)/shard_map/ppermute | solution.py:307
  62.5 3.5 %all-to-all-start = ((bf16[8,256,128]{2,1,0:T(8,128)(2,1)}), bf16[8,256,128]{2,1,0:T(8,128)(2,1)S(1)}, u32[]{:S(2)}, u32[]{:S(2)}) async-start(bf16[8,256,128]{2,1,0:T(8,128)(2,1)} %get-tuple-element.39), calls=%async_computation | async-start | bytes 1048576 | tf_op jit(solution)/shard_map/all_to_all | solution.py:271
  66.0 4.9 %collective-permute-done.16 = bf16[1024,256]{1,0:T(8,128)(2,1)S(1)} collective-permute-done((bf16[1024,256]{1,0:T(8,128)(2,1)}, bf16[1024,256]{1,0:T(8,128)(2,1)S(1)}, u32[]{:S(2)}, u32[]{:S(2)}) %collective-permute-start.16) | collective-permute-done | bytes 524320 | tf_op jit(solution)/shard_map/ppermute | solution.py:308
  70.9 4.0 %collective-permute-done.17 = bf16[1024,256]{1,0:T(8,128)(2,1)S(1)} collective-permute-done((bf16[1024,256]{1,0:T(8,128)(2,1)}, bf16[1024,256]{1,0:T(8,128)(2,1)S(1)}, u32[]{:S(2)}, u32[]{:S(2)}) %collective-permute-start.17) | collective-permute-done | bytes 524320 | tf_op jit(solution)/shard_map/ppermute | solution.py:307
  74.9 1.2 %add_convert_fusion = bf16[2048,256]{1,0:T(8,128)(2,1)} fusion(bf16[2048,256]{1,0:T(8,128)(2,1)S(1)} %copy-done, bf16[1024,256]{1,0:T(8,128)(2,1)S(1)} %collective-permute-done.17, bf16[1024,256]{1,0:T(8,128)(2,1)S(1)} %collective-permute-done.16), kind=kLoop, calls=%fused_computation | loop fusion | flops 3670016 | bytes 3145728 | tf_op jit(solution)/shard_map/convert_element_type | solution.py:311
  76.1 3.6 %all-to-all-start.1 = ((bf16[8,256,256]{2,1,0:T(8,128)(2,1)}), bf16[8,256,256]{2,1,0:T(8,128)(2,1)S(1)}, u32[]{:S(2)}, u32[]{:S(2)}) async-start(bf16[8,256,256]{2,1,0:T(8,128)(2,1)} %bitcast.11), calls=%async_computation.1 | async-start | bytes 2097152 | tf_op jit(solution)/shard_map/all_to_all | solution.py:271
  79.7 0.2 copy.20
  79.9 1.0 %copy.23 = bf16[256,1024]{1,0:T(8,128)(2,1)} copy(bf16[256,1024]{0,1:T(8,128)(2,1)S(1)} %bitcast.23) | data formatting | bytes 1048576
  80.9 13.6 %all-to-all-done.1 = bf16[8,256,256]{2,1,0:T(8,128)(2,1)S(1)} async-done(((bf16[8,256,256]{2,1,0:T(8,128)(2,1)}), bf16[8,256,256]{2,1,0:T(8,128)(2,1)S(1)}, u32[]{:S(2)}, u32[]{:S(2)}) %all-to-all-start.1) | async-done | bytes 1048608 | tf_op jit(solution)/shard_map/all_to_all | solution.py:271
  94.6 0.3 slice_bitcast_fusion
  94.8 1.1 %copy_bitcast_fusion = (bf16[256,1024]{1,0:T(8,128)(2,1)}, bf16[256,1024]{1,0:T(8,128)(2,1)}) fusion(bf16[8,32,8,128]{3,2,1,0:T(8,128)(2,1)S(1)} %get-tuple-element.51, bf16[8,32,8,128]{3,2,1,0:T(8,128)(2,1)S(1)} %get-tuple-element.52), kind=kLoop, calls=%fused_computation.1 | loop fusion | bytes 2097152 | tf_op jit(solution)/shard_map/reshape | solution.py:315
  (57 shorter events, 0.2 us)
Async XLA Ops:
  0.6 9.9 %copy-start.9 = (s32[128,16]{0,1:T(8,128)S(1)}, s32[128,16]{0,1:T(8,128)}, u32[]{:S(2)}) copy-start(s32[128,16]{0,1:T(8,128)} %param.10) | copy-start | bytes 24580
  0.6 14.5 %copy-start.21 = (s32[128]{0:T(128)S(1)}, s32[128]{0:T(128)}, u32[]{:S(2)}) copy-start(s32[128]{0:T(128)} %param.11) | copy-start | bytes 1540
  2.8 7.8 %collective-permute-start.7 = (bf16[256,256]{1,0:T(8,128)(2,1)}, bf16[256,256]{1,0:T(8,128)(2,1)S(1)}, u32[]{:S(2)}, u32[]{:S(2)}) collective-permute-start(bf16[256,256]{1,0:T(8,128)(2,1)} %get-tuple-element.32), channel_id=1, source_target_pairs={{0,4},{1,5},{2,6},{3,7},{4,0},{5,1},{6,2},{7,3},{8,12},{9,13},{10,... | collective-permute-start | bytes 393224 | tf_op jit(solution)/shard_map/ppermute | solution.py:278
  5.8 15.5 %collective-permute-start.8 = (bf16[256,256]{1,0:T(8,128)(2,1)}, bf16[256,256]{1,0:T(8,128)(2,1)S(1)}, u32[]{:S(2)}, u32[]{:S(2)}) collective-permute-start(bf16[256,256]{1,0:T(8,128)(2,1)} %get-tuple-element.33), channel_id=1, source_target_pairs={{0,1},{1,0},{2,3},{3,2},{4,5},{5,4},{6,7},{7,6},{8,9},{9,8},{10,11... | collective-permute-start | bytes 393224 | tf_op jit(solution)/shard_map/ppermute | solution.py:278
  7.3 7.6 %collective-permute-start.9 = (bf16[256,256]{1,0:T(8,128)(2,1)}, bf16[256,256]{1,0:T(8,128)(2,1)S(1)}, u32[]{:S(2)}, u32[]{:S(2)}) collective-permute-start(bf16[256,256]{1,0:T(8,128)(2,1)} %get-tuple-element.34), channel_id=1, source_target_pairs={{0,5},{1,4},{2,7},{3,6},{4,1},{5,0},{6,3},{7,2},{8,13},{9,12},{10,... | collective-permute-start | bytes 393224 | tf_op jit(solution)/shard_map/ppermute | solution.py:278
  7.4 11.2 %collective-permute-start.10 = (bf16[256,256]{1,0:T(8,128)(2,1)}, bf16[256,256]{1,0:T(8,128)(2,1)S(1)}, u32[]{:S(2)}, u32[]{:S(2)}) collective-permute-start(bf16[256,256]{1,0:T(8,128)(2,1)} %get-tuple-element.35), channel_id=1, source_target_pairs={{0,6},{1,7},{2,4},{3,5},{4,2},{5,3},{6,0},{7,1},{8,14},{9,15},{10,... | collective-permute-start | bytes 393224 | tf_op jit(solution)/shard_map/ppermute | solution.py:278
  7.9 11.9 %collective-permute-start.12 = (bf16[256,256]{1,0:T(8,128)(2,1)}, bf16[256,256]{1,0:T(8,128)(2,1)S(1)}, u32[]{:S(2)}, u32[]{:S(2)}) collective-permute-start(bf16[256,256]{1,0:T(8,128)(2,1)} %get-tuple-element.37), channel_id=1, source_target_pairs={{0,7},{1,6},{2,5},{3,4},{4,3},{5,2},{6,1},{7,0},{8,15},{9,14},{10,... | collective-permute-start | bytes 393224 | tf_op jit(solution)/shard_map/ppermute | solution.py:278
  10.6 10.8 %copy-start.2 = (bf16[256,256]{1,0:T(8,128)(2,1)}, bf16[256,256]{1,0:T(8,128)(2,1)S(1)}, u32[]{:S(2)}) copy-start(bf16[256,256]{1,0:T(8,128)(2,1)S(1)} %collective-permute-done.7.refs_9_) | copy-start | bytes 393220
  10.6 11.7 %collective-permute-start.11 = (bf16[256,256]{1,0:T(8,128)(2,1)}, bf16[256,256]{1,0:T(8,128)(2,1)S(1)}, u32[]{:S(2)}, u32[]{:S(2)}) collective-permute-start(bf16[256,256]{1,0:T(8,128)(2,1)} %get-tuple-element.36), channel_id=1, source_target_pairs={{0,3},{1,2},{2,1},{3,0},{4,7},{5,6},{6,5},{7,4},{8,11},{9,10},{10,... | collective-permute-start | bytes 393224 | tf_op jit(solution)/shard_map/ppermute | solution.py:278
  15.0 6.4 %copy-start.4 = (bf16[256,256]{1,0:T(8,128)(2,1)}, bf16[256,256]{1,0:T(8,128)(2,1)S(1)}, u32[]{:S(2)}) copy-start(bf16[256,256]{1,0:T(8,128)(2,1)S(1)} %collective-permute-done.9.refs_11_) | copy-start | bytes 393220
  15.0 11.3 %collective-permute-start.13 = (bf16[256,256]{1,0:T(8,128)(2,1)}, bf16[256,256]{1,0:T(8,128)(2,1)S(1)}, u32[]{:S(2)}, u32[]{:S(2)}) collective-permute-start(bf16[256,256]{1,0:T(8,128)(2,1)} %get-tuple-element.38), channel_id=1, source_target_pairs={{0,2},{1,3},{2,0},{3,1},{4,6},{5,7},{6,4},{7,5},{8,10},{9,11},{10,... | collective-permute-start | bytes 393224 | tf_op jit(solution)/shard_map/ppermute | solution.py:278
  15.2 11.1 %copy-start.1 = (bf16[256,256]{1,0:T(8,128)(2,1)S(1)}, bf16[256,256]{1,0:T(8,128)(2,1)}, u32[]{:S(2)}) copy-start(bf16[256,256]{1,0:T(8,128)(2,1)} %get-tuple-element.31.refs_8_) | copy-start | bytes 393220
  17.4 4.0 %copy-start.18 = (bf16[256,256]{1,0:T(8,128)(2,1)S(1)}, bf16[256,256]{1,0:T(8,128)(2,1)}, u32[]{:S(2)}) copy-start(bf16[256,256]{1,0:T(8,128)(2,1)} %get-tuple-element.26) | copy-start | bytes 393220
  18.6 7.7 %copy-start.5 = (bf16[256,256]{1,0:T(8,128)(2,1)}, bf16[256,256]{1,0:T(8,128)(2,1)S(1)}, u32[]{:S(2)}) copy-start(bf16[256,256]{1,0:T(8,128)(2,1)S(1)} %collective-permute-done.10.refs_12_) | copy-start | bytes 393220
  18.6 9.1 %collective-permute-start = (bf16[256,256]{1,0:T(8,128)(2,1)}, bf16[256,256]{1,0:T(8,128)(2,1)S(1)}, u32[]{:S(2)}, u32[]{:S(2)}) collective-permute-start(bf16[256,256]{1,0:T(8,128)(2,1)} %get-tuple-element.24), channel_id=1, source_target_pairs={{0,4},{1,5},{2,6},{3,7},{4,0},{5,1},{6,2},{7,3},{8,12},{9,13},{10,... | collective-permute-start | bytes 393224 | tf_op jit(solution)/shard_map/ppermute | solution.py:278
  19.8 6.6 %copy-start.6 = (bf16[256,256]{1,0:T(8,128)(2,1)}, bf16[256,256]{1,0:T(8,128)(2,1)S(1)}, u32[]{:S(2)}) copy-start(bf16[256,256]{1,0:T(8,128)(2,1)S(1)} %collective-permute-done.12.refs_14_) | copy-start | bytes 393220
  19.8 8.2 %collective-permute-start.1 = (bf16[256,256]{1,0:T(8,128)(2,1)}, bf16[256,256]{1,0:T(8,128)(2,1)S(1)}, u32[]{:S(2)}, u32[]{:S(2)}) collective-permute-start(bf16[256,256]{1,0:T(8,128)(2,1)} %get-tuple-element.25), channel_id=1, source_target_pairs={{0,1},{1,0},{2,3},{3,2},{4,5},{5,4},{6,7},{7,6},{8,9},{9,8},{10,11... | collective-permute-start | bytes 393224 | tf_op jit(solution)/shard_map/ppermute | solution.py:278
  21.3 6.4 %copy-start.16 = (bf16[256,256]{1,0:T(8,128)(2,1)S(1)}, bf16[256,256]{1,0:T(8,128)(2,1)}, u32[]{:S(2)}) copy-start(bf16[256,256]{1,0:T(8,128)(2,1)} %get-tuple-element.27) | copy-start | bytes 393220
  21.4 20.5 %copy-start.3 = (bf16[256,256]{1,0:T(8,128)(2,1)}, bf16[256,256]{1,0:T(8,128)(2,1)S(1)}, u32[]{:S(2)}) copy-start(bf16[256,256]{1,0:T(8,128)(2,1)S(1)} %collective-permute-done.8.refs_10_) | copy-start | bytes 393220
  21.4 9.7 %collective-permute-start.2 = (bf16[256,256]{1,0:T(8,128)(2,1)S(1)}, bf16[256,256]{1,0:T(8,128)(2,1)S(1)}, u32[]{:S(2)}, u32[]{:S(2)}) collective-permute-start(bf16[256,256]{1,0:T(8,128)(2,1)S(1)} %copy-done.18), channel_id=1, source_target_pairs={{0,5},{1,4},{2,7},{3,6},{4,1},{5,0},{6,3},{7,2},{8,13},{9,12},{10,... | collective-permute-start | bytes 393224 | tf_op jit(solution)/shard_map/ppermute | solution.py:278
  22.3 19.6 %copy-start.7 = (bf16[256,256]{1,0:T(8,128)(2,1)}, bf16[256,256]{1,0:T(8,128)(2,1)S(1)}, u32[]{:S(2)}) copy-start(bf16[256,256]{1,0:T(8,128)(2,1)S(1)} %collective-permute-done.11.refs_13_) | copy-start | bytes 393220
  22.3 15.7 %collective-permute-start.15 = (bf16[4,256,256]{2,1,0:T(8,128)(2,1)S(1)}, bf16[4,256,256]{2,1,0:T(8,128)(2,1)S(1)}, u32[]{:S(2)}, u32[]{:S(2)}) collective-permute-start(bf16[4,256,256]{2,1,0:T(8,128)(2,1)S(1)} %pad_maximum_fusion.1), channel_id=1, source_target_pairs={{0,8},{1,9},{2,10},{3,11},{8,16},{9,17},{10,18},{11,19},{12,4},{13... | collective-permute-start | bytes 1572872 | tf_op jit(solution)/shard_map/ppermute | solution.py:291
  26.2 14.8 %copy-start.8 = (bf16[256,256]{1,0:T(8,128)(2,1)}, bf16[256,256]{1,0:T(8,128)(2,1)S(1)}, u32[]{:S(2)}) copy-start(bf16[256,256]{1,0:T(8,128)(2,1)S(1)} %collective-permute-done.13.refs_15_) | copy-start | bytes 393220
  26.4 14.7 %collective-permute-start.14 = (bf16[4,256,256]{2,1,0:T(8,128)(2,1)S(1)}, bf16[4,256,256]{2,1,0:T(8,128)(2,1)S(1)}, u32[]{:S(2)}, u32[]{:S(2)}) collective-permute-start(bf16[4,256,256]{2,1,0:T(8,128)(2,1)S(1)} %pad_maximum_fusion), channel_id=1, source_target_pairs={{4,12},{5,13},{6,14},{7,15},{8,0},{9,1},{10,2},{11,3},{12,20},{13,... | collective-permute-start | bytes 1572872 | tf_op jit(solution)/shard_map/ppermute | solution.py:291
  27.7 14.2 %copy-start.10 = (s32[32]{0:T(128)}, s32[32]{0:T(128)S(1)}, u32[]{:S(2)}) copy-start(s32[32]{0:T(128)S(1)} %get-tuple-element.49.counts_ref) | copy-start | bytes 388
  27.7 14.2 %copy-start.13 = (bf16[256,256]{1,0:T(8,128)(2,1)}, bf16[256,256]{1,0:T(8,128)(2,1)S(1)}, u32[]{:S(2)}) copy-start(bf16[256,256]{1,0:T(8,128)(2,1)S(1)} %collective-permute-done.refs_1_) | copy-start | bytes 393220
  27.7 5.6 %collective-permute-start.3 = (bf16[256,256]{1,0:T(8,128)(2,1)S(1)}, bf16[256,256]{1,0:T(8,128)(2,1)S(1)}, u32[]{:S(2)}, u32[]{:S(2)}) collective-permute-start(bf16[256,256]{1,0:T(8,128)(2,1)S(1)} %copy-done.16), channel_id=1, source_target_pairs={{0,6},{1,7},{2,4},{3,5},{4,2},{5,3},{6,0},{7,1},{8,14},{9,15},{10,... | collective-permute-start | bytes 393224 | tf_op jit(solution)/shard_map/ppermute | solution.py:278
  28.0 13.1 %copy-start.14 = (bf16[256,256]{1,0:T(8,128)(2,1)}, bf16[256,256]{1,0:T(8,128)(2,1)S(1)}, u32[]{:S(2)}) copy-start(bf16[256,256]{1,0:T(8,128)(2,1)S(1)} %collective-permute-done.1.refs_2_) | copy-start | bytes 393220
  28.0 7.2 %collective-permute-start.4 = (bf16[256,256]{1,0:T(8,128)(2,1)}, bf16[256,256]{1,0:T(8,128)(2,1)S(1)}, u32[]{:S(2)}, u32[]{:S(2)}) collective-permute-start(bf16[256,256]{1,0:T(8,128)(2,1)} %get-tuple-element.28), channel_id=1, source_target_pairs={{0,3},{1,2},{2,1},{3,0},{4,7},{5,6},{6,5},{7,4},{8,11},{9,10},{10,... | collective-permute-start | bytes 393224 | tf_op jit(solution)/shard_map/ppermute | solution.py:278
  31.1 10.0 %copy-start.15 = (bf16[256,256]{1,0:T(8,128)(2,1)}, bf16[256,256]{1,0:T(8,128)(2,1)S(1)}, u32[]{:S(2)}) copy-start(bf16[256,256]{1,0:T(8,128)(2,1)S(1)} %collective-permute-done.2.refs_3_) | copy-start | bytes 393220
  31.1 7.0 %collective-permute-start.5 = (bf16[256,256]{1,0:T(8,128)(2,1)}, bf16[256,256]{1,0:T(8,128)(2,1)S(1)}, u32[]{:S(2)}, u32[]{:S(2)}) collective-permute-start(bf16[256,256]{1,0:T(8,128)(2,1)} %get-tuple-element.29), channel_id=1, source_target_pairs={{0,7},{1,6},{2,5},{3,4},{4,3},{5,2},{6,1},{7,0},{8,15},{9,14},{10,... | collective-permute-start | bytes 393224 | tf_op jit(solution)/shard_map/ppermute | solution.py:278
  33.3 7.8 %copy-start.17 = (bf16[256,256]{1,0:T(8,128)(2,1)}, bf16[256,256]{1,0:T(8,128)(2,1)S(1)}, u32[]{:S(2)}) copy-start(bf16[256,256]{1,0:T(8,128)(2,1)S(1)} %collective-permute-done.3.refs_4_) | copy-start | bytes 393220
  33.3 4.7 %collective-permute-start.6 = (bf16[256,256]{1,0:T(8,128)(2,1)}, bf16[256,256]{1,0:T(8,128)(2,1)}, u32[]{:S(2)}, u32[]{:S(2)}) collective-permute-start(bf16[256,256]{1,0:T(8,128)(2,1)} %get-tuple-element.30), channel_id=1, source_target_pairs={{0,2},{1,3},{2,0},{3,1},{4,6},{5,7},{6,4},{7,5},{8,10},{9,11},{10,... | collective-permute-start | bytes 393224 | tf_op jit(solution)/shard_map/ppermute | solution.py:278
  35.2 5.9 %copy-start.19 = (bf16[256,256]{1,0:T(8,128)(2,1)}, bf16[256,256]{1,0:T(8,128)(2,1)S(1)}, u32[]{:S(2)}) copy-start(bf16[256,256]{1,0:T(8,128)(2,1)S(1)} %collective-permute-done.4.refs_5_) | copy-start | bytes 393220
  38.1 3.1 %copy-start.20 = (bf16[256,256]{1,0:T(8,128)(2,1)}, bf16[256,256]{1,0:T(8,128)(2,1)S(1)}, u32[]{:S(2)}) copy-start(bf16[256,256]{1,0:T(8,128)(2,1)S(1)} %collective-permute-done.5.refs_6_) | copy-start | bytes 393220
  38.1 3.1 %copy-start.11 = (bf16[4,256,256]{2,1,0:T(8,128)(2,1)}, bf16[4,256,256]{2,1,0:T(8,128)(2,1)S(1)}, u32[]{:S(2)}) copy-start(bf16[4,256,256]{2,1,0:T(8,128)(2,1)S(1)} %collective-permute-done.15.refs_17_) | copy-start | bytes 1572868
  41.1 0.8 copy-start.12
  57.0 17.9 %copy-start = (bf16[2048,256]{1,0:T(8,128)(2,1)S(1)}, bf16[2048,256]{1,0:T(8,128)(2,1)}, u32[]{:S(2)}) copy-start(bf16[2048,256]{1,0:T(8,128)(2,1)} %get-tuple-element.40) | copy-start | bytes 3145732
  57.0 13.9 %collective-permute-start.16 = (bf16[1024,256]{1,0:T(8,128)(2,1)}, bf16[1024,256]{1,0:T(8,128)(2,1)S(1)}, u32[]{:S(2)}, u32[]{:S(2)}) collective-permute-start(bf16[1024,256]{1,0:T(8,128)(2,1)} %get-tuple-element.41), channel_id=1, source_target_pairs={{0,8},{8,16},{16,24},{1,9},{9,17},{17,25},{2,10},{10,18},{18,26},{... | collective-permute-start | bytes 1572872 | tf_op jit(solution)/shard_map/ppermute | solution.py:308
  61.2 13.7 %collective-permute-start.17 = (bf16[1024,256]{1,0:T(8,128)(2,1)}, bf16[1024,256]{1,0:T(8,128)(2,1)S(1)}, u32[]{:S(2)}, u32[]{:S(2)}) collective-permute-start(bf16[1024,256]{1,0:T(8,128)(2,1)} %get-tuple-element.42), channel_id=1, source_target_pairs={{8,0},{16,8},{24,16},{9,1},{17,9},{25,17},{10,2},{18,10},{26,18},{... | collective-permute-start | bytes 1572872 | tf_op jit(solution)/shard_map/ppermute | solution.py:307
  62.5 13.7 %all-to-all-start = ((bf16[8,256,128]{2,1,0:T(8,128)(2,1)}), bf16[8,256,128]{2,1,0:T(8,128)(2,1)S(1)}, u32[]{:S(2)}, u32[]{:S(2)}) async-start(bf16[8,256,128]{2,1,0:T(8,128)(2,1)} %get-tuple-element.39), calls=%async_computation | async-start | bytes 1048576 | tf_op jit(solution)/shard_map/all_to_all | solution.py:271
  76.1 18.4 %all-to-all-start.1 = ((bf16[8,256,256]{2,1,0:T(8,128)(2,1)}), bf16[8,256,256]{2,1,0:T(8,128)(2,1)S(1)}, u32[]{:S(2)}, u32[]{:S(2)}) async-start(bf16[8,256,256]{2,1,0:T(8,128)(2,1)} %bitcast.11), calls=%async_computation.1 | async-start | bytes 2097152 | tf_op jit(solution)/shard_map/all_to_all | solution.py:271

commit v2 on v1

--- a/solution.py
+++ b/solution.py
@@ -12,7 +12,7 @@
 PERSONS_GROUP = 4
 CHUNK = 4
 STEP = 4
-SENDS = (4, 1, 5, 6, 3, 7, 2)
+SENDS = (2, 5, 4, 1, 7, 6, 3)
 VMEM_BYTES = 63 * 1024 * 1024
 LANES = 2 * HEAD_DIM
 masked_value = -1e30

time: 96.6 us -> 99.4 us (1.029)
  waiting for transfers between devices: 36.1 us -> 39.6 us
    ppermute x14, waiting for transfers between devices: 10.6 us -> 12.3 us  [send(): return lax.ppermute(slab, group, [(i, i ^ k) for i in range(peers)])]
    ppermute x1, waiting for transfers between devices: 4.04 us -> 5.34 us  [on_device(): from_above = lax.ppermute(grad_left, 'outer', down)]
    ppermute x1, waiting for transfers between devices: 4.87 us -> 5.92 us  [on_device(): from_below = lax.ppermute(grad_right, 'outer', up)]
    unnamed x46 -> x44, local copies, waits for them, and re-layouts: 2.14 us -> 2.13 us
  transfers between devices with their start and end apart: 20 -> 20, of which waited for: 8 -> 10; matrix products, arithmetic and copies ran while one was open for 5% -> 5% of each run, Pallas kernels for 2% -> 2%
where the time goes in v2:
time: 99.4 us; the launch traced here: 99.5 us
  waiting for transfers between devices  39.6 us (40%)
  starting transfers between devices  32.3 us (32%)
  Pallas kernels  19.8 us (20%)
  local copies, waits for them, and re-layouts  4.22 us (4%)
  other arithmetic  2.54 us (3%)
  between operations  1.01 us (1%)
    pallas_call x1, Pallas kernels, attend(): pl.pallas_call(attend_kernel, out_shape=(shaped((peers, rows // peers, LA...  15.5 us
    ppermute x14, starting transfers between devices, send(): return lax.ppermute(slab, group, [(i, i ^ k) for i in range(peers)])  15.3 us
    all_to_all x2, waiting for transfers between devices, exchange(): return lax.all_to_all(parts, group, split_axis=0, concat_axis=0, tiled=True)  13.6 us
    ppermute x14, waiting for transfers between devices, send(): return lax.ppermute(slab, group, [(i, i ^ k) for i in range(peers)])  12.3 us
    all_to_all x2, starting transfers between devices, exchange(): return lax.all_to_all(parts, group, split_axis=0, concat_axis=0, tiled=True)  7.06 us
    ppermute x1, waiting for transfers between devices, on_device(): from_below = lax.ppermute(grad_right, 'outer', up)  5.92 us
    ppermute x1, waiting for transfers between devices, on_device(): from_above = lax.ppermute(grad_left, 'outer', down)  5.34 us
    ppermute x2, starting transfers between devices, beside(): return lax.ppermute(slabs, ('outer',) + group, pairs)  5 us
  transfers between devices with their start and end apart: 20, of which 10 were waited for; matrix products, arithmetic and copies ran while one was open for 5% of the time, Pallas kernels for 2%

profile of v2, /device:TPU:0, one launch (start us, length us, event | category | flops | bytes accessed | tf_op | source)
XLA Modules:
  0.0 99.5 jit_solution(9566572328399918798)
XLA Ops:
  0.7 2.1 %pack.3 = (bf16[256,256]{1,0:T(8,128)(2,1)}, bf16[256,256]{1,0:T(8,128)(2,1)}, bf16[256,256]{1,0:T(8,128)(2,1)}, bf16[256,256]{1,0:T(8,128)(2,1)}, bf16[256,256]...) custom-call(s32[1]{0:T(128)} %bitcast.me_ref, ...), custom_call_target="tpu_custom_call" | custom-call | bytes 2000000 | tf_op jit(solution)/shard_map/pack/pallas_call | solution.py:225
  2.8 0.5 collective-permute-start.7
  3.3 3.5 %collective-permute-start.8 = (bf16[256,256]{1,0:T(8,128)(2,1)}, bf16[256,256]{1,0:T(8,128)(2,1)S(1)}, u32[]{:S(2)}, u32[]{:S(2)}) collective-permute-start(bf16[256,256]{1,0:T(8,128)(2,1)} %get-tuple-element.33), channel_id=1, source_target_pairs={{0,5},{1,4},{2,7},{3,6},{4,1},{5,0},{6,3},{7,2},{8,13},{9,12},{10,... | collective-permute-start | bytes 393224 | tf_op jit(solution)/shard_map/ppermute | solution.py:278
  6.8 0.5 collective-permute-start.9
  7.3 1.0 collective-permute-start.11
  8.3 0.3 collective-permute-start.12
  8.7 0.1 subtract_clamp_fusion
  8.8 2.5 %collective-permute-done.8.refs_10_ = bf16[256,256]{1,0:T(8,128)(2,1)S(1)} collective-permute-done((bf16[256,256]{1,0:T(8,128)(2,1)}, bf16[256,256]{1,0:T(8,128)(2,1)S(1)}, u32[]{:S(2)}, u32[]{:S(2)}) %collective-permute-start.8) | collective-permute-done | bytes 131104 | tf_op jit(solution)/shard_map/ppermute | solution.py:278
  11.2 2.1 %collective-permute-start.10 = (bf16[256,256]{1,0:T(8,128)(2,1)}, bf16[256,256]{1,0:T(8,128)(2,1)S(1)}, u32[]{:S(2)}, u32[]{:S(2)}) collective-permute-start(bf16[256,256]{1,0:T(8,128)(2,1)} %get-tuple-element.35), channel_id=1, source_target_pairs={{0,1},{1,0},{2,3},{3,2},{4,5},{5,4},{6,7},{7,6},{8,9},{9,8},{10,11... | collective-permute-start | bytes 393224 | tf_op jit(solution)/shard_map/ppermute | solution.py:278
  13.4 3.4 %collective-permute-done.9.refs_11_ = bf16[256,256]{1,0:T(8,128)(2,1)S(1)} collective-permute-done((bf16[256,256]{1,0:T(8,128)(2,1)}, bf16[256,256]{1,0:T(8,128)(2,1)S(1)}, u32[]{:S(2)}, u32[]{:S(2)}) %collective-permute-start.9) | collective-permute-done | bytes 131104 | tf_op jit(solution)/shard_map/ppermute | solution.py:278
  16.8 1.3 %collective-permute-start.13 = (bf16[256,256]{1,0:T(8,128)(2,1)}, bf16[256,256]{1,0:T(8,128)(2,1)S(1)}, u32[]{:S(2)}, u32[]{:S(2)}) collective-permute-start(bf16[256,256]{1,0:T(8,128)(2,1)} %get-tuple-element.38), channel_id=1, source_target_pairs={{0,3},{1,2},{2,1},{3,0},{4,7},{5,6},{6,5},{7,4},{8,11},{9,10},{10,... | collective-permute-start | bytes 393224 | tf_op jit(solution)/shard_map/ppermute | solution.py:278
  18.1 0.1 and_reduce_fusion
  18.2 0.1 dynamic_slice.6
  18.3 2.1 %pack.2 = (bf16[256,256]{1,0:T(8,128)(2,1)}, bf16[256,256]{1,0:T(8,128)(2,1)}, bf16[256,256]{1,0:T(8,128)(2,1)}, bf16[256,256]{1,0:T(8,128)(2,1)}, bf16[256,256]...) custom-call(s32[1]{0:T(128)} %bitcast.me_ref, ...), custom_call_target="tpu_custom_call" | custom-call | bytes 2000000 | tf_op jit(solution)/shard_map/pack/pallas_call | solution.py:225
  20.5 0.6 collective-permute-start
  21.1 1.5 %collective-permute-start.1 = (bf16[256,256]{1,0:T(8,128)(2,1)}, bf16[256,256]{1,0:T(8,128)(2,1)S(1)}, u32[]{:S(2)}, u32[]{:S(2)}) collective-permute-start(bf16[256,256]{1,0:T(8,128)(2,1)} %get-tuple-element.25), channel_id=1, source_target_pairs={{0,5},{1,4},{2,7},{3,6},{4,1},{5,0},{6,3},{7,2},{8,13},{9,12},{10,... | collective-permute-start | bytes 393224 | tf_op jit(solution)/shard_map/ppermute | solution.py:278
  22.6 0.1 pad_maximum_fusion.1
  22.7 0.4 collective-permute-start.2
  23.1 3.7 %collective-permute-start.15 = (bf16[4,256,256]{2,1,0:T(8,128)(2,1)S(1)}, bf16[4,256,256]{2,1,0:T(8,128)(2,1)S(1)}, u32[]{:S(2)}, u32[]{:S(2)}) collective-permute-start(bf16[4,256,256]{2,1,0:T(8,128)(2,1)S(1)} %pad_maximum_fusion.1), channel_id=1, source_target_pairs={{0,8},{1,9},{2,10},{3,11},{8,16},{9,17},{10,18},{11,19},{12,4},{13... | collective-permute-start | bytes 1572872 | tf_op jit(solution)/shard_map/ppermute | solution.py:291
  26.8 0.1 pad_maximum_fusion
  26.9 1.3 %collective-permute-start.14 = (bf16[4,256,256]{2,1,0:T(8,128)(2,1)S(1)}, bf16[4,256,256]{2,1,0:T(8,128)(2,1)S(1)}, u32[]{:S(2)}, u32[]{:S(2)}) collective-permute-start(bf16[4,256,256]{2,1,0:T(8,128)(2,1)S(1)} %pad_maximum_fusion), channel_id=1, source_target_pairs={{4,12},{5,13},{6,14},{7,15},{8,0},{9,1},{10,2},{11,3},{12,20},{13,... | collective-permute-start | bytes 1572872 | tf_op jit(solution)/shard_map/ppermute | solution.py:291
  28.3 1.6 %collective-permute-start.3 = (bf16[256,256]{1,0:T(8,128)(2,1)S(1)}, bf16[256,256]{1,0:T(8,128)(2,1)S(1)}, u32[]{:S(2)}, u32[]{:S(2)}) collective-permute-start(bf16[256,256]{1,0:T(8,128)(2,1)S(1)} %copy-done.16), channel_id=1, source_target_pairs={{0,1},{1,0},{2,3},{3,2},{4,5},{5,4},{6,7},{7,6},{8,9},{9,8},{10,11... | collective-permute-start | bytes 393224 | tf_op jit(solution)/shard_map/ppermute | solution.py:278
  29.9 0.1 select_reduce_fusion.1
  30.1 0.9 collective-permute-start.4
  31.0 0.9 collective-permute-start.5
  31.8 1.5 %collective-permute-done.3.refs_4_ = bf16[256,256]{1,0:T(8,128)(2,1)S(1)} collective-permute-done((bf16[256,256]{1,0:T(8,128)(2,1)S(1)}, bf16[256,256]{1,0:T(8,128)(2,1)S(1)}, u32[]{:S(2)}, u32[]{:S(2)}) %collective-permute-start.3) | collective-permute-done | bytes 131104 | tf_op jit(solution)/shard_map/ppermute | solution.py:278
  33.4 0.2 collective-permute-start.6
  33.6 0.2 convert_reduce_fusion
  33.8 0.7 copy.19.lists_ref
  34.4 0.6 select_reduce_fusion.2.order_ref
  35.0 2.1 %collective-permute-done.4.refs_5_ = bf16[256,256]{1,0:T(8,128)(2,1)S(1)} collective-permute-done((bf16[256,256]{1,0:T(8,128)(2,1)}, bf16[256,256]{1,0:T(8,128)(2,1)S(1)}, u32[]{:S(2)}, u32[]{:S(2)}) %collective-permute-start.4) | collective-permute-done | bytes 131104 | tf_op jit(solution)/shard_map/ppermute | solution.py:278
  37.1 1.7 %collective-permute-done.5.refs_6_ = bf16[256,256]{1,0:T(8,128)(2,1)} collective-permute-done((bf16[256,256]{1,0:T(8,128)(2,1)}, bf16[256,256]{1,0:T(8,128)(2,1)}, u32[]{:S(2)}, u32[]{:S(2)}) %collective-permute-start.5) | collective-permute-done | bytes 131104 | tf_op jit(solution)/shard_map/ppermute | solution.py:278
  38.8 1.0 %collective-permute-done.6.refs_7_ = bf16[256,256]{1,0:T(8,128)(2,1)} collective-permute-done((bf16[256,256]{1,0:T(8,128)(2,1)}, bf16[256,256]{1,0:T(8,128)(2,1)}, u32[]{:S(2)}, u32[]{:S(2)}) %collective-permute-start.6) | collective-permute-done | bytes 131104 | tf_op jit(solution)/shard_map/ppermute | solution.py:278
  39.8 2.5 %collective-permute-done.14.refs_16_ = bf16[4,256,256]{2,1,0:T(8,128)(2,1)S(1)} collective-permute-done((bf16[4,256,256]{2,1,0:T(8,128)(2,1)S(1)}, bf16[4,256,256]{2,1,0:T(8,128)(2,1)S(1)}, u32[]{:S(2)}, u32[]{:S(2)}) %collective-permute-start.14) | collective-permute-done | bytes 524320 | tf_op jit(solution)/shard_map/ppermute | solution.py:291
  42.3 0.8 copy-done.12
  43.1 15.5 %attend.1 = (bf16[8,256,128]{2,1,0:T(8,128)(2,1)}, bf16[1024,256]{1,0:T(8,128)(2,1)}, bf16[2048,256]{1,0:T(8,128)(2,1)}, bf16[1024,256]{1,0:T(8,128)(2,1)}) custom-call(s32[1]{0:T(128)} %bitcast.me_ref, s32[32,16]{1,0:T(8,128)} %copy.19.lists_ref, s32[32]{0:T(128)} %copy-done.10, s32[32]{0:T(128)} %select_reduce_fusion.2.order_ref, ...), custom_call_target="tpu_custom_call" | custom-call | flops 4000000000 | bytes 6000000 | tf_op jit(solution)/shard_map/attend/pallas_call | solution.py:161
  58.6 3.7 %collective-permute-start.16 = (bf16[1024,256]{1,0:T(8,128)(2,1)}, bf16[1024,256]{1,0:T(8,128)(2,1)S(1)}, u32[]{:S(2)}, u32[]{:S(2)}) collective-permute-start(bf16[1024,256]{1,0:T(8,128)(2,1)} %get-tuple-element.41), channel_id=1, source_target_pairs={{0,8},{8,16},{16,24},{1,9},{9,17},{17,25},{2,10},{10,18},{18,26},{... | collective-permute-start | bytes 1572872 | tf_op jit(solution)/shard_map/ppermute | solution.py:308
  62.3 1.3 %collective-permute-start.17 = (bf16[1024,256]{1,0:T(8,128)(2,1)}, bf16[1024,256]{1,0:T(8,128)(2,1)S(1)}, u32[]{:S(2)}, u32[]{:S(2)}) collective-permute-start(bf16[1024,256]{1,0:T(8,128)(2,1)} %get-tuple-element.42), channel_id=1, source_target_pairs={{8,0},{16,8},{24,16},{9,1},{17,9},{25,17},{10,2},{18,10},{26,18},{... | collective-permute-start | bytes 1572872 | tf_op jit(solution)/shard_map/ppermute | solution.py:307
  63.6 3.5 %all-to-all-start = ((bf16[8,256,128]{2,1,0:T(8,128)(2,1)}), bf16[8,256,128]{2,1,0:T(8,128)(2,1)S(1)}, u32[]{:S(2)}, u32[]{:S(2)}) async-start(bf16[8,256,128]{2,1,0:T(8,128)(2,1)} %get-tuple-element.39), calls=%async_computation | async-start | bytes 1048576 | tf_op jit(solution)/shard_map/all_to_all | solution.py:271
  67.1 5.9 %collective-permute-done.16 = bf16[1024,256]{1,0:T(8,128)(2,1)S(1)} collective-permute-done((bf16[1024,256]{1,0:T(8,128)(2,1)}, bf16[1024,256]{1,0:T(8,128)(2,1)S(1)}, u32[]{:S(2)}, u32[]{:S(2)}) %collective-permute-start.16) | collective-permute-done | bytes 524320 | tf_op jit(solution)/shard_map/ppermute | solution.py:308
  73.1 5.3 %collective-permute-done.17 = bf16[1024,256]{1,0:T(8,128)(2,1)S(1)} collective-permute-done((bf16[1024,256]{1,0:T(8,128)(2,1)}, bf16[1024,256]{1,0:T(8,128)(2,1)S(1)}, u32[]{:S(2)}, u32[]{:S(2)}) %collective-permute-start.17) | collective-permute-done | bytes 524320 | tf_op jit(solution)/shard_map/ppermute | solution.py:307
  78.4 1.2 %add_convert_fusion = bf16[2048,256]{1,0:T(8,128)(2,1)} fusion(bf16[2048,256]{1,0:T(8,128)(2,1)S(1)} %copy-done, bf16[1024,256]{1,0:T(8,128)(2,1)S(1)} %collective-permute-done.17, bf16[1024,256]{1,0:T(8,128)(2,1)S(1)} %collective-permute-done.16), kind=kLoop, calls=%fused_computation | loop fusion | flops 3670016 | bytes 3145728 | tf_op jit(solution)/shard_map/convert_element_type | solution.py:311
  79.7 3.6 %all-to-all-start.1 = ((bf16[8,256,256]{2,1,0:T(8,128)(2,1)}), bf16[8,256,256]{2,1,0:T(8,128)(2,1)S(1)}, u32[]{:S(2)}, u32[]{:S(2)}) async-start(bf16[8,256,256]{2,1,0:T(8,128)(2,1)} %bitcast.11), calls=%async_computation.1 | async-start | bytes 2097152 | tf_op jit(solution)/shard_map/all_to_all | solution.py:271
  83.2 0.2 copy.20
  83.5 1.0 %copy.23 = bf16[256,1024]{1,0:T(8,128)(2,1)} copy(bf16[256,1024]{0,1:T(8,128)(2,1)S(1)} %bitcast.23) | data formatting | bytes 1048576
  84.5 13.6 %all-to-all-done.1 = bf16[8,256,256]{2,1,0:T(8,128)(2,1)S(1)} async-done(((bf16[8,256,256]{2,1,0:T(8,128)(2,1)}), bf16[8,256,256]{2,1,0:T(8,128)(2,1)S(1)}, u32[]{:S(2)}, u32[]{:S(2)}) %all-to-all-start.1) | async-done | bytes 1048608 | tf_op jit(solution)/shard_map/all_to_all | solution.py:271
  98.1 0.3 slice_bitcast_fusion
  98.4 1.1 %copy_bitcast_fusion = (bf16[256,1024]{1,0:T(8,128)(2,1)}, bf16[256,1024]{1,0:T(8,128)(2,1)}) fusion(bf16[8,32,8,128]{3,2,1,0:T(8,128)(2,1)S(1)} %get-tuple-element.51, bf16[8,32,8,128]{3,2,1,0:T(8,128)(2,1)S(1)} %get-tuple-element.52), kind=kLoop, calls=%fused_computation.1 | loop fusion | bytes 2097152 | tf_op jit(solution)/shard_map/reshape | solution.py:315
  (55 shorter events, 0.2 us)
Async XLA Ops:
  0.6 8.0 %copy-start.9 = (s32[128,16]{0,1:T(8,128)S(1)}, s32[128,16]{0,1:T(8,128)}, u32[]{:S(2)}) copy-start(s32[128,16]{0,1:T(8,128)} %param.10) | copy-start | bytes 24580
  0.6 17.6 %copy-start.20 = (s32[128]{0:T(128)S(1)}, s32[128]{0:T(128)}, u32[]{:S(2)}) copy-start(s32[128]{0:T(128)} %param.11) | copy-start | bytes 1540
  2.8 19.9 %collective-permute-start.7 = (bf16[256,256]{1,0:T(8,128)(2,1)}, bf16[256,256]{1,0:T(8,128)(2,1)S(1)}, u32[]{:S(2)}, u32[]{:S(2)}) collective-permute-start(bf16[256,256]{1,0:T(8,128)(2,1)} %get-tuple-element.32), channel_id=1, source_target_pairs={{0,2},{1,3},{2,0},{3,1},{4,6},{5,7},{6,4},{7,5},{8,10},{9,11},{10,... | collective-permute-start | bytes 393224 | tf_op jit(solution)/shard_map/ppermute | solution.py:278
  3.3 7.9 %collective-permute-start.8 = (bf16[256,256]{1,0:T(8,128)(2,1)}, bf16[256,256]{1,0:T(8,128)(2,1)S(1)}, u32[]{:S(2)}, u32[]{:S(2)}) collective-permute-start(bf16[256,256]{1,0:T(8,128)(2,1)} %get-tuple-element.33), channel_id=1, source_target_pairs={{0,5},{1,4},{2,7},{3,6},{4,1},{5,0},{6,3},{7,2},{8,13},{9,12},{10,... | collective-permute-start | bytes 393224 | tf_op jit(solution)/shard_map/ppermute | solution.py:278
  6.8 10.0 %collective-permute-start.9 = (bf16[256,256]{1,0:T(8,128)(2,1)}, bf16[256,256]{1,0:T(8,128)(2,1)S(1)}, u32[]{:S(2)}, u32[]{:S(2)}) collective-permute-start(bf16[256,256]{1,0:T(8,128)(2,1)} %get-tuple-element.34), channel_id=1, source_target_pairs={{0,4},{1,5},{2,6},{3,7},{4,0},{5,1},{6,2},{7,3},{8,12},{9,13},{10,... | collective-permute-start | bytes 393224 | tf_op jit(solution)/shard_map/ppermute | solution.py:278
  7.3 13.1 %collective-permute-start.11 = (bf16[256,256]{1,0:T(8,128)(2,1)}, bf16[256,256]{1,0:T(8,128)(2,1)S(1)}, u32[]{:S(2)}, u32[]{:S(2)}) collective-permute-start(bf16[256,256]{1,0:T(8,128)(2,1)} %get-tuple-element.36), channel_id=1, source_target_pairs={{0,7},{1,6},{2,5},{3,4},{4,3},{5,2},{6,1},{7,0},{8,15},{9,14},{10,... | collective-permute-start | bytes 393224 | tf_op jit(solution)/shard_map/ppermute | solution.py:278
  8.3 12.8 %collective-permute-start.12 = (bf16[256,256]{1,0:T(8,128)(2,1)}, bf16[256,256]{1,0:T(8,128)(2,1)S(1)}, u32[]{:S(2)}, u32[]{:S(2)}) collective-permute-start(bf16[256,256]{1,0:T(8,128)(2,1)} %get-tuple-element.37), channel_id=1, source_target_pairs={{0,6},{1,7},{2,4},{3,5},{4,2},{5,3},{6,0},{7,1},{8,14},{9,15},{10,... | collective-permute-start | bytes 393224 | tf_op jit(solution)/shard_map/ppermute | solution.py:278
  11.2 11.4 %copy-start.3 = (bf16[256,256]{1,0:T(8,128)(2,1)}, bf16[256,256]{1,0:T(8,128)(2,1)S(1)}, u32[]{:S(2)}) copy-start(bf16[256,256]{1,0:T(8,128)(2,1)S(1)} %collective-permute-done.8.refs_10_) | copy-start | bytes 393220
  11.2 11.8 %collective-permute-start.10 = (bf16[256,256]{1,0:T(8,128)(2,1)}, bf16[256,256]{1,0:T(8,128)(2,1)S(1)}, u32[]{:S(2)}, u32[]{:S(2)}) collective-permute-start(bf16[256,256]{1,0:T(8,128)(2,1)} %get-tuple-element.35), channel_id=1, source_target_pairs={{0,1},{1,0},{2,3},{3,2},{4,5},{5,4},{6,7},{7,6},{8,9},{9,8},{10,11... | collective-permute-start | bytes 393224 | tf_op jit(solution)/shard_map/ppermute | solution.py:278
  16.8 5.9 %copy-start.4 = (bf16[256,256]{1,0:T(8,128)(2,1)}, bf16[256,256]{1,0:T(8,128)(2,1)S(1)}, u32[]{:S(2)}) copy-start(bf16[256,256]{1,0:T(8,128)(2,1)S(1)} %collective-permute-done.9.refs_11_) | copy-start | bytes 393220
  16.8 10.0 %collective-permute-start.13 = (bf16[256,256]{1,0:T(8,128)(2,1)}, bf16[256,256]{1,0:T(8,128)(2,1)S(1)}, u32[]{:S(2)}, u32[]{:S(2)}) collective-permute-start(bf16[256,256]{1,0:T(8,128)(2,1)} %get-tuple-element.38), channel_id=1, source_target_pairs={{0,3},{1,2},{2,1},{3,0},{4,7},{5,6},{6,5},{7,4},{8,11},{9,10},{10,... | collective-permute-start | bytes 393224 | tf_op jit(solution)/shard_map/ppermute | solution.py:278
  18.3 8.5 %copy-start.1 = (bf16[256,256]{1,0:T(8,128)(2,1)S(1)}, bf16[256,256]{1,0:T(8,128)(2,1)}, u32[]{:S(2)}) copy-start(bf16[256,256]{1,0:T(8,128)(2,1)} %get-tuple-element.31.refs_8_) | copy-start | bytes 393220
  20.5 2.3 %copy-start.18 = (bf16[256,256]{1,0:T(8,128)(2,1)S(1)}, bf16[256,256]{1,0:T(8,128)(2,1)}, u32[]{:S(2)}) copy-start(bf16[256,256]{1,0:T(8,128)(2,1)} %get-tuple-element.26) | copy-start | bytes 393220
  20.5 6.4 %copy-start.5 = (bf16[256,256]{1,0:T(8,128)(2,1)}, bf16[256,256]{1,0:T(8,128)(2,1)S(1)}, u32[]{:S(2)}) copy-start(bf16[256,256]{1,0:T(8,128)(2,1)S(1)} %collective-permute-done.11.refs_13_) | copy-start | bytes 393220
  20.5 7.8 %collective-permute-start = (bf16[256,256]{1,0:T(8,128)(2,1)}, bf16[256,256]{1,0:T(8,128)(2,1)S(1)}, u32[]{:S(2)}, u32[]{:S(2)}) collective-permute-start(bf16[256,256]{1,0:T(8,128)(2,1)} %get-tuple-element.24), channel_id=1, source_target_pairs={{0,2},{1,3},{2,0},{3,1},{4,6},{5,7},{6,4},{7,5},{8,10},{9,11},{10,... | collective-permute-start | bytes 393224 | tf_op jit(solution)/shard_map/ppermute | solution.py:278
  21.1 5.8 %copy-start.6 = (bf16[256,256]{1,0:T(8,128)(2,1)}, bf16[256,256]{1,0:T(8,128)(2,1)S(1)}, u32[]{:S(2)}) copy-start(bf16[256,256]{1,0:T(8,128)(2,1)S(1)} %collective-permute-done.12.refs_14_) | copy-start | bytes 393220
  21.1 8.9 %collective-permute-start.1 = (bf16[256,256]{1,0:T(8,128)(2,1)}, bf16[256,256]{1,0:T(8,128)(2,1)S(1)}, u32[]{:S(2)}, u32[]{:S(2)}) collective-permute-start(bf16[256,256]{1,0:T(8,128)(2,1)} %get-tuple-element.25), channel_id=1, source_target_pairs={{0,5},{1,4},{2,7},{3,6},{4,1},{5,0},{6,3},{7,2},{8,13},{9,12},{10,... | collective-permute-start | bytes 393224 | tf_op jit(solution)/shard_map/ppermute | solution.py:278
  22.6 5.7 %copy-start.16 = (bf16[256,256]{1,0:T(8,128)(2,1)S(1)}, bf16[256,256]{1,0:T(8,128)(2,1)}, u32[]{:S(2)}) copy-start(bf16[256,256]{1,0:T(8,128)(2,1)} %get-tuple-element.27) | copy-start | bytes 393220
  22.7 20.4 %copy-start.2 = (bf16[256,256]{1,0:T(8,128)(2,1)}, bf16[256,256]{1,0:T(8,128)(2,1)S(1)}, u32[]{:S(2)}) copy-start(bf16[256,256]{1,0:T(8,128)(2,1)S(1)} %collective-permute-done.7.refs_9_) | copy-start | bytes 393220
  22.7 8.3 %collective-permute-start.2 = (bf16[256,256]{1,0:T(8,128)(2,1)S(1)}, bf16[256,256]{1,0:T(8,128)(2,1)S(1)}, u32[]{:S(2)}, u32[]{:S(2)}) collective-permute-start(bf16[256,256]{1,0:T(8,128)(2,1)S(1)} %copy-done.18), channel_id=1, source_target_pairs={{0,4},{1,5},{2,6},{3,7},{4,0},{5,1},{6,2},{7,3},{8,12},{9,13},{10,... | collective-permute-start | bytes 393224 | tf_op jit(solution)/shard_map/ppermute | solution.py:278
  23.1 20.0 %copy-start.7 = (bf16[256,256]{1,0:T(8,128)(2,1)}, bf16[256,256]{1,0:T(8,128)(2,1)S(1)}, u32[]{:S(2)}) copy-start(bf16[256,256]{1,0:T(8,128)(2,1)S(1)} %collective-permute-done.10.refs_12_) | copy-start | bytes 393220
  23.1 16.7 %collective-permute-start.15 = (bf16[4,256,256]{2,1,0:T(8,128)(2,1)S(1)}, bf16[4,256,256]{2,1,0:T(8,128)(2,1)S(1)}, u32[]{:S(2)}, u32[]{:S(2)}) collective-permute-start(bf16[4,256,256]{2,1,0:T(8,128)(2,1)S(1)} %pad_maximum_fusion.1), channel_id=1, source_target_pairs={{0,8},{1,9},{2,10},{3,11},{8,16},{9,17},{10,18},{11,19},{12,4},{13... | collective-permute-start | bytes 1572872 | tf_op jit(solution)/shard_map/ppermute | solution.py:291
  26.8 15.5 %copy-start.8 = (bf16[256,256]{1,0:T(8,128)(2,1)}, bf16[256,256]{1,0:T(8,128)(2,1)S(1)}, u32[]{:S(2)}) copy-start(bf16[256,256]{1,0:T(8,128)(2,1)S(1)} %collective-permute-done.13.refs_15_) | copy-start | bytes 393220
  26.9 15.3 %collective-permute-start.14 = (bf16[4,256,256]{2,1,0:T(8,128)(2,1)S(1)}, bf16[4,256,256]{2,1,0:T(8,128)(2,1)S(1)}, u32[]{:S(2)}, u32[]{:S(2)}) collective-permute-start(bf16[4,256,256]{2,1,0:T(8,128)(2,1)S(1)} %pad_maximum_fusion), channel_id=1, source_target_pairs={{4,12},{5,13},{6,14},{7,15},{8,0},{9,1},{10,2},{11,3},{12,20},{13,... | collective-permute-start | bytes 1572872 | tf_op jit(solution)/shard_map/ppermute | solution.py:291
  28.3 14.8 %copy-start.10 = (s32[32]{0:T(128)}, s32[32]{0:T(128)S(1)}, u32[]{:S(2)}) copy-start(s32[32]{0:T(128)S(1)} %get-tuple-element.49.counts_ref) | copy-start | bytes 388
  28.3 14.0 %copy-start.13 = (bf16[256,256]{1,0:T(8,128)(2,1)}, bf16[256,256]{1,0:T(8,128)(2,1)S(1)}, u32[]{:S(2)}) copy-start(bf16[256,256]{1,0:T(8,128)(2,1)S(1)} %collective-permute-done.refs_1_) | copy-start | bytes 393220
  28.3 5.1 %collective-permute-start.3 = (bf16[256,256]{1,0:T(8,128)(2,1)S(1)}, bf16[256,256]{1,0:T(8,128)(2,1)S(1)}, u32[]{:S(2)}, u32[]{:S(2)}) collective-permute-start(bf16[256,256]{1,0:T(8,128)(2,1)S(1)} %copy-done.16), channel_id=1, source_target_pairs={{0,1},{1,0},{2,3},{3,2},{4,5},{5,4},{6,7},{7,6},{8,9},{9,8},{10,11... | collective-permute-start | bytes 393224 | tf_op jit(solution)/shard_map/ppermute | solution.py:278
  30.0 12.2 %copy-start.14 = (bf16[256,256]{1,0:T(8,128)(2,1)}, bf16[256,256]{1,0:T(8,128)(2,1)S(1)}, u32[]{:S(2)}) copy-start(bf16[256,256]{1,0:T(8,128)(2,1)S(1)} %collective-permute-done.1.refs_2_) | copy-start | bytes 393220
  30.1 7.1 %collective-permute-start.4 = (bf16[256,256]{1,0:T(8,128)(2,1)}, bf16[256,256]{1,0:T(8,128)(2,1)S(1)}, u32[]{:S(2)}, u32[]{:S(2)}) collective-permute-start(bf16[256,256]{1,0:T(8,128)(2,1)} %get-tuple-element.28), channel_id=1, source_target_pairs={{0,7},{1,6},{2,5},{3,4},{4,3},{5,2},{6,1},{7,0},{8,15},{9,14},{10,... | collective-permute-start | bytes 393224 | tf_op jit(solution)/shard_map/ppermute | solution.py:278
  31.0 12.1 %copy-start.15 = (bf16[256,256]{1,0:T(8,128)(2,1)}, bf16[256,256]{1,0:T(8,128)(2,1)S(1)}, u32[]{:S(2)}) copy-start(bf16[256,256]{1,0:T(8,128)(2,1)S(1)} %collective-permute-done.2.refs_3_) | copy-start | bytes 393220
  31.0 7.8 %collective-permute-start.5 = (bf16[256,256]{1,0:T(8,128)(2,1)}, bf16[256,256]{1,0:T(8,128)(2,1)}, u32[]{:S(2)}, u32[]{:S(2)}) collective-permute-start(bf16[256,256]{1,0:T(8,128)(2,1)} %get-tuple-element.29), channel_id=1, source_target_pairs={{0,6},{1,7},{2,4},{3,5},{4,2},{5,3},{6,0},{7,1},{8,14},{9,15},{10,... | collective-permute-start | bytes 393224 | tf_op jit(solution)/shard_map/ppermute | solution.py:278
  33.4 9.7 %copy-start.17 = (bf16[256,256]{1,0:T(8,128)(2,1)}, bf16[256,256]{1,0:T(8,128)(2,1)S(1)}, u32[]{:S(2)}) copy-start(bf16[256,256]{1,0:T(8,128)(2,1)S(1)} %collective-permute-done.3.refs_4_) | copy-start | bytes 393220
  33.4 6.4 %collective-permute-start.6 = (bf16[256,256]{1,0:T(8,128)(2,1)}, bf16[256,256]{1,0:T(8,128)(2,1)}, u32[]{:S(2)}, u32[]{:S(2)}) collective-permute-start(bf16[256,256]{1,0:T(8,128)(2,1)} %get-tuple-element.30), channel_id=1, source_target_pairs={{0,3},{1,2},{2,1},{3,0},{4,7},{5,6},{6,5},{7,4},{8,11},{9,10},{10,... | collective-permute-start | bytes 393224 | tf_op jit(solution)/shard_map/ppermute | solution.py:278
  37.1 6.0 %copy-start.19 = (bf16[256,256]{1,0:T(8,128)(2,1)}, bf16[256,256]{1,0:T(8,128)(2,1)S(1)}, u32[]{:S(2)}) copy-start(bf16[256,256]{1,0:T(8,128)(2,1)S(1)} %collective-permute-done.4.refs_5_) | copy-start | bytes 393220
  39.8 2.5 %copy-start.11 = (bf16[4,256,256]{2,1,0:T(8,128)(2,1)}, bf16[4,256,256]{2,1,0:T(8,128)(2,1)S(1)}, u32[]{:S(2)}) copy-start(bf16[4,256,256]{2,1,0:T(8,128)(2,1)S(1)} %collective-permute-done.15.refs_17_) | copy-start | bytes 1572868
  42.3 0.8 copy-start.12
  58.6 19.8 %copy-start = (bf16[2048,256]{1,0:T(8,128)(2,1)S(1)}, bf16[2048,256]{1,0:T(8,128)(2,1)}, u32[]{:S(2)}) copy-start(bf16[2048,256]{1,0:T(8,128)(2,1)} %get-tuple-element.40) | copy-start | bytes 3145732
  58.6 14.4 %collective-permute-start.16 = (bf16[1024,256]{1,0:T(8,128)(2,1)}, bf16[1024,256]{1,0:T(8,128)(2,1)S(1)}, u32[]{:S(2)}, u32[]{:S(2)}) collective-permute-start(bf16[1024,256]{1,0:T(8,128)(2,1)} %get-tuple-element.41), channel_id=1, source_target_pairs={{0,8},{8,16},{16,24},{1,9},{9,17},{17,25},{2,10},{10,18},{18,26},{... | collective-permute-start | bytes 1572872 | tf_op jit(solution)/shard_map/ppermute | solution.py:308
  62.3 16.1 %collective-permute-start.17 = (bf16[1024,256]{1,0:T(8,128)(2,1)}, bf16[1024,256]{1,0:T(8,128)(2,1)S(1)}, u32[]{:S(2)}, u32[]{:S(2)}) collective-permute-start(bf16[1024,256]{1,0:T(8,128)(2,1)} %get-tuple-element.42), channel_id=1, source_target_pairs={{8,0},{16,8},{24,16},{9,1},{17,9},{25,17},{10,2},{18,10},{26,18},{... | collective-permute-start | bytes 1572872 | tf_op jit(solution)/shard_map/ppermute | solution.py:307
  63.6 16.0 %all-to-all-start = ((bf16[8,256,128]{2,1,0:T(8,128)(2,1)}), bf16[8,256,128]{2,1,0:T(8,128)(2,1)S(1)}, u32[]{:S(2)}, u32[]{:S(2)}) async-start(bf16[8,256,128]{2,1,0:T(8,128)(2,1)} %get-tuple-element.39), calls=%async_computation | async-start | bytes 1048576 | tf_op jit(solution)/shard_map/all_to_all | solution.py:271
  79.7 18.4 %all-to-all-start.1 = ((bf16[8,256,256]{2,1,0:T(8,128)(2,1)}), bf16[8,256,256]{2,1,0:T(8,128)(2,1)S(1)}, u32[]{:S(2)}, u32[]{:S(2)}) async-start(bf16[8,256,256]{2,1,0:T(8,128)(2,1)} %bitcast.11), calls=%async_computation.1 | async-start | bytes 2097152 | tf_op jit(solution)/shard_map/all_to_all | solution.py:271

commit v3 on v2

--- a/solution.py
+++ b/solution.py
@@ -12,7 +12,7 @@
 PERSONS_GROUP = 4
 CHUNK = 4
 STEP = 4
-SENDS = (2, 5, 4, 1, 7, 6, 3)
+SENDS = (4, 1, 5, 7, 3, 6, 2)
 VMEM_BYTES = 63 * 1024 * 1024
 LANES = 2 * HEAD_DIM
 masked_value = -1e30

time: 99.4 us -> 96.2 us (0.968); the launches traced: 99.5 us -> 95.1 us
  waiting for transfers between devices: 39.6 us -> 35.3 us
  Pallas kernels: 19.8 us -> 15.8 us
  starting transfers between devices: 32.3 us -> 36.2 us
    ppermute x14, waiting for transfers between devices: 12.3 us -> 8.2 us  [send(): return lax.ppermute(slab, group, [(i, i ^ k) for i in range(peers)])]
    pallas_call x1, Pallas kernels: 15.5 us -> 11.5 us  [attend(): pl.pallas_call(attend_kernel, out_shape=(shaped((peers, rows // peers, LA...]
    ppermute x1, starting transfers between devices: 3.69 us -> 6.69 us  [on_device(): from_below = lax.ppermute(grad_right, 'outer', up)]
    ppermute x2, waiting for transfers between devices: 2.46 us -> 3.93 us  [beside(): return lax.ppermute(slabs, ('outer',) + group, pairs)]
    ppermute x14, starting transfers between devices: 15.3 us -> 16.4 us  [send(): return lax.ppermute(slab, group, [(i, i ^ k) for i in range(peers)])]
    unnamed x44 -> x46, local copies, waits for them, and re-layouts: 2.13 us -> 2.14 us
  transfers between devices with their start and end apart: 20 -> 20, of which waited for: 10 -> 8; matrix products, arithmetic and copies ran while one was open for 5% -> 5% of each run, Pallas kernels for 2% -> 2%
where the time goes in v3:
time: 96.2 us; the launch traced here: 95.1 us
  starting transfers between devices  36.2 us (38%)
  waiting for transfers between devices  35.3 us (37%)
  Pallas kernels  15.8 us (16%)
  local copies, waits for them, and re-layouts  4.23 us (4%)
  other arithmetic  2.6 us (3%)
  between operations  1.04 us (1%)
    ppermute x14, starting transfers between devices, send(): return lax.ppermute(slab, group, [(i, i ^ k) for i in range(peers)])  16.4 us
    all_to_all x2, waiting for transfers between devices, exchange(): return lax.all_to_all(parts, group, split_axis=0, concat_axis=0, tiled=True)  13.6 us
    pallas_call x1, Pallas kernels, attend(): pl.pallas_call(attend_kernel, out_shape=(shaped((peers, rows // peers, LA...  11.5 us
    ppermute x14, waiting for transfers between devices, send(): return lax.ppermute(slab, group, [(i, i ^ k) for i in range(peers)])  8.2 us
    all_to_all x2, starting transfers between devices, exchange(): return lax.all_to_all(parts, group, split_axis=0, concat_axis=0, tiled=True)  7.06 us
    ppermute x1, starting transfers between devices, on_device(): from_below = lax.ppermute(grad_right, 'outer', up)  6.69 us
    ppermute x1, waiting for transfers between devices, on_device(): from_below = lax.ppermute(grad_right, 'outer', up)  5.15 us
    ppermute x2, starting transfers between devices, beside(): return lax.ppermute(slabs, ('outer',) + group, pairs)  4.79 us
  transfers between devices with their start and end apart: 20, of which 8 were waited for; matrix products, arithmetic and copies ran while one was open for 5% of the time, Pallas kernels for 2%

profile of v3, /device:TPU:0, one launch (start us, length us, event | category | flops | bytes accessed | tf_op | source)
XLA Modules:
  0.0 95.1 jit_solution(2247931938283444589)
XLA Ops:
  0.7 2.1 %pack.3 = (bf16[256,256]{1,0:T(8,128)(2,1)}, bf16[256,256]{1,0:T(8,128)(2,1)}, bf16[256,256]{1,0:T(8,128)(2,1)}, bf16[256,256]{1,0:T(8,128)(2,1)}, bf16[256,256]...) custom-call(s32[1]{0:T(128)} %bitcast.me_ref, ...), custom_call_target="tpu_custom_call" | custom-call | bytes 2000000 | tf_op jit(solution)/shard_map/pack/pallas_call | solution.py:225
  2.8 3.0 %collective-permute-start.7 = (bf16[256,256]{1,0:T(8,128)(2,1)}, bf16[256,256]{1,0:T(8,128)(2,1)S(1)}, u32[]{:S(2)}, u32[]{:S(2)}) collective-permute-start(bf16[256,256]{1,0:T(8,128)(2,1)} %get-tuple-element.32), channel_id=1, source_target_pairs={{0,4},{1,5},{2,6},{3,7},{4,0},{5,1},{6,2},{7,3},{8,12},{9,13},{10,... | collective-permute-start | bytes 393224 | tf_op jit(solution)/shard_map/ppermute | solution.py:278
  5.8 1.5 %collective-permute-start.8 = (bf16[256,256]{1,0:T(8,128)(2,1)}, bf16[256,256]{1,0:T(8,128)(2,1)S(1)}, u32[]{:S(2)}, u32[]{:S(2)}) collective-permute-start(bf16[256,256]{1,0:T(8,128)(2,1)} %get-tuple-element.33), channel_id=1, source_target_pairs={{0,1},{1,0},{2,3},{3,2},{4,5},{5,4},{6,7},{7,6},{8,9},{9,8},{10,11... | collective-permute-start | bytes 393224 | tf_op jit(solution)/shard_map/ppermute | solution.py:278
  7.3 0.0 collective-permute-start.9
  7.4 1.5 %collective-permute-start.10 = (bf16[256,256]{1,0:T(8,128)(2,1)}, bf16[256,256]{1,0:T(8,128)(2,1)S(1)}, u32[]{:S(2)}, u32[]{:S(2)}) collective-permute-start(bf16[256,256]{1,0:T(8,128)(2,1)} %get-tuple-element.35), channel_id=1, source_target_pairs={{0,7},{1,6},{2,5},{3,4},{4,3},{5,2},{6,1},{7,0},{8,15},{9,14},{10,... | collective-permute-start | bytes 393224 | tf_op jit(solution)/shard_map/ppermute | solution.py:278
  8.9 1.6 %collective-permute-start.12 = (bf16[256,256]{1,0:T(8,128)(2,1)}, bf16[256,256]{1,0:T(8,128)(2,1)S(1)}, u32[]{:S(2)}, u32[]{:S(2)}) collective-permute-start(bf16[256,256]{1,0:T(8,128)(2,1)} %get-tuple-element.37), channel_id=1, source_target_pairs={{0,6},{1,7},{2,4},{3,5},{4,2},{5,3},{6,0},{7,1},{8,14},{9,15},{10,... | collective-permute-start | bytes 393224 | tf_op jit(solution)/shard_map/ppermute | solution.py:278
  10.5 0.1 subtract_clamp_fusion
  10.6 0.0 collective-permute-done.7.refs_9_
  10.6 0.1 collective-permute-start.11
  10.7 4.3 %collective-permute-done.9.refs_11_ = bf16[256,256]{1,0:T(8,128)(2,1)S(1)} collective-permute-done((bf16[256,256]{1,0:T(8,128)(2,1)}, bf16[256,256]{1,0:T(8,128)(2,1)S(1)}, u32[]{:S(2)}, u32[]{:S(2)}) %collective-permute-start.9) | collective-permute-done | bytes 131104 | tf_op jit(solution)/shard_map/ppermute | solution.py:278
  15.0 0.1 and_reduce_fusion
  15.1 0.1 dynamic_slice.6
  15.2 2.2 %pack.2 = (bf16[256,256]{1,0:T(8,128)(2,1)}, bf16[256,256]{1,0:T(8,128)(2,1)}, bf16[256,256]{1,0:T(8,128)(2,1)}, bf16[256,256]{1,0:T(8,128)(2,1)}, bf16[256,256]...) custom-call(s32[1]{0:T(128)} %bitcast.me_ref, ...), custom_call_target="tpu_custom_call" | custom-call | bytes 2000000 | tf_op jit(solution)/shard_map/pack/pallas_call | solution.py:225
  17.4 1.8 %collective-permute-start = (bf16[256,256]{1,0:T(8,128)(2,1)}, bf16[256,256]{1,0:T(8,128)(2,1)S(1)}, u32[]{:S(2)}, u32[]{:S(2)}) collective-permute-start(bf16[256,256]{1,0:T(8,128)(2,1)} %get-tuple-element.24), channel_id=1, source_target_pairs={{0,4},{1,5},{2,6},{3,7},{4,0},{5,1},{6,2},{7,3},{8,12},{9,13},{10,... | collective-permute-start | bytes 393224 | tf_op jit(solution)/shard_map/ppermute | solution.py:278
  19.2 1.5 %collective-permute-start.1 = (bf16[256,256]{1,0:T(8,128)(2,1)}, bf16[256,256]{1,0:T(8,128)(2,1)S(1)}, u32[]{:S(2)}, u32[]{:S(2)}) collective-permute-start(bf16[256,256]{1,0:T(8,128)(2,1)} %get-tuple-element.25), channel_id=1, source_target_pairs={{0,1},{1,0},{2,3},{3,2},{4,5},{5,4},{6,7},{7,6},{8,9},{9,8},{10,11... | collective-permute-start | bytes 393224 | tf_op jit(solution)/shard_map/ppermute | solution.py:278
  20.7 0.1 pad_maximum_fusion.1
  20.9 1.2 %collective-permute-start.2 = (bf16[256,256]{1,0:T(8,128)(2,1)S(1)}, bf16[256,256]{1,0:T(8,128)(2,1)S(1)}, u32[]{:S(2)}, u32[]{:S(2)}) collective-permute-start(bf16[256,256]{1,0:T(8,128)(2,1)S(1)} %copy-done.18), channel_id=1, source_target_pairs={{0,5},{1,4},{2,7},{3,6},{4,1},{5,0},{6,3},{7,2},{8,13},{9,12},{10,... | collective-permute-start | bytes 393224 | tf_op jit(solution)/shard_map/ppermute | solution.py:278
  22.1 3.5 %collective-permute-start.15 = (bf16[4,256,256]{2,1,0:T(8,128)(2,1)S(1)}, bf16[4,256,256]{2,1,0:T(8,128)(2,1)S(1)}, u32[]{:S(2)}, u32[]{:S(2)}) collective-permute-start(bf16[4,256,256]{2,1,0:T(8,128)(2,1)S(1)} %pad_maximum_fusion.1), channel_id=1, source_target_pairs={{0,8},{1,9},{2,10},{3,11},{8,16},{9,17},{10,18},{11,19},{12,4},{13... | collective-permute-start | bytes 1572872 | tf_op jit(solution)/shard_map/ppermute | solution.py:291
  25.6 0.1 pad_maximum_fusion
  25.7 1.3 %collective-permute-start.14 = (bf16[4,256,256]{2,1,0:T(8,128)(2,1)S(1)}, bf16[4,256,256]{2,1,0:T(8,128)(2,1)S(1)}, u32[]{:S(2)}, u32[]{:S(2)}) collective-permute-start(bf16[4,256,256]{2,1,0:T(8,128)(2,1)S(1)} %pad_maximum_fusion), channel_id=1, source_target_pairs={{4,12},{5,13},{6,14},{7,15},{8,0},{9,1},{10,2},{11,3},{12,20},{13,... | collective-permute-start | bytes 1572872 | tf_op jit(solution)/shard_map/ppermute | solution.py:291
  27.1 1.7 %collective-permute-start.3 = (bf16[256,256]{1,0:T(8,128)(2,1)S(1)}, bf16[256,256]{1,0:T(8,128)(2,1)S(1)}, u32[]{:S(2)}, u32[]{:S(2)}) collective-permute-start(bf16[256,256]{1,0:T(8,128)(2,1)S(1)} %copy-done.16), channel_id=1, source_target_pairs={{0,7},{1,6},{2,5},{3,4},{4,3},{5,2},{6,1},{7,0},{8,15},{9,14},{10,... | collective-permute-start | bytes 393224 | tf_op jit(solution)/shard_map/ppermute | solution.py:278
  28.7 0.1 select_reduce_fusion.1
  28.9 1.6 %collective-permute-start.4 = (bf16[256,256]{1,0:T(8,128)(2,1)}, bf16[256,256]{1,0:T(8,128)(2,1)S(1)}, u32[]{:S(2)}, u32[]{:S(2)}) collective-permute-start(bf16[256,256]{1,0:T(8,128)(2,1)} %get-tuple-element.28), channel_id=1, source_target_pairs={{0,3},{1,2},{2,1},{3,0},{4,7},{5,6},{6,5},{7,4},{8,11},{9,10},{10,... | collective-permute-start | bytes 393224 | tf_op jit(solution)/shard_map/ppermute | solution.py:278
  30.5 0.0 collective-permute-start.5
  30.6 2.8 %collective-permute-done.3.refs_4_ = bf16[256,256]{1,0:T(8,128)(2,1)S(1)} collective-permute-done((bf16[256,256]{1,0:T(8,128)(2,1)S(1)}, bf16[256,256]{1,0:T(8,128)(2,1)S(1)}, u32[]{:S(2)}, u32[]{:S(2)}) %collective-permute-start.3) | collective-permute-done | bytes 131104 | tf_op jit(solution)/shard_map/ppermute | solution.py:278
  33.4 0.7 collective-permute-start.6
  34.1 0.2 convert_reduce_fusion
  34.3 0.7 copy.19.lists_ref
  35.0 0.7 select_reduce_fusion.2.order_ref
  35.6 0.6 collective-permute-done.4.refs_5_
  36.2 0.6 collective-permute-done.5.refs_6_
  36.8 0.0 copy-start.11
  36.8 3.9 %collective-permute-done.14.refs_16_ = bf16[4,256,256]{2,1,0:T(8,128)(2,1)S(1)} collective-permute-done((bf16[4,256,256]{2,1,0:T(8,128)(2,1)S(1)}, bf16[4,256,256]{2,1,0:T(8,128)(2,1)S(1)}, u32[]{:S(2)}, u32[]{:S(2)}) %collective-permute-start.14) | collective-permute-done | bytes 524320 | tf_op jit(solution)/shard_map/ppermute | solution.py:291
  40.7 0.0 copy-start.12
  40.8 0.8 copy-done.12
  41.6 11.5 %attend.1 = (bf16[8,256,128]{2,1,0:T(8,128)(2,1)}, bf16[1024,256]{1,0:T(8,128)(2,1)}, bf16[2048,256]{1,0:T(8,128)(2,1)}, bf16[1024,256]{1,0:T(8,128)(2,1)}) custom-call(s32[1]{0:T(128)} %bitcast.me_ref, s32[32,16]{1,0:T(8,128)} %copy.19.lists_ref, s32[32]{0:T(128)} %copy-done.10, s32[32]{0:T(128)} %select_reduce_fusion.2.order_ref, ...), custom_call_target="tpu_custom_call" | custom-call | flops 4000000000 | bytes 6000000 | tf_op jit(solution)/shard_map/attend/pallas_call | solution.py:161
  53.0 6.7 %collective-permute-start.16 = (bf16[1024,256]{1,0:T(8,128)(2,1)}, bf16[1024,256]{1,0:T(8,128)(2,1)S(1)}, u32[]{:S(2)}, u32[]{:S(2)}) collective-permute-start(bf16[1024,256]{1,0:T(8,128)(2,1)} %get-tuple-element.41), channel_id=1, source_target_pairs={{0,8},{8,16},{16,24},{1,9},{9,17},{17,25},{2,10},{10,18},{18,26},{... | collective-permute-start | bytes 1572872 | tf_op jit(solution)/shard_map/ppermute | solution.py:308
  59.7 1.3 %collective-permute-start.17 = (bf16[1024,256]{1,0:T(8,128)(2,1)}, bf16[1024,256]{1,0:T(8,128)(2,1)S(1)}, u32[]{:S(2)}, u32[]{:S(2)}) collective-permute-start(bf16[1024,256]{1,0:T(8,128)(2,1)} %get-tuple-element.42), channel_id=1, source_target_pairs={{8,0},{16,8},{24,16},{9,1},{17,9},{25,17},{10,2},{18,10},{26,18},{... | collective-permute-start | bytes 1572872 | tf_op jit(solution)/shard_map/ppermute | solution.py:307
  61.0 3.5 %all-to-all-start = ((bf16[8,256,128]{2,1,0:T(8,128)(2,1)}), bf16[8,256,128]{2,1,0:T(8,128)(2,1)S(1)}, u32[]{:S(2)}, u32[]{:S(2)}) async-start(bf16[8,256,128]{2,1,0:T(8,128)(2,1)} %get-tuple-element.39), calls=%async_computation | async-start | bytes 1048576 | tf_op jit(solution)/shard_map/all_to_all | solution.py:271
  64.5 5.2 %collective-permute-done.16 = bf16[1024,256]{1,0:T(8,128)(2,1)S(1)} collective-permute-done((bf16[1024,256]{1,0:T(8,128)(2,1)}, bf16[1024,256]{1,0:T(8,128)(2,1)S(1)}, u32[]{:S(2)}, u32[]{:S(2)}) %collective-permute-start.16) | collective-permute-done | bytes 524320 | tf_op jit(solution)/shard_map/ppermute | solution.py:308
  69.7 4.4 %collective-permute-done.17 = bf16[1024,256]{1,0:T(8,128)(2,1)S(1)} collective-permute-done((bf16[1024,256]{1,0:T(8,128)(2,1)}, bf16[1024,256]{1,0:T(8,128)(2,1)S(1)}, u32[]{:S(2)}, u32[]{:S(2)}) %collective-permute-start.17) | collective-permute-done | bytes 524320 | tf_op jit(solution)/shard_map/ppermute | solution.py:307
  74.1 1.2 %add_convert_fusion = bf16[2048,256]{1,0:T(8,128)(2,1)} fusion(bf16[2048,256]{1,0:T(8,128)(2,1)S(1)} %copy-done, bf16[1024,256]{1,0:T(8,128)(2,1)S(1)} %collective-permute-done.17, bf16[1024,256]{1,0:T(8,128)(2,1)S(1)} %collective-permute-done.16), kind=kLoop, calls=%fused_computation | loop fusion | flops 3670016 | bytes 3145728 | tf_op jit(solution)/shard_map/convert_element_type | solution.py:311
  75.3 3.6 %all-to-all-start.1 = ((bf16[8,256,256]{2,1,0:T(8,128)(2,1)}), bf16[8,256,256]{2,1,0:T(8,128)(2,1)S(1)}, u32[]{:S(2)}, u32[]{:S(2)}) async-start(bf16[8,256,256]{2,1,0:T(8,128)(2,1)} %bitcast.11), calls=%async_computation.1 | async-start | bytes 2097152 | tf_op jit(solution)/shard_map/all_to_all | solution.py:271
  78.9 0.2 copy.20
  79.1 1.0 %copy.23 = bf16[256,1024]{1,0:T(8,128)(2,1)} copy(bf16[256,1024]{0,1:T(8,128)(2,1)S(1)} %bitcast.23) | data formatting | bytes 1048576
  80.1 13.6 %all-to-all-done.1 = bf16[8,256,256]{2,1,0:T(8,128)(2,1)S(1)} async-done(((bf16[8,256,256]{2,1,0:T(8,128)(2,1)}), bf16[8,256,256]{2,1,0:T(8,128)(2,1)S(1)}, u32[]{:S(2)}, u32[]{:S(2)}) %all-to-all-start.1) | async-done | bytes 1048608 | tf_op jit(solution)/shard_map/all_to_all | solution.py:271
  93.7 0.3 slice_bitcast_fusion
  94.0 1.1 %copy_bitcast_fusion = (bf16[256,1024]{1,0:T(8,128)(2,1)}, bf16[256,1024]{1,0:T(8,128)(2,1)}) fusion(bf16[8,32,8,128]{3,2,1,0:T(8,128)(2,1)S(1)} %get-tuple-element.51, bf16[8,32,8,128]{3,2,1,0:T(8,128)(2,1)S(1)} %get-tuple-element.52), kind=kLoop, calls=%fused_computation.1 | loop fusion | bytes 2097152 | tf_op jit(solution)/shard_map/reshape | solution.py:315
  (57 shorter events, 0.2 us)
Async XLA Ops:
  0.6 9.9 %copy-start.9 = (s32[128,16]{0,1:T(8,128)S(1)}, s32[128,16]{0,1:T(8,128)}, u32[]{:S(2)}) copy-start(s32[128,16]{0,1:T(8,128)} %param.10) | copy-start | bytes 24580
  0.6 14.5 %copy-start.21 = (s32[128]{0:T(128)S(1)}, s32[128]{0:T(128)}, u32[]{:S(2)}) copy-start(s32[128]{0:T(128)} %param.11) | copy-start | bytes 1540
  2.8 7.8 %collective-permute-start.7 = (bf16[256,256]{1,0:T(8,128)(2,1)}, bf16[256,256]{1,0:T(8,128)(2,1)S(1)}, u32[]{:S(2)}, u32[]{:S(2)}) collective-permute-start(bf16[256,256]{1,0:T(8,128)(2,1)} %get-tuple-element.32), channel_id=1, source_target_pairs={{0,4},{1,5},{2,6},{3,7},{4,0},{5,1},{6,2},{7,3},{8,12},{9,13},{10,... | collective-permute-start | bytes 393224 | tf_op jit(solution)/shard_map/ppermute | solution.py:278
  5.8 15.0 %collective-permute-start.8 = (bf16[256,256]{1,0:T(8,128)(2,1)}, bf16[256,256]{1,0:T(8,128)(2,1)S(1)}, u32[]{:S(2)}, u32[]{:S(2)}) collective-permute-start(bf16[256,256]{1,0:T(8,128)(2,1)} %get-tuple-element.33), channel_id=1, source_target_pairs={{0,1},{1,0},{2,3},{3,2},{4,5},{5,4},{6,7},{7,6},{8,9},{9,8},{10,11... | collective-permute-start | bytes 393224 | tf_op jit(solution)/shard_map/ppermute | solution.py:278
  7.3 7.6 %collective-permute-start.9 = (bf16[256,256]{1,0:T(8,128)(2,1)}, bf16[256,256]{1,0:T(8,128)(2,1)S(1)}, u32[]{:S(2)}, u32[]{:S(2)}) collective-permute-start(bf16[256,256]{1,0:T(8,128)(2,1)} %get-tuple-element.34), channel_id=1, source_target_pairs={{0,5},{1,4},{2,7},{3,6},{4,1},{5,0},{6,3},{7,2},{8,13},{9,12},{10,... | collective-permute-start | bytes 393224 | tf_op jit(solution)/shard_map/ppermute | solution.py:278
  7.4 10.0 %collective-permute-start.10 = (bf16[256,256]{1,0:T(8,128)(2,1)}, bf16[256,256]{1,0:T(8,128)(2,1)S(1)}, u32[]{:S(2)}, u32[]{:S(2)}) collective-permute-start(bf16[256,256]{1,0:T(8,128)(2,1)} %get-tuple-element.35), channel_id=1, source_target_pairs={{0,7},{1,6},{2,5},{3,4},{4,3},{5,2},{6,1},{7,0},{8,15},{9,14},{10,... | collective-permute-start | bytes 393224 | tf_op jit(solution)/shard_map/ppermute | solution.py:278
  8.9 10.4 %collective-permute-start.12 = (bf16[256,256]{1,0:T(8,128)(2,1)}, bf16[256,256]{1,0:T(8,128)(2,1)S(1)}, u32[]{:S(2)}, u32[]{:S(2)}) collective-permute-start(bf16[256,256]{1,0:T(8,128)(2,1)} %get-tuple-element.37), channel_id=1, source_target_pairs={{0,6},{1,7},{2,4},{3,5},{4,2},{5,3},{6,0},{7,1},{8,14},{9,15},{10,... | collective-permute-start | bytes 393224 | tf_op jit(solution)/shard_map/ppermute | solution.py:278
  10.6 10.2 %copy-start.2 = (bf16[256,256]{1,0:T(8,128)(2,1)}, bf16[256,256]{1,0:T(8,128)(2,1)S(1)}, u32[]{:S(2)}) copy-start(bf16[256,256]{1,0:T(8,128)(2,1)S(1)} %collective-permute-done.7.refs_9_) | copy-start | bytes 393220
  10.6 11.5 %collective-permute-start.11 = (bf16[256,256]{1,0:T(8,128)(2,1)}, bf16[256,256]{1,0:T(8,128)(2,1)S(1)}, u32[]{:S(2)}, u32[]{:S(2)}) collective-permute-start(bf16[256,256]{1,0:T(8,128)(2,1)} %get-tuple-element.36), channel_id=1, source_target_pairs={{0,3},{1,2},{2,1},{3,0},{4,7},{5,6},{6,5},{7,4},{8,11},{9,10},{10,... | collective-permute-start | bytes 393224 | tf_op jit(solution)/shard_map/ppermute | solution.py:278
  15.0 5.8 %copy-start.4 = (bf16[256,256]{1,0:T(8,128)(2,1)}, bf16[256,256]{1,0:T(8,128)(2,1)S(1)}, u32[]{:S(2)}) copy-start(bf16[256,256]{1,0:T(8,128)(2,1)S(1)} %collective-permute-done.9.refs_11_) | copy-start | bytes 393220
  15.0 10.6 %collective-permute-start.13 = (bf16[256,256]{1,0:T(8,128)(2,1)}, bf16[256,256]{1,0:T(8,128)(2,1)S(1)}, u32[]{:S(2)}, u32[]{:S(2)}) collective-permute-start(bf16[256,256]{1,0:T(8,128)(2,1)} %get-tuple-element.38), channel_id=1, source_target_pairs={{0,2},{1,3},{2,0},{3,1},{4,6},{5,7},{6,4},{7,5},{8,10},{9,11},{10,... | collective-permute-start | bytes 393224 | tf_op jit(solution)/shard_map/ppermute | solution.py:278
  15.2 10.4 %copy-start.1 = (bf16[256,256]{1,0:T(8,128)(2,1)S(1)}, bf16[256,256]{1,0:T(8,128)(2,1)}, u32[]{:S(2)}) copy-start(bf16[256,256]{1,0:T(8,128)(2,1)} %get-tuple-element.31.refs_8_) | copy-start | bytes 393220
  17.4 3.5 %copy-start.18 = (bf16[256,256]{1,0:T(8,128)(2,1)S(1)}, bf16[256,256]{1,0:T(8,128)(2,1)}, u32[]{:S(2)}) copy-start(bf16[256,256]{1,0:T(8,128)(2,1)} %get-tuple-element.26) | copy-start | bytes 393220
  17.4 8.3 %copy-start.5 = (bf16[256,256]{1,0:T(8,128)(2,1)}, bf16[256,256]{1,0:T(8,128)(2,1)S(1)}, u32[]{:S(2)}) copy-start(bf16[256,256]{1,0:T(8,128)(2,1)S(1)} %collective-permute-done.10.refs_12_) | copy-start | bytes 393220
  17.4 9.6 %collective-permute-start = (bf16[256,256]{1,0:T(8,128)(2,1)}, bf16[256,256]{1,0:T(8,128)(2,1)S(1)}, u32[]{:S(2)}, u32[]{:S(2)}) collective-permute-start(bf16[256,256]{1,0:T(8,128)(2,1)} %get-tuple-element.24), channel_id=1, source_target_pairs={{0,4},{1,5},{2,6},{3,7},{4,0},{5,1},{6,2},{7,3},{8,12},{9,13},{10,... | collective-permute-start | bytes 393224 | tf_op jit(solution)/shard_map/ppermute | solution.py:278
  19.2 6.4 %copy-start.6 = (bf16[256,256]{1,0:T(8,128)(2,1)}, bf16[256,256]{1,0:T(8,128)(2,1)S(1)}, u32[]{:S(2)}) copy-start(bf16[256,256]{1,0:T(8,128)(2,1)S(1)} %collective-permute-done.12.refs_14_) | copy-start | bytes 393220
  19.2 9.6 %collective-permute-start.1 = (bf16[256,256]{1,0:T(8,128)(2,1)}, bf16[256,256]{1,0:T(8,128)(2,1)S(1)}, u32[]{:S(2)}, u32[]{:S(2)}) collective-permute-start(bf16[256,256]{1,0:T(8,128)(2,1)} %get-tuple-element.25), channel_id=1, source_target_pairs={{0,1},{1,0},{2,3},{3,2},{4,5},{5,4},{6,7},{7,6},{8,9},{9,8},{10,11... | collective-permute-start | bytes 393224 | tf_op jit(solution)/shard_map/ppermute | solution.py:278
  20.7 6.3 %copy-start.16 = (bf16[256,256]{1,0:T(8,128)(2,1)S(1)}, bf16[256,256]{1,0:T(8,128)(2,1)}, u32[]{:S(2)}) copy-start(bf16[256,256]{1,0:T(8,128)(2,1)} %get-tuple-element.27) | copy-start | bytes 393220
  20.8 20.7 %copy-start.3 = (bf16[256,256]{1,0:T(8,128)(2,1)}, bf16[256,256]{1,0:T(8,128)(2,1)S(1)}, u32[]{:S(2)}) copy-start(bf16[256,256]{1,0:T(8,128)(2,1)S(1)} %collective-permute-done.8.refs_10_) | copy-start | bytes 393220
  20.9 9.6 %collective-permute-start.2 = (bf16[256,256]{1,0:T(8,128)(2,1)S(1)}, bf16[256,256]{1,0:T(8,128)(2,1)S(1)}, u32[]{:S(2)}, u32[]{:S(2)}) collective-permute-start(bf16[256,256]{1,0:T(8,128)(2,1)S(1)} %copy-done.18), channel_id=1, source_target_pairs={{0,5},{1,4},{2,7},{3,6},{4,1},{5,0},{6,3},{7,2},{8,13},{9,12},{10,... | collective-permute-start | bytes 393224 | tf_op jit(solution)/shard_map/ppermute | solution.py:278
  22.1 19.5 %copy-start.7 = (bf16[256,256]{1,0:T(8,128)(2,1)}, bf16[256,256]{1,0:T(8,128)(2,1)S(1)}, u32[]{:S(2)}) copy-start(bf16[256,256]{1,0:T(8,128)(2,1)S(1)} %collective-permute-done.11.refs_13_) | copy-start | bytes 393220
  22.1 14.7 %collective-permute-start.15 = (bf16[4,256,256]{2,1,0:T(8,128)(2,1)S(1)}, bf16[4,256,256]{2,1,0:T(8,128)(2,1)S(1)}, u32[]{:S(2)}, u32[]{:S(2)}) collective-permute-start(bf16[4,256,256]{2,1,0:T(8,128)(2,1)S(1)} %pad_maximum_fusion.1), channel_id=1, source_target_pairs={{0,8},{1,9},{2,10},{3,11},{8,16},{9,17},{10,18},{11,19},{12,4},{13... | collective-permute-start | bytes 1572872 | tf_op jit(solution)/shard_map/ppermute | solution.py:291
  25.6 15.1 %copy-start.8 = (bf16[256,256]{1,0:T(8,128)(2,1)}, bf16[256,256]{1,0:T(8,128)(2,1)S(1)}, u32[]{:S(2)}) copy-start(bf16[256,256]{1,0:T(8,128)(2,1)S(1)} %collective-permute-done.13.refs_15_) | copy-start | bytes 393220
  25.7 15.0 %collective-permute-start.14 = (bf16[4,256,256]{2,1,0:T(8,128)(2,1)S(1)}, bf16[4,256,256]{2,1,0:T(8,128)(2,1)S(1)}, u32[]{:S(2)}, u32[]{:S(2)}) collective-permute-start(bf16[4,256,256]{2,1,0:T(8,128)(2,1)S(1)} %pad_maximum_fusion), channel_id=1, source_target_pairs={{4,12},{5,13},{6,14},{7,15},{8,0},{9,1},{10,2},{11,3},{12,20},{13,... | collective-permute-start | bytes 1572872 | tf_op jit(solution)/shard_map/ppermute | solution.py:291
  27.0 14.5 %copy-start.10 = (s32[32]{0:T(128)}, s32[32]{0:T(128)S(1)}, u32[]{:S(2)}) copy-start(s32[32]{0:T(128)S(1)} %get-tuple-element.49.counts_ref) | copy-start | bytes 388
  27.0 14.5 %copy-start.13 = (bf16[256,256]{1,0:T(8,128)(2,1)}, bf16[256,256]{1,0:T(8,128)(2,1)S(1)}, u32[]{:S(2)}) copy-start(bf16[256,256]{1,0:T(8,128)(2,1)S(1)} %collective-permute-done.refs_1_) | copy-start | bytes 393220
  27.1 6.3 %collective-permute-start.3 = (bf16[256,256]{1,0:T(8,128)(2,1)S(1)}, bf16[256,256]{1,0:T(8,128)(2,1)S(1)}, u32[]{:S(2)}, u32[]{:S(2)}) collective-permute-start(bf16[256,256]{1,0:T(8,128)(2,1)S(1)} %copy-done.16), channel_id=1, source_target_pairs={{0,7},{1,6},{2,5},{3,4},{4,3},{5,2},{6,1},{7,0},{8,15},{9,14},{10,... | collective-permute-start | bytes 393224 | tf_op jit(solution)/shard_map/ppermute | solution.py:278
  28.9 11.8 %copy-start.14 = (bf16[256,256]{1,0:T(8,128)(2,1)}, bf16[256,256]{1,0:T(8,128)(2,1)S(1)}, u32[]{:S(2)}) copy-start(bf16[256,256]{1,0:T(8,128)(2,1)S(1)} %collective-permute-done.1.refs_2_) | copy-start | bytes 393220
  28.9 7.3 %collective-permute-start.4 = (bf16[256,256]{1,0:T(8,128)(2,1)}, bf16[256,256]{1,0:T(8,128)(2,1)S(1)}, u32[]{:S(2)}, u32[]{:S(2)}) collective-permute-start(bf16[256,256]{1,0:T(8,128)(2,1)} %get-tuple-element.28), channel_id=1, source_target_pairs={{0,3},{1,2},{2,1},{3,0},{4,7},{5,6},{6,5},{7,4},{8,11},{9,10},{10,... | collective-permute-start | bytes 393224 | tf_op jit(solution)/shard_map/ppermute | solution.py:278
  30.5 10.2 %copy-start.15 = (bf16[256,256]{1,0:T(8,128)(2,1)}, bf16[256,256]{1,0:T(8,128)(2,1)S(1)}, u32[]{:S(2)}) copy-start(bf16[256,256]{1,0:T(8,128)(2,1)S(1)} %collective-permute-done.2.refs_3_) | copy-start | bytes 393220
  30.5 6.2 %collective-permute-start.5 = (bf16[256,256]{1,0:T(8,128)(2,1)}, bf16[256,256]{1,0:T(8,128)(2,1)S(1)}, u32[]{:S(2)}, u32[]{:S(2)}) collective-permute-start(bf16[256,256]{1,0:T(8,128)(2,1)} %get-tuple-element.29), channel_id=1, source_target_pairs={{0,6},{1,7},{2,4},{3,5},{4,2},{5,3},{6,0},{7,1},{8,14},{9,15},{10,... | collective-permute-start | bytes 393224 | tf_op jit(solution)/shard_map/ppermute | solution.py:278
  33.4 7.3 %copy-start.17 = (bf16[256,256]{1,0:T(8,128)(2,1)}, bf16[256,256]{1,0:T(8,128)(2,1)S(1)}, u32[]{:S(2)}) copy-start(bf16[256,256]{1,0:T(8,128)(2,1)S(1)} %collective-permute-done.3.refs_4_) | copy-start | bytes 393220
  33.4 3.4 %collective-permute-start.6 = (bf16[256,256]{1,0:T(8,128)(2,1)}, bf16[256,256]{1,0:T(8,128)(2,1)}, u32[]{:S(2)}, u32[]{:S(2)}) collective-permute-start(bf16[256,256]{1,0:T(8,128)(2,1)} %get-tuple-element.30), channel_id=1, source_target_pairs={{0,2},{1,3},{2,0},{3,1},{4,6},{5,7},{6,4},{7,5},{8,10},{9,11},{10,... | collective-permute-start | bytes 393224 | tf_op jit(solution)/shard_map/ppermute | solution.py:278
  36.2 4.5 %copy-start.19 = (bf16[256,256]{1,0:T(8,128)(2,1)}, bf16[256,256]{1,0:T(8,128)(2,1)S(1)}, u32[]{:S(2)}) copy-start(bf16[256,256]{1,0:T(8,128)(2,1)S(1)} %collective-permute-done.4.refs_5_) | copy-start | bytes 393220
  36.7 4.0 %copy-start.20 = (bf16[256,256]{1,0:T(8,128)(2,1)}, bf16[256,256]{1,0:T(8,128)(2,1)S(1)}, u32[]{:S(2)}) copy-start(bf16[256,256]{1,0:T(8,128)(2,1)S(1)} %collective-permute-done.5.refs_6_) | copy-start | bytes 393220
  36.8 4.0 %copy-start.11 = (bf16[4,256,256]{2,1,0:T(8,128)(2,1)}, bf16[4,256,256]{2,1,0:T(8,128)(2,1)S(1)}, u32[]{:S(2)}) copy-start(bf16[4,256,256]{2,1,0:T(8,128)(2,1)S(1)} %collective-permute-done.15.refs_17_) | copy-start | bytes 1572868
  40.7 0.8 copy-start.12
  53.0 21.0 %copy-start = (bf16[2048,256]{1,0:T(8,128)(2,1)S(1)}, bf16[2048,256]{1,0:T(8,128)(2,1)}, u32[]{:S(2)}) copy-start(bf16[2048,256]{1,0:T(8,128)(2,1)} %get-tuple-element.40) | copy-start | bytes 3145732
  53.0 16.7 %collective-permute-start.16 = (bf16[1024,256]{1,0:T(8,128)(2,1)}, bf16[1024,256]{1,0:T(8,128)(2,1)S(1)}, u32[]{:S(2)}, u32[]{:S(2)}) collective-permute-start(bf16[1024,256]{1,0:T(8,128)(2,1)} %get-tuple-element.41), channel_id=1, source_target_pairs={{0,8},{8,16},{16,24},{1,9},{9,17},{17,25},{2,10},{10,18},{18,26},{... | collective-permute-start | bytes 1572872 | tf_op jit(solution)/shard_map/ppermute | solution.py:308
  59.7 14.3 %collective-permute-start.17 = (bf16[1024,256]{1,0:T(8,128)(2,1)}, bf16[1024,256]{1,0:T(8,128)(2,1)S(1)}, u32[]{:S(2)}, u32[]{:S(2)}) collective-permute-start(bf16[1024,256]{1,0:T(8,128)(2,1)} %get-tuple-element.42), channel_id=1, source_target_pairs={{8,0},{16,8},{24,16},{9,1},{17,9},{25,17},{10,2},{18,10},{26,18},{... | collective-permute-start | bytes 1572872 | tf_op jit(solution)/shard_map/ppermute | solution.py:307
  61.0 14.3 %all-to-all-start = ((bf16[8,256,128]{2,1,0:T(8,128)(2,1)}), bf16[8,256,128]{2,1,0:T(8,128)(2,1)S(1)}, u32[]{:S(2)}, u32[]{:S(2)}) async-start(bf16[8,256,128]{2,1,0:T(8,128)(2,1)} %get-tuple-element.39), calls=%async_computation | async-start | bytes 1048576 | tf_op jit(solution)/shard_map/all_to_all | solution.py:271
  75.3 18.4 %all-to-all-start.1 = ((bf16[8,256,256]{2,1,0:T(8,128)(2,1)}), bf16[8,256,256]{2,1,0:T(8,128)(2,1)S(1)}, u32[]{:S(2)}, u32[]{:S(2)}) async-start(bf16[8,256,256]{2,1,0:T(8,128)(2,1)} %bitcast.11), calls=%async_computation.1 | async-start | bytes 2097152 | tf_op jit(solution)/shard_map/all_to_all | solution.py:271

commit v4 on v3

--- a/solution.py
+++ b/solution.py
@@ -293,9 +293,13 @@
     up = [(i, i + 1) for i in range(outer - 1)]
     down = [(i + 1, i) for i in range(outer - 1)]
     own = scatter(join_columns(my_slab, keys_in, values, peers))
-    qd = scatter(join_columns(my_slab, queries, d_out, peers))
-    near = beside(jnp.stack(own[:half]), -1, 1)
-    across = beside(jnp.stack(own[half:]), 1, -1)
+    near, across = jnp.stack(own[:half]), jnp.stack(own[half:])
+    qd = list(join_columns(my_slab, queries, d_out, peers))
+    across, *held = lax.optimization_barrier([across] + [qd[k] for k in SENDS[1:]])
+    for k, slab in zip(SENDS[1:], held):
+        qd[k] = slab
+    near, across = beside(near, -1, 1), beside(across, 1, -1)
+    qd = scatter(qd)
     first = lax.axis_index("outer") * blocks
     lists, counts, order = compact_lists(
         pair_blocks, pair_count, first, blocks, first - halo_blocks, blocks + 2 * halo_blocks

time: 96.2 us -> 101 us (1.050); the launches traced: 95.1 us -> 102 us
  Pallas kernels: 15.8 us -> 19.3 us
  waiting for transfers between devices: 35.3 us -> 38.8 us
  starting transfers between devices: 36.2 us -> 35.1 us
    ppermute x14, waiting for transfers between devices: 8.2 us -> 14.2 us  [send(): return lax.ppermute(slab, group, [(i, i ^ k) for i in range(peers)])]
    ppermute x2, waiting for transfers between devices: 3.93 us -> 0.01 us  [beside(): return lax.ppermute(slabs, ('outer',) + group, pairs)]
    pallas_call x1, Pallas kernels: 11.5 us -> 15 us  [attend(): pl.pallas_call(attend_kernel, out_shape=(shaped((peers, rows // peers, LA...]
    ppermute x1, waiting for transfers between devices: 5.15 us -> 6.91 us  [on_device(): from_below = lax.ppermute(grad_right, 'outer', up)]
    ppermute x1, starting transfers between devices: 6.69 us -> 5.57 us  [on_device(): from_below = lax.ppermute(grad_right, 'outer', up)]
    unnamed x46 -> x48, local copies, waits for them, and re-layouts: 2.14 us -> 2.9 us
  transfers between devices with their start and end apart: 20 -> 20, of which waited for: 8 -> 8; matrix products, arithmetic and copies ran while one was open for 5% -> 4% of each run, Pallas kernels for 2% -> 2%
where the time goes in v4:
time: 101 us; the launch traced here: 102 us
  waiting for transfers between devices  38.8 us (38%)
  starting transfers between devices  35.1 us (35%)
  Pallas kernels  19.3 us (19%)
  local copies, waits for them, and re-layouts  5 us (5%)
  other arithmetic  2.55 us (3%)
  between operations  1.03 us (1%)
    ppermute x14, starting transfers between devices, send(): return lax.ppermute(slab, group, [(i, i ^ k) for i in range(peers)])  16.3 us
    pallas_call x1, Pallas kernels, attend(): pl.pallas_call(attend_kernel, out_shape=(shaped((peers, rows // peers, LA...  15 us
    ppermute x14, waiting for transfers between devices, send(): return lax.ppermute(slab, group, [(i, i ^ k) for i in range(peers)])  14.2 us
    all_to_all x2, waiting for transfers between devices, exchange(): return lax.all_to_all(parts, group, split_axis=0, concat_axis=0, tiled=True)  13.6 us
    all_to_all x2, starting transfers between devices, exchange(): return lax.all_to_all(parts, group, split_axis=0, concat_axis=0, tiled=True)  7.06 us
    ppermute x1, waiting for transfers between devices, on_device(): from_below = lax.ppermute(grad_right, 'outer', up)  6.91 us
    ppermute x1, starting transfers between devices, on_device(): from_below = lax.ppermute(grad_right, 'outer', up)  5.57 us
    ppermute x2, starting transfers between devices, beside(): return lax.ppermute(slabs, ('outer',) + group, pairs)  4.94 us
  transfers between devices with their start and end apart: 20, of which 8 were waited for; matrix products, arithmetic and copies ran while one was open for 4% of the time, Pallas kernels for 2%

profile of v4, /device:TPU:0, one launch (start us, length us, event | category | flops | bytes accessed | tf_op | source)
XLA Modules:
  0.0 101.8 jit_solution(16281173845617507925)
XLA Ops:
  0.7 2.1 %pack.3 = (bf16[256,256]{1,0:T(8,128)(2,1)}, bf16[256,256]{1,0:T(8,128)(2,1)}, bf16[256,256]{1,0:T(8,128)(2,1)}, bf16[256,256]{1,0:T(8,128)(2,1)}, bf16[256,256]...) custom-call(s32[1]{0:T(128)} %bitcast.me_ref, ...), custom_call_target="tpu_custom_call" | custom-call | bytes 2000000 | tf_op jit(solution)/shard_map/pack/pallas_call | solution.py:225
  2.8 3.0 %collective-permute-start.1 = (bf16[256,256]{1,0:T(8,128)(2,1)}, bf16[256,256]{1,0:T(8,128)(2,1)S(1)}, u32[]{:S(2)}, u32[]{:S(2)}) collective-permute-start(bf16[256,256]{1,0:T(8,128)(2,1)} %get-tuple-element.32), channel_id=1, source_target_pairs={{0,4},{1,5},{2,6},{3,7},{4,0},{5,1},{6,2},{7,3},{8,12},{9,13},{10,... | collective-permute-start | bytes 393224 | tf_op jit(solution)/shard_map/ppermute | solution.py:278
  5.8 1.4 %collective-permute-start.2 = (bf16[256,256]{1,0:T(8,128)(2,1)}, bf16[256,256]{1,0:T(8,128)(2,1)S(1)}, u32[]{:S(2)}, u32[]{:S(2)}) collective-permute-start(bf16[256,256]{1,0:T(8,128)(2,1)} %get-tuple-element.33), channel_id=1, source_target_pairs={{0,5},{1,4},{2,7},{3,6},{4,1},{5,0},{6,3},{7,2},{8,13},{9,12},{10,... | collective-permute-start | bytes 393224 | tf_op jit(solution)/shard_map/ppermute | solution.py:278
  7.3 0.4 collective-permute-start.3
  7.7 0.9 collective-permute-start.4
  8.6 1.9 %collective-permute-start.11 = (bf16[256,256]{1,0:T(8,128)(2,1)}, bf16[256,256]{1,0:T(8,128)(2,1)S(1)}, u32[]{:S(2)}, u32[]{:S(2)}) collective-permute-start(bf16[256,256]{1,0:T(8,128)(2,1)} %get-tuple-element.49), channel_id=1, source_target_pairs={{0,1},{1,0},{2,3},{3,2},{4,5},{5,4},{6,7},{7,6},{8,9},{9,8},{10,11... | collective-permute-start | bytes 393224 | tf_op jit(solution)/shard_map/ppermute | solution.py:278
  10.5 0.1 subtract_clamp_fusion
  10.6 5.0 %collective-permute-done.1.refs_9_ = bf16[256,256]{1,0:T(8,128)(2,1)S(1)} collective-permute-done((bf16[256,256]{1,0:T(8,128)(2,1)}, bf16[256,256]{1,0:T(8,128)(2,1)S(1)}, u32[]{:S(2)}, u32[]{:S(2)}) %collective-permute-start.1) | collective-permute-done | bytes 131104 | tf_op jit(solution)/shard_map/ppermute | solution.py:278
  15.6 0.0 collective-permute-done.2.refs_11_
  15.6 2.0 %collective-permute-start.13 = (bf16[256,256]{1,0:T(8,128)(2,1)}, bf16[256,256]{1,0:T(8,128)(2,1)S(1)}, u32[]{:S(2)}, u32[]{:S(2)}) collective-permute-start(bf16[256,256]{1,0:T(8,128)(2,1)} %get-tuple-element.51), channel_id=1, source_target_pairs={{0,2},{1,3},{2,0},{3,1},{4,6},{5,7},{6,4},{7,5},{8,10},{9,11},{10,... | collective-permute-start | bytes 393224 | tf_op jit(solution)/shard_map/ppermute | solution.py:278
  17.7 0.1 and_reduce_fusion
  17.8 0.1 dynamic_slice.6
  17.9 2.1 %pack.2 = (bf16[256,256]{1,0:T(8,128)(2,1)}, bf16[256,256]{1,0:T(8,128)(2,1)}, bf16[256,256]{1,0:T(8,128)(2,1)}, bf16[256,256]{1,0:T(8,128)(2,1)}, bf16[256,256]...) custom-call(s32[1]{0:T(128)} %bitcast.me_ref, ...), custom_call_target="tpu_custom_call" | custom-call | bytes 2000000 | tf_op jit(solution)/shard_map/pack/pallas_call | solution.py:225
  20.0 0.0 collective-permute-done.3.refs_14_
  20.1 2.0 %collective-permute-start = (bf16[256,256]{1,0:T(8,128)(2,1)}, bf16[256,256]{1,0:T(8,128)(2,1)S(1)}, u32[]{:S(2)}, u32[]{:S(2)}) collective-permute-start(bf16[256,256]{1,0:T(8,128)(2,1)} %get-tuple-element.31), channel_id=1, source_target_pairs={{0,4},{1,5},{2,6},{3,7},{4,0},{5,1},{6,2},{7,3},{8,12},{9,13},{10,... | collective-permute-start | bytes 393224 | tf_op jit(solution)/shard_map/ppermute | solution.py:278
  22.1 0.0 collective-permute-done.4.refs_12_
  22.1 0.0 copy-start.14
  22.1 0.1 pad_maximum_fusion
  22.2 3.6 %collective-permute-start.15 = (bf16[4,256,256]{2,1,0:T(8,128)(2,1)S(1)}, bf16[4,256,256]{2,1,0:T(8,128)(2,1)S(1)}, u32[]{:S(2)}, u32[]{:S(2)}) collective-permute-start(bf16[4,256,256]{2,1,0:T(8,128)(2,1)S(1)} %pad_maximum_fusion), channel_id=1, source_target_pairs={{0,8},{1,9},{2,10},{3,11},{8,16},{9,17},{10,18},{11,19},{12,4},{13... | collective-permute-start | bytes 1572872 | tf_op jit(solution)/shard_map/ppermute | solution.py:291
  26.0 0.1 pad_maximum_fusion.1
  26.1 1.3 %collective-permute-start.14 = (bf16[4,256,256]{2,1,0:T(8,128)(2,1)S(1)}, bf16[4,256,256]{2,1,0:T(8,128)(2,1)S(1)}, u32[]{:S(2)}, u32[]{:S(2)}) collective-permute-start(bf16[4,256,256]{2,1,0:T(8,128)(2,1)S(1)} %pad_maximum_fusion.1), channel_id=1, source_target_pairs={{4,12},{5,13},{6,14},{7,15},{8,0},{9,1},{10,2},{11,3},{12,20},{13,... | collective-permute-start | bytes 1572872 | tf_op jit(solution)/shard_map/ppermute | solution.py:291
  27.4 0.6 collective-permute-start.5
  28.0 2.0 %collective-permute-start.6 = (bf16[256,256]{1,0:T(8,128)(2,1)S(1)}, bf16[256,256]{1,0:T(8,128)(2,1)S(1)}, u32[]{:S(2)}, u32[]{:S(2)}) collective-permute-start(bf16[256,256]{1,0:T(8,128)(2,1)S(1)} %copy-done.19), channel_id=1, source_target_pairs={{0,5},{1,4},{2,7},{3,6},{4,1},{5,0},{6,3},{7,2},{8,13},{9,12},{10,... | collective-permute-start | bytes 393224 | tf_op jit(solution)/shard_map/ppermute | solution.py:278
  30.1 0.1 collective-permute-start.7
  30.1 0.1 select_reduce_fusion.1
  30.3 3.6 %collective-permute-done.5.refs_2_ = bf16[256,256]{1,0:T(8,128)(2,1)S(1)} collective-permute-done((bf16[256,256]{1,0:T(8,128)(2,1)S(1)}, bf16[256,256]{1,0:T(8,128)(2,1)S(1)}, u32[]{:S(2)}, u32[]{:S(2)}) %collective-permute-start.5) | collective-permute-done | bytes 131104 | tf_op jit(solution)/shard_map/ppermute | solution.py:278
  33.9 3.2 %collective-permute-done.6.refs_3_ = bf16[256,256]{1,0:T(8,128)(2,1)S(1)} collective-permute-done((bf16[256,256]{1,0:T(8,128)(2,1)S(1)}, bf16[256,256]{1,0:T(8,128)(2,1)S(1)}, u32[]{:S(2)}, u32[]{:S(2)}) %collective-permute-start.6) | collective-permute-done | bytes 131104 | tf_op jit(solution)/shard_map/ppermute | solution.py:278
  37.1 0.2 collective-permute-done.7.refs_4_
  37.3 1.8 %collective-permute-start.10 = (bf16[256,256]{1,0:T(8,128)(2,1)S(1)}, bf16[256,256]{1,0:T(8,128)(2,1)}, u32[]{:S(2)}, u32[]{:S(2)}) collective-permute-start(bf16[256,256]{1,0:T(8,128)(2,1)S(1)} %copy-done.14), channel_id=1, source_target_pairs={{0,2},{1,3},{2,0},{3,1},{4,6},{5,7},{6,4},{7,5},{8,10},{9,11},{10,... | collective-permute-start | bytes 393224 | tf_op jit(solution)/shard_map/ppermute | solution.py:278
  39.1 0.2 convert_reduce_fusion
  39.3 0.7 copy.19.lists_ref
  39.9 0.6 select_reduce_fusion.2.order_ref
  40.5 2.1 %collective-permute-done.9.refs_6_ = bf16[256,256]{1,0:T(8,128)(2,1)} collective-permute-done((bf16[256,256]{1,0:T(8,128)(2,1)}, bf16[256,256]{1,0:T(8,128)(2,1)}, u32[]{:S(2)}, u32[]{:S(2)}) %collective-permute-start.9) | collective-permute-done | bytes 131104 | tf_op jit(solution)/shard_map/ppermute | solution.py:278
  42.7 0.8 copy-done.11
  43.5 0.8 copy-done.12
  44.3 15.0 %attend.1 = (bf16[8,256,128]{2,1,0:T(8,128)(2,1)}, bf16[1024,256]{1,0:T(8,128)(2,1)}, bf16[2048,256]{1,0:T(8,128)(2,1)}, bf16[1024,256]{1,0:T(8,128)(2,1)}) custom-call(s32[1]{0:T(128)} %bitcast.me_ref, s32[32,16]{1,0:T(8,128)} %copy.19.lists_ref, s32[32]{0:T(128)} %copy-done.10, s32[32]{0:T(128)} %select_reduce_fusion.2.order_ref, ...), custom_call_target="tpu_custom_call" | custom-call | flops 4000000000 | bytes 6000000 | tf_op jit(solution)/shard_map/attend/pallas_call | solution.py:161
  59.4 5.6 %collective-permute-start.16 = (bf16[1024,256]{1,0:T(8,128)(2,1)}, bf16[1024,256]{1,0:T(8,128)(2,1)S(1)}, u32[]{:S(2)}, u32[]{:S(2)}) collective-permute-start(bf16[1024,256]{1,0:T(8,128)(2,1)} %get-tuple-element.55), channel_id=1, source_target_pairs={{0,8},{8,16},{16,24},{1,9},{9,17},{17,25},{2,10},{10,18},{18,26},{... | collective-permute-start | bytes 1572872 | tf_op jit(solution)/shard_map/ppermute | solution.py:312
  64.9 1.3 %collective-permute-start.17 = (bf16[1024,256]{1,0:T(8,128)(2,1)}, bf16[1024,256]{1,0:T(8,128)(2,1)S(1)}, u32[]{:S(2)}, u32[]{:S(2)}) collective-permute-start(bf16[1024,256]{1,0:T(8,128)(2,1)} %get-tuple-element.56), channel_id=1, source_target_pairs={{8,0},{16,8},{24,16},{9,1},{17,9},{25,17},{10,2},{18,10},{26,18},{... | collective-permute-start | bytes 1572872 | tf_op jit(solution)/shard_map/ppermute | solution.py:311
  66.2 3.5 %all-to-all-start = ((bf16[8,256,128]{2,1,0:T(8,128)(2,1)}), bf16[8,256,128]{2,1,0:T(8,128)(2,1)S(1)}, u32[]{:S(2)}, u32[]{:S(2)}) async-start(bf16[8,256,128]{2,1,0:T(8,128)(2,1)} %get-tuple-element.53), calls=%async_computation | async-start | bytes 1048576 | tf_op jit(solution)/shard_map/all_to_all | solution.py:271
  69.8 6.9 %collective-permute-done.16 = bf16[1024,256]{1,0:T(8,128)(2,1)S(1)} collective-permute-done((bf16[1024,256]{1,0:T(8,128)(2,1)}, bf16[1024,256]{1,0:T(8,128)(2,1)S(1)}, u32[]{:S(2)}, u32[]{:S(2)}) %collective-permute-start.16) | collective-permute-done | bytes 524320 | tf_op jit(solution)/shard_map/ppermute | solution.py:312
  76.7 4.0 %collective-permute-done.17 = bf16[1024,256]{1,0:T(8,128)(2,1)S(1)} collective-permute-done((bf16[1024,256]{1,0:T(8,128)(2,1)}, bf16[1024,256]{1,0:T(8,128)(2,1)S(1)}, u32[]{:S(2)}, u32[]{:S(2)}) %collective-permute-start.17) | collective-permute-done | bytes 524320 | tf_op jit(solution)/shard_map/ppermute | solution.py:311
  80.7 1.2 %add_convert_fusion = bf16[2048,256]{1,0:T(8,128)(2,1)} fusion(bf16[2048,256]{1,0:T(8,128)(2,1)S(1)} %copy-done, bf16[1024,256]{1,0:T(8,128)(2,1)S(1)} %collective-permute-done.17, bf16[1024,256]{1,0:T(8,128)(2,1)S(1)} %collective-permute-done.16), kind=kLoop, calls=%fused_computation | loop fusion | flops 3670016 | bytes 3145728 | tf_op jit(solution)/shard_map/convert_element_type | solution.py:315
  82.0 3.6 %all-to-all-start.1 = ((bf16[8,256,256]{2,1,0:T(8,128)(2,1)}), bf16[8,256,256]{2,1,0:T(8,128)(2,1)S(1)}, u32[]{:S(2)}, u32[]{:S(2)}) async-start(bf16[8,256,256]{2,1,0:T(8,128)(2,1)} %bitcast.11), calls=%async_computation.1 | async-start | bytes 2097152 | tf_op jit(solution)/shard_map/all_to_all | solution.py:271
  85.5 0.2 copy.20
  85.7 1.0 copy.23
  86.7 13.6 %all-to-all-done.1 = bf16[8,256,256]{2,1,0:T(8,128)(2,1)S(1)} async-done(((bf16[8,256,256]{2,1,0:T(8,128)(2,1)}), bf16[8,256,256]{2,1,0:T(8,128)(2,1)S(1)}, u32[]{:S(2)}, u32[]{:S(2)}) %all-to-all-start.1) | async-done | bytes 1048608 | tf_op jit(solution)/shard_map/all_to_all | solution.py:271
  100.4 0.3 slice_bitcast_fusion
  100.6 1.1 %copy_bitcast_fusion = (bf16[256,1024]{1,0:T(8,128)(2,1)}, bf16[256,1024]{1,0:T(8,128)(2,1)}) fusion(bf16[8,32,8,128]{3,2,1,0:T(8,128)(2,1)S(1)} %get-tuple-element.65, bf16[8,32,8,128]{3,2,1,0:T(8,128)(2,1)S(1)} %get-tuple-element.66), kind=kLoop, calls=%fused_computation.1 | loop fusion | bytes 2097152 | tf_op jit(solution)/shard_map/reshape | solution.py:319
  (59 shorter events, 0.2 us)
Async XLA Ops:
  0.6 9.8 %copy-start.9 = (s32[128,16]{0,1:T(8,128)S(1)}, s32[128,16]{0,1:T(8,128)}, u32[]{:S(2)}) copy-start(s32[128,16]{0,1:T(8,128)} %param.10) | copy-start | bytes 24580
  0.6 17.2 %copy-start.22 = (s32[128]{0:T(128)S(1)}, s32[128]{0:T(128)}, u32[]{:S(2)}) copy-start(s32[128]{0:T(128)} %param.11) | copy-start | bytes 1540
  2.8 12.8 %collective-permute-start.1 = (bf16[256,256]{1,0:T(8,128)(2,1)}, bf16[256,256]{1,0:T(8,128)(2,1)S(1)}, u32[]{:S(2)}, u32[]{:S(2)}) collective-permute-start(bf16[256,256]{1,0:T(8,128)(2,1)} %get-tuple-element.32), channel_id=1, source_target_pairs={{0,4},{1,5},{2,6},{3,7},{4,0},{5,1},{6,2},{7,3},{8,12},{9,13},{10,... | collective-permute-start | bytes 393224 | tf_op jit(solution)/shard_map/ppermute | solution.py:278
  5.8 9.8 %collective-permute-start.2 = (bf16[256,256]{1,0:T(8,128)(2,1)}, bf16[256,256]{1,0:T(8,128)(2,1)S(1)}, u32[]{:S(2)}, u32[]{:S(2)}) collective-permute-start(bf16[256,256]{1,0:T(8,128)(2,1)} %get-tuple-element.33), channel_id=1, source_target_pairs={{0,5},{1,4},{2,7},{3,6},{4,1},{5,0},{6,3},{7,2},{8,13},{9,12},{10,... | collective-permute-start | bytes 393224 | tf_op jit(solution)/shard_map/ppermute | solution.py:278
  7.3 12.8 %collective-permute-start.3 = (bf16[256,256]{1,0:T(8,128)(2,1)}, bf16[256,256]{1,0:T(8,128)(2,1)S(1)}, u32[]{:S(2)}, u32[]{:S(2)}) collective-permute-start(bf16[256,256]{1,0:T(8,128)(2,1)} %get-tuple-element.34), channel_id=1, source_target_pairs={{0,6},{1,7},{2,4},{3,5},{4,2},{5,3},{6,0},{7,1},{8,14},{9,15},{10,... | collective-permute-start | bytes 393224 | tf_op jit(solution)/shard_map/ppermute | solution.py:278
  7.7 14.4 %collective-permute-start.4 = (bf16[256,256]{1,0:T(8,128)(2,1)}, bf16[256,256]{1,0:T(8,128)(2,1)S(1)}, u32[]{:S(2)}, u32[]{:S(2)}) collective-permute-start(bf16[256,256]{1,0:T(8,128)(2,1)} %get-tuple-element.35), channel_id=1, source_target_pairs={{0,7},{1,6},{2,5},{3,4},{4,3},{5,2},{6,1},{7,0},{8,15},{9,14},{10,... | collective-permute-start | bytes 393224 | tf_op jit(solution)/shard_map/ppermute | solution.py:278
  8.6 17.3 %collective-permute-start.11 = (bf16[256,256]{1,0:T(8,128)(2,1)}, bf16[256,256]{1,0:T(8,128)(2,1)S(1)}, u32[]{:S(2)}, u32[]{:S(2)}) collective-permute-start(bf16[256,256]{1,0:T(8,128)(2,1)} %get-tuple-element.49), channel_id=1, source_target_pairs={{0,1},{1,0},{2,3},{3,2},{4,5},{5,4},{6,7},{7,6},{8,9},{9,8},{10,11... | collective-permute-start | bytes 393224 | tf_op jit(solution)/shard_map/ppermute | solution.py:278
  15.6 6.6 %copy-start.2 = (bf16[256,256]{1,0:T(8,128)(2,1)}, bf16[256,256]{1,0:T(8,128)(2,1)S(1)}, u32[]{:S(2)}) copy-start(bf16[256,256]{1,0:T(8,128)(2,1)S(1)} %collective-permute-done.1.refs_9_) | copy-start | bytes 393220
  15.6 10.3 %collective-permute-start.12 = (bf16[256,256]{1,0:T(8,128)(2,1)}, bf16[256,256]{1,0:T(8,128)(2,1)S(1)}, u32[]{:S(2)}, u32[]{:S(2)}) collective-permute-start(bf16[256,256]{1,0:T(8,128)(2,1)} %get-tuple-element.50), channel_id=1, source_target_pairs={{0,3},{1,2},{2,1},{3,0},{4,7},{5,6},{6,5},{7,4},{8,11},{9,10},{10,... | collective-permute-start | bytes 393224 | tf_op jit(solution)/shard_map/ppermute | solution.py:278
  15.6 6.6 %copy-start.3 = (bf16[256,256]{1,0:T(8,128)(2,1)}, bf16[256,256]{1,0:T(8,128)(2,1)S(1)}, u32[]{:S(2)}) copy-start(bf16[256,256]{1,0:T(8,128)(2,1)S(1)} %collective-permute-done.2.refs_11_) | copy-start | bytes 393220
  15.6 10.3 %collective-permute-start.13 = (bf16[256,256]{1,0:T(8,128)(2,1)}, bf16[256,256]{1,0:T(8,128)(2,1)S(1)}, u32[]{:S(2)}, u32[]{:S(2)}) collective-permute-start(bf16[256,256]{1,0:T(8,128)(2,1)} %get-tuple-element.51), channel_id=1, source_target_pairs={{0,2},{1,3},{2,0},{3,1},{4,6},{5,7},{6,4},{7,5},{8,10},{9,11},{10,... | collective-permute-start | bytes 393224 | tf_op jit(solution)/shard_map/ppermute | solution.py:278
  17.9 8.1 %copy-start.1 = (bf16[256,256]{1,0:T(8,128)(2,1)S(1)}, bf16[256,256]{1,0:T(8,128)(2,1)}, u32[]{:S(2)}) copy-start(bf16[256,256]{1,0:T(8,128)(2,1)} %get-tuple-element.48.refs_8_) | copy-start | bytes 393220
  20.0 6.0 %copy-start.4 = (bf16[256,256]{1,0:T(8,128)(2,1)}, bf16[256,256]{1,0:T(8,128)(2,1)S(1)}, u32[]{:S(2)}) copy-start(bf16[256,256]{1,0:T(8,128)(2,1)S(1)} %collective-permute-done.3.refs_14_) | copy-start | bytes 393220
  20.1 10.0 %collective-permute-start = (bf16[256,256]{1,0:T(8,128)(2,1)}, bf16[256,256]{1,0:T(8,128)(2,1)S(1)}, u32[]{:S(2)}, u32[]{:S(2)}) collective-permute-start(bf16[256,256]{1,0:T(8,128)(2,1)} %get-tuple-element.31), channel_id=1, source_target_pairs={{0,4},{1,5},{2,6},{3,7},{4,0},{5,1},{6,2},{7,3},{8,12},{9,13},{10,... | collective-permute-start | bytes 393224 | tf_op jit(solution)/shard_map/ppermute | solution.py:278
  22.1 3.9 %copy-start.5 = (bf16[256,256]{1,0:T(8,128)(2,1)}, bf16[256,256]{1,0:T(8,128)(2,1)S(1)}, u32[]{:S(2)}) copy-start(bf16[256,256]{1,0:T(8,128)(2,1)S(1)} %collective-permute-done.4.refs_12_) | copy-start | bytes 393220
  22.1 5.3 %copy-start.20 = (bf16[256,256]{1,0:T(8,128)(2,1)S(1)}, bf16[256,256]{1,0:T(8,128)(2,1)}, u32[]{:S(2)}) copy-start(bf16[256,256]{1,0:T(8,128)(2,1)} %get-tuple-element.42) | copy-start | bytes 393220
  22.1 5.9 %copy-start.19 = (bf16[256,256]{1,0:T(8,128)(2,1)S(1)}, bf16[256,256]{1,0:T(8,128)(2,1)}, u32[]{:S(2)}) copy-start(bf16[256,256]{1,0:T(8,128)(2,1)} %get-tuple-element.43) | copy-start | bytes 393220
  22.1 7.9 %copy-start.17 = (bf16[256,256]{1,0:T(8,128)(2,1)S(1)}, bf16[256,256]{1,0:T(8,128)(2,1)}, u32[]{:S(2)}) copy-start(bf16[256,256]{1,0:T(8,128)(2,1)} %get-tuple-element.44) | copy-start | bytes 393220
  22.1 15.2 %copy-start.14 = (bf16[256,256]{1,0:T(8,128)(2,1)S(1)}, bf16[256,256]{1,0:T(8,128)(2,1)}, u32[]{:S(2)}) copy-start(bf16[256,256]{1,0:T(8,128)(2,1)} %get-tuple-element.47) | copy-start | bytes 393220
  22.2 20.4 %collective-permute-start.15 = (bf16[4,256,256]{2,1,0:T(8,128)(2,1)S(1)}, bf16[4,256,256]{2,1,0:T(8,128)(2,1)S(1)}, u32[]{:S(2)}, u32[]{:S(2)}) collective-permute-start(bf16[4,256,256]{2,1,0:T(8,128)(2,1)S(1)} %pad_maximum_fusion), channel_id=1, source_target_pairs={{0,8},{1,9},{2,10},{3,11},{8,16},{9,17},{10,18},{11,19},{12,4},{13... | collective-permute-start | bytes 1572872 | tf_op jit(solution)/shard_map/ppermute | solution.py:291
  25.9 18.4 %copy-start.6 = (bf16[256,256]{1,0:T(8,128)(2,1)}, bf16[256,256]{1,0:T(8,128)(2,1)S(1)}, u32[]{:S(2)}) copy-start(bf16[256,256]{1,0:T(8,128)(2,1)S(1)} %collective-permute-done.11.refs_10_) | copy-start | bytes 393220
  25.9 18.3 %copy-start.7 = (bf16[256,256]{1,0:T(8,128)(2,1)}, bf16[256,256]{1,0:T(8,128)(2,1)S(1)}, u32[]{:S(2)}) copy-start(bf16[256,256]{1,0:T(8,128)(2,1)S(1)} %collective-permute-done.12.refs_13_) | copy-start | bytes 393220
  25.9 16.8 %copy-start.8 = (bf16[256,256]{1,0:T(8,128)(2,1)}, bf16[256,256]{1,0:T(8,128)(2,1)S(1)}, u32[]{:S(2)}) copy-start(bf16[256,256]{1,0:T(8,128)(2,1)S(1)} %collective-permute-done.13.refs_15_) | copy-start | bytes 393220
  26.1 16.6 %collective-permute-start.14 = (bf16[4,256,256]{2,1,0:T(8,128)(2,1)S(1)}, bf16[4,256,256]{2,1,0:T(8,128)(2,1)S(1)}, u32[]{:S(2)}, u32[]{:S(2)}) collective-permute-start(bf16[4,256,256]{2,1,0:T(8,128)(2,1)S(1)} %pad_maximum_fusion.1), channel_id=1, source_target_pairs={{4,12},{5,13},{6,14},{7,15},{8,0},{9,1},{10,2},{11,3},{12,20},{13,... | collective-permute-start | bytes 1572872 | tf_op jit(solution)/shard_map/ppermute | solution.py:291
  27.4 16.9 %copy-start.10 = (s32[32]{0:T(128)}, s32[32]{0:T(128)S(1)}, u32[]{:S(2)}) copy-start(s32[32]{0:T(128)S(1)} %get-tuple-element.63.counts_ref) | copy-start | bytes 388
  27.4 6.5 %collective-permute-start.5 = (bf16[256,256]{1,0:T(8,128)(2,1)S(1)}, bf16[256,256]{1,0:T(8,128)(2,1)S(1)}, u32[]{:S(2)}, u32[]{:S(2)}) collective-permute-start(bf16[256,256]{1,0:T(8,128)(2,1)S(1)} %copy-done.20), channel_id=1, source_target_pairs={{0,1},{1,0},{2,3},{3,2},{4,5},{5,4},{6,7},{7,6},{8,9},{9,8},{10,11... | collective-permute-start | bytes 393224 | tf_op jit(solution)/shard_map/ppermute | solution.py:278
  28.0 9.1 %collective-permute-start.6 = (bf16[256,256]{1,0:T(8,128)(2,1)S(1)}, bf16[256,256]{1,0:T(8,128)(2,1)S(1)}, u32[]{:S(2)}, u32[]{:S(2)}) collective-permute-start(bf16[256,256]{1,0:T(8,128)(2,1)S(1)} %copy-done.19), channel_id=1, source_target_pairs={{0,5},{1,4},{2,7},{3,6},{4,1},{5,0},{6,3},{7,2},{8,13},{9,12},{10,... | collective-permute-start | bytes 393224 | tf_op jit(solution)/shard_map/ppermute | solution.py:278
  30.1 12.6 %copy-start.13 = (bf16[256,256]{1,0:T(8,128)(2,1)}, bf16[256,256]{1,0:T(8,128)(2,1)S(1)}, u32[]{:S(2)}) copy-start(bf16[256,256]{1,0:T(8,128)(2,1)S(1)} %collective-permute-done.refs_1_) | copy-start | bytes 393220
  30.1 7.2 %collective-permute-start.7 = (bf16[256,256]{1,0:T(8,128)(2,1)S(1)}, bf16[256,256]{1,0:T(8,128)(2,1)S(1)}, u32[]{:S(2)}, u32[]{:S(2)}) collective-permute-start(bf16[256,256]{1,0:T(8,128)(2,1)S(1)} %copy-done.17), channel_id=1, source_target_pairs={{0,7},{1,6},{2,5},{3,4},{4,3},{5,2},{6,1},{7,0},{8,15},{9,14},{10,... | collective-permute-start | bytes 393224 | tf_op jit(solution)/shard_map/ppermute | solution.py:278
  33.9 10.4 %copy-start.15 = (bf16[256,256]{1,0:T(8,128)(2,1)}, bf16[256,256]{1,0:T(8,128)(2,1)S(1)}, u32[]{:S(2)}) copy-start(bf16[256,256]{1,0:T(8,128)(2,1)S(1)} %collective-permute-done.5.refs_2_) | copy-start | bytes 393220
  33.9 6.6 %collective-permute-start.8 = (bf16[256,256]{1,0:T(8,128)(2,1)}, bf16[256,256]{1,0:T(8,128)(2,1)S(1)}, u32[]{:S(2)}, u32[]{:S(2)}) collective-permute-start(bf16[256,256]{1,0:T(8,128)(2,1)} %get-tuple-element.45), channel_id=1, source_target_pairs={{0,3},{1,2},{2,1},{3,0},{4,7},{5,6},{6,5},{7,4},{8,11},{9,10},{10,... | collective-permute-start | bytes 393224 | tf_op jit(solution)/shard_map/ppermute | solution.py:278
  37.1 7.2 %copy-start.16 = (bf16[256,256]{1,0:T(8,128)(2,1)}, bf16[256,256]{1,0:T(8,128)(2,1)S(1)}, u32[]{:S(2)}) copy-start(bf16[256,256]{1,0:T(8,128)(2,1)S(1)} %collective-permute-done.6.refs_3_) | copy-start | bytes 393220
  37.1 5.6 %collective-permute-start.9 = (bf16[256,256]{1,0:T(8,128)(2,1)}, bf16[256,256]{1,0:T(8,128)(2,1)}, u32[]{:S(2)}, u32[]{:S(2)}) collective-permute-start(bf16[256,256]{1,0:T(8,128)(2,1)} %get-tuple-element.46), channel_id=1, source_target_pairs={{0,6},{1,7},{2,4},{3,5},{4,2},{5,3},{6,0},{7,1},{8,14},{9,15},{10,... | collective-permute-start | bytes 393224 | tf_op jit(solution)/shard_map/ppermute | solution.py:278
  37.3 7.0 %copy-start.18 = (bf16[256,256]{1,0:T(8,128)(2,1)}, bf16[256,256]{1,0:T(8,128)(2,1)S(1)}, u32[]{:S(2)}) copy-start(bf16[256,256]{1,0:T(8,128)(2,1)S(1)} %collective-permute-done.7.refs_4_) | copy-start | bytes 393220
  37.3 5.4 %collective-permute-start.10 = (bf16[256,256]{1,0:T(8,128)(2,1)S(1)}, bf16[256,256]{1,0:T(8,128)(2,1)}, u32[]{:S(2)}, u32[]{:S(2)}) collective-permute-start(bf16[256,256]{1,0:T(8,128)(2,1)S(1)} %copy-done.14), channel_id=1, source_target_pairs={{0,2},{1,3},{2,0},{3,1},{4,6},{5,7},{6,4},{7,5},{8,10},{9,11},{10,... | collective-permute-start | bytes 393224 | tf_op jit(solution)/shard_map/ppermute | solution.py:278
  40.5 3.8 %copy-start.21 = (bf16[256,256]{1,0:T(8,128)(2,1)}, bf16[256,256]{1,0:T(8,128)(2,1)S(1)}, u32[]{:S(2)}) copy-start(bf16[256,256]{1,0:T(8,128)(2,1)S(1)} %collective-permute-done.8.refs_5_) | copy-start | bytes 393220
  42.7 0.8 copy-start.11
  43.5 0.8 copy-start.12
  59.4 21.4 %copy-start = (bf16[2048,256]{1,0:T(8,128)(2,1)S(1)}, bf16[2048,256]{1,0:T(8,128)(2,1)}, u32[]{:S(2)}) copy-start(bf16[2048,256]{1,0:T(8,128)(2,1)} %get-tuple-element.54) | copy-start | bytes 3145732
  59.4 17.3 %collective-permute-start.16 = (bf16[1024,256]{1,0:T(8,128)(2,1)}, bf16[1024,256]{1,0:T(8,128)(2,1)S(1)}, u32[]{:S(2)}, u32[]{:S(2)}) collective-permute-start(bf16[1024,256]{1,0:T(8,128)(2,1)} %get-tuple-element.55), channel_id=1, source_target_pairs={{0,8},{8,16},{16,24},{1,9},{9,17},{17,25},{2,10},{10,18},{18,26},{... | collective-permute-start | bytes 1572872 | tf_op jit(solution)/shard_map/ppermute | solution.py:312
  64.9 15.8 %collective-permute-start.17 = (bf16[1024,256]{1,0:T(8,128)(2,1)}, bf16[1024,256]{1,0:T(8,128)(2,1)S(1)}, u32[]{:S(2)}, u32[]{:S(2)}) collective-permute-start(bf16[1024,256]{1,0:T(8,128)(2,1)} %get-tuple-element.56), channel_id=1, source_target_pairs={{8,0},{16,8},{24,16},{9,1},{17,9},{25,17},{10,2},{18,10},{26,18},{... | collective-permute-start | bytes 1572872 | tf_op jit(solution)/shard_map/ppermute | solution.py:311
  66.2 15.7 %all-to-all-start = ((bf16[8,256,128]{2,1,0:T(8,128)(2,1)}), bf16[8,256,128]{2,1,0:T(8,128)(2,1)S(1)}, u32[]{:S(2)}, u32[]{:S(2)}) async-start(bf16[8,256,128]{2,1,0:T(8,128)(2,1)} %get-tuple-element.53), calls=%async_computation | async-start | bytes 1048576 | tf_op jit(solution)/shard_map/all_to_all | solution.py:271
  82.0 18.4 %all-to-all-start.1 = ((bf16[8,256,256]{2,1,0:T(8,128)(2,1)}), bf16[8,256,256]{2,1,0:T(8,128)(2,1)S(1)}, u32[]{:S(2)}, u32[]{:S(2)}) async-start(bf16[8,256,256]{2,1,0:T(8,128)(2,1)} %bitcast.11), calls=%async_computation.1 | async-start | bytes 2097152 | tf_op jit(solution)/shard_map/all_to_all | solution.py:271
